TPU v7x, 32 devices: a whole 2x2x4 slice. The times are simulated.
32 devices in a mesh: row: 8 (over y, x, core), col: 4 (over z).
Axes of the slice: x: 2, y: 2, z: 4, core: 2. Of those that a mesh axis runs over, the one named last changes fastest.
Arguments:
- orbitals: bfloat16 [6144, 2, 2048], P(('row', 'col')), may hold values from -6 to 6
- applied_orbitals: bfloat16 [6144, 2, 2048], P(('row', 'col')), may hold values from -6 to 6
- ritz_matrix: bfloat16 [2, 2048, 2048], P(None, 'row', 'col'), may hold values from -0.09375 to 0.09375
Outputs:
- rotated_orbitals: bfloat16 [6144, 2, 2048], P(('row', 'col'))
- rotated_applied: bfloat16 [6144, 2, 2048], P(('row', 'col'))
All inputs are finite; a program needn't handle non-finite values.
Results may differ from a plain program's by a relative error of at most 0.001.
Values may be sent and summed in bfloat16 or wider, within the bound.
No kernel may reach another device: no remote copies, remote signals or barrier semaphores. Data moves between devices by JAX's collectives and lax.ppermute only.
A program may use at most 128 MiB of HBM per device.

v0:
```python
import jax
import jax.numpy as jnp
from jax import lax
from jax.sharding import PartitionSpec as P


def shards(orbitals, applied_orbitals, ritz_matrix):
    row_count = orbitals.shape[0]
    band_count = orbitals.shape[2]
    stacked = jnp.concatenate(
        [
            orbitals.reshape(row_count, 2 * band_count),
            applied_orbitals.reshape(row_count, 2 * band_count),
        ],
        0,
    )
    strip = lax.all_gather(ritz_matrix, "col", axis=2, tiled=True)
    shard_piece = lax.all_gather(strip, "row", axis=1, tiled=True)
    height = shard_piece.shape[1]
    real_cols = lax.slice_in_dim(stacked, 0, height, axis=1)
    imag_cols = lax.dynamic_slice_in_dim(stacked, band_count, height, 1)
    upper_half = jnp.concatenate([shard_piece[0], shard_piece[1]], 1)
    lower_half = jnp.concatenate([-shard_piece[1], shard_piece[0]], 1)
    running = jnp.dot(real_cols, upper_half, preferred_element_type=jnp.float32)
    running = running + jnp.dot(imag_cols, lower_half, preferred_element_type=jnp.float32)
    result = running.reshape(2 * row_count, 2, band_count)
    result = result.astype(jnp.bfloat16)
    return (result[:row_count], result[row_count:])


def solution(mesh):
    in_specs = (P(("row", "col"), None, None), P(("row", "col"), None, None), P(None, "row", "col"))
    out_specs = (P(("row", "col"), None, None), P(("row", "col"), None, None))
    return jax.shard_map(shards, mesh=mesh, in_specs=in_specs, out_specs=out_specs, check_vma=False)
```

profile of v0, /device:TPU:0, one launch (start us, length us, event | category | flops | bytes accessed | tf_op | source)
XLA Modules:
  0.0 208.3 jit_solution(13244597676617920388)
XLA Ops:
  7.2 0.0 copy-start
  7.2 0.0 all-gather.3.cloned.1.call-start
  7.2 0.7 all-gather.3.cloned.1.call-update
  7.9 0.0 all-gather.5.cloned.1.call-start
  8.0 50.3 %all-gather.3.cloned.1.call-done = bf16[2,256,2048]{2,1,0:T(8,128)(2,1)} async-done(((bf16[2,256,512]{2,1,0:T(8,128)(2,1)}), bf16[2,256,2048]{2,1,0:T(8,128)(2,1)}) %all-gather.3.cloned.1.call-update) | async-done | bytes 2097168 | tf_op jit(solution)/shard_map/all_gather | solution.py:17
  58.3 0.0 all-gather.5.cloned.1.call-update
  58.3 2.1 copy.5
  60.3 0.0 copy-done
  60.3 0.6 copy.6
  61.0 0.1 constant_dynamic-update-slice_fusion.1
  61.1 0.1 constant_dynamic-update-slice_fusion
  61.3 87.5 %all-gather.5.cloned.1.call-done = bf16[2,2048,2048]{2,1,0:T(8,128)(2,1)} async-done(((bf16[2,256,2048]{2,1,0:T(8,128)(2,1)}), bf16[2,2048,2048]{2,1,0:T(8,128)(2,1)}) %all-gather.5.cloned.1.call-update) | async-done | bytes 16777232 | tf_op jit(solution)/shard_map/all_gather | solution.py:18
  148.8 11.8 %slice_bitcast_fusion.1 = (bf16[2048,2048]{1,0:T(8,128)(2,1)}, bf16[2048,2048]{1,0:T(8,128)(2,1)}) fusion(bf16[2,2048,2048]{2,1,0:T(8,128)(2,1)} %all-gather.5.cloned.1.call-done), kind=kLoop, calls=%fused_computation.9 | loop fusion | bytes 33554432 | tf_op jit(solution)/shard_map/squeeze | solution.py:22
  160.6 12.6 %fusion = f32[384,4096]{1,0:T(8,128)} fusion(bf16[2048,2048]{1,0:T(8,128)(2,1)} %get-tuple-element.3, bf16[2048,2048]{1,0:T(8,128)(2,1)} %get-tuple-element.2, bf16[384,4096]{1,0:T(8,128)(2,1)S(1)} %constant_dynamic-update-slice_fusion), kind=kOutput, calls=%fused_computation | convolution fusion | flops 6476005376 | bytes 24641536 | tf_op jit(solution)/shard_map/dot_general | solution.py:24
  173.2 7.1 %fusion.14 = bf16[2048,2048]{1,0:T(8,128)(2,1)} fusion(bf16[2,2048,2048]{2,1,0:T(8,128)(2,1)} %all-gather.5.cloned.1.call-done), kind=kLoop, calls=%fused_computation.17 | loop fusion | flops 4194304 | bytes 16777216 | tf_op jit(solution)/shard_map/neg | solution.py:23
  180.3 14.3 %add_convert_fusion = bf16[384,4096]{1,0:T(8,128)(2,1)} fusion(f32[384,4096]{1,0:T(8,128)} %fusion, bf16[2048,2048]{1,0:T(8,128)(2,1)} %get-tuple-element.2, bf16[2048,2048]{1,0:T(8,128)(2,1)} %fusion.14, bf16[384,4096]{1,0:T(8,128)(2,1)S(1)} %constant_dynamic-update-slice_fusion), kind=kOutput, calls=%fused_computation.10 | convolution fusion | flops 6479151104 | bytes 27787264 | tf_op jit(solution)/shard_map/dot_general | solution.py:25
  194.6 2.1 %fusion.15 = (bf16[192,4096]{1,0:T(8,128)(2,1)S(1)}, bf16[192,4096]{1,0:T(8,128)(2,1)S(1)}) fusion(bf16[384,4096]{1,0:T(8,128)(2,1)} %add_convert_fusion), kind=kLoop, calls=%fused_computation.18 | loop fusion | bytes 6291456 | tf_op jit(solution)/shard_map/slice | solution.py:28
  196.7 2.4 %slice.27 = bf16[192,2,2048]{2,1,0:T(2,128)(2,1)} reshape(bf16[192,4096]{1,0:T(8,128)(2,1)S(1)} %get-tuple-element.5) | data formatting | bytes 3145728 | tf_op jit(solution)/shard_map/slice | solution.py:28
  199.1 2.4 %slice.29 = bf16[192,2,2048]{2,1,0:T(2,128)(2,1)} reshape(bf16[192,4096]{1,0:T(8,128)(2,1)S(1)} %get-tuple-element.4) | data formatting | bytes 3145728 | tf_op jit(solution)/shard_map/slice | solution.py:28
Async XLA Ops:
  7.2 53.2 %copy-start = (bf16[192,2,2048]{2,1,0:T(2,128)(2,1)S(1)}, bf16[192,2,2048]{2,1,0:T(2,128)(2,1)}, u32[]{:S(2)}) copy-start(bf16[192,2,2048]{2,1,0:T(2,128)(2,1)} %param.4) | copy-start | bytes 4718596
  7.2 51.1 %all-gather.3.cloned.1.call-start = ((), (), s32[]{:S(2)}) async-start(), calls=%async_computation | async-start | bytes 2621440 | tf_op jit(solution)/shard_map/all_gather | solution.py:17
  7.9 140.9 %all-gather.5.cloned.1.call-start = ((), (), s32[]{:S(2)}) async-start(), calls=%async_computation.1 | async-start | bytes 18874368 | tf_op jit(solution)/shard_map/all_gather | solution.py:18
Sparse Core Ops, SparseCore 0:
  9.6 48.6 all-gather.2
  60.2 88.5 all-gather.4
where the time goes:
time: 208 us
  waiting for transfers between devices  138 us (66%)
  matrix products  26.9 us (13%)
  local copies, waits for them, and re-layouts  21.6 us (10%)
  between operations  14.1 us (7%)
  other arithmetic  7.14 us (3%)
    all_gather x1, waiting for transfers between devices, shards(): shard_piece = lax.all_gather(strip, 'row', axis=1, tiled=True)  87.5 us
    all_gather x1, waiting for transfers between devices, shards(): strip = lax.all_gather(ritz_matrix, 'col', axis=2, tiled=True)  50.3 us
    dot_general x1, matrix products, shards(): jnp.dot(imag_cols, lower_half, preferred_element_type=jnp.float32)  14.3 us
    dot_general x1, matrix products, shards(): running = jnp.dot(real_cols, upper_half, preferred_element_type=jnp.float32)  12.6 us
    squeeze x1, local copies, waits for them, and re-layouts, shards(): upper_half = jnp.concatenate([shard_piece[0], shard_piece[1]], 1)  11.8 us
    neg x1, other arithmetic, shards(): lower_half = jnp.concatenate([-shard_piece[1], shard_piece[0]], 1)  7.14 us
    slice x3, local copies, waits for them, and re-layouts, shards(): return (result[:row_count], result[row_count:])  6.8 us
  transfers between devices with their start and end apart: 2, of which 2 were waited for; matrix products, arithmetic and copies ran while one was open for 1% of the time, Pallas kernels for 0%

commit v1 on v0

v1 whole, which is shorter than its diff:
```python
import functools

import jax
import jax.numpy as jnp
from jax import lax
from jax.experimental import pallas as pl
from jax.experimental.pallas import tpu as pltpu
from jax.sharding import PartitionSpec as P

AXES = ("row", "col")


def chip_at(place, chips):
    place = place % chips
    return 2 * place if 2 * place < chips else 2 * (chips - 1 - place) + 1


class Moves:
    def __init__(self, rows, cols):
        self.chips, self.cols = rows // 2, cols

    def every(self):
        for place in range(self.chips):
            for core in range(2):
                for layer in range(self.cols):
                    yield place, core, layer

    def device(self, place, core, layer):
        return (chip_at(place, self.chips) * 2 + core) * self.cols + layer % self.cols

    def ring(self, value, step):
        pairs = [(self.device(p, k, z), self.device(p + (step if k == 0 else -step), k, z)) for p, k, z in self.every()]
        return lax.ppermute(value, AXES, pairs)

    def up(self, value):
        pairs = [(self.device(p, k, z), self.device(p, k, z + 1)) for p, k, z in self.every()]
        return lax.ppermute(value, AXES, pairs)

    def other(self, value):
        pairs = [(self.device(p, k, z), self.device(p, 1 - k, z)) for p, k, z in self.every()]
        return lax.ppermute(value, AXES, pairs)


def after(value, *earlier):
    return lax.optimization_barrier((value,) + earlier)[0]


def stage_kernel(hops, rows, cols, stage, fresh, lhs, *refs):
    count = 2 * len(hops)
    blocks = refs[:count]
    first_out, second_out, first_tile, second_tile, sems = refs[count if fresh else count + 2 :]
    chips = rows // 2
    g = first_tile.shape[0]
    depth, width = blocks[0].shape[1:]
    row, layer = lax.axis_index("row"), lax.axis_index("col")
    chip, core = row // 2, row % 2
    place = jnp.where(chip % 2 == 0, chip // 2, chips - 1 - chip // 2)
    total = jnp.zeros((4 * g, width), jnp.float32)
    for i, block in enumerate(blocks):
        hop = hops[i % len(hops)]
        owner_core = core if i < len(hops) else 1 - core
        at = (place + chips + jnp.where(owner_core == 0, -hop, hop)) % chips
        owner = jnp.where(2 * at < chips, 2 * at, 2 * (chips - 1 - at) + 1) * 2 + owner_core
        k = pl.ds(pl.multiple_of(owner * depth, depth), depth)
        total += jnp.dot(lhs[2 * g :, k], block[0], preferred_element_type=jnp.float32)
        total += jnp.dot(lhs[: 4 * g, k], block[1], preferred_element_type=jnp.float32)
    rounded = total.astype(jnp.bfloat16)
    first_tile[:, 0, :] = rounded[:g]
    first_tile[:, 1, :] = rounded[2 * g : 3 * g]
    second_tile[:, 0, :] = rounded[g : 2 * g]
    second_tile[:, 1, :] = rounded[3 * g :]
    columns = pl.ds(pl.multiple_of(((layer + cols - stage) % cols) * width, width), width)
    copies = [
        pltpu.make_async_copy(first_tile, first_out.at[:, :, columns], sems.at[0]),
        pltpu.make_async_copy(second_tile, second_out.at[:, :, columns], sems.at[1]),
    ]
    for copy in copies:
        copy.start()
    for copy in copies:
        copy.wait()


def run_stage(hops, rows, cols, stage, outs, lhs, blocks, like):
    fresh = outs is None
    g, _, bands = like.shape
    depth, width = blocks[0].shape[1:]
    vmem, hbm = pl.BlockSpec(memory_space=pltpu.VMEM), pl.BlockSpec(memory_space=pl.ANY)
    count = len(blocks)
    flops = 2 * 4 * g * 2 * depth * width * count
    return pl.pallas_call(
        functools.partial(stage_kernel, hops, rows, cols, stage, fresh),
        out_shape=(jax.ShapeDtypeStruct(like.shape, like.dtype),) * 2,
        in_specs=[vmem] * (1 + count) + ([] if fresh else [hbm] * 2),
        out_specs=(hbm, hbm),
        scratch_shapes=[pltpu.VMEM((g, 2, width), like.dtype)] * 2 + [pltpu.SemaphoreType.DMA((2,))],
        input_output_aliases={} if fresh else {1 + count: 0, 2 + count: 1},
        compiler_params=pltpu.CompilerParams(vmem_limit_bytes=24 * 2**20),
        cost_estimate=pl.CostEstimate(flops=flops, bytes_accessed=8 * 2**20, transcendentals=0),
    )(lhs, *blocks, *(() if fresh else outs))


def shards(rows, cols, orbitals, applied, ritz):
    moves = Moves(rows, cols)
    chips = rows // 2
    ahead, back = chips // 2, (chips - 1) // 2
    hops = [0, *range(1, ahead + 1), *(-h for h in range(1, back + 1))]

    real = jnp.concatenate([orbitals[:, 0], applied[:, 0]], 0)
    imag = jnp.concatenate([orbitals[:, 1], applied[:, 1]], 0)
    lhs = jnp.concatenate([-imag, real, imag], 0)

    def chain(first, count, step, *earlier):
        out = []
        for _ in range(count):
            first = moves.ring(after(first, *earlier) if earlier else first, step)
            out.append(first)
        return out

    own_ahead, own_back = chain(ritz, ahead, 1), chain(ritz, back, -1)
    layers = [ritz]
    for s in range(1, cols):
        layers.append(moves.up(layers[-1] if s == 1 else after(layers[-1], own_ahead[0], *own_back[:1])))
    stages = [[ritz, *own_ahead, *own_back]]
    if cols > 1:
        near_back = chain(after(layers[1], own_ahead[0], *own_back[:1]), back, -1)
        gate = (own_ahead[-1], *near_back[-1:])
        rings = {}
        for s in range(2, cols):
            source = after(layers[s], *gate)
            a, b = chain(source, ahead, 1), chain(source, back, -1)
            rings[s] = [layers[s], *a, *b]
            gate = (a[0], *b[-1:])
        near_ahead = []
        gate = (layers[-1],)
        for value in own_ahead:
            near_ahead.append(moves.up(after(value, *gate)))
            gate = (near_ahead[-1],)
        stages.append([layers[1], *near_ahead, *near_back])
        stages.extend(rings[s] for s in range(2, cols))
    outs = None
    for s in [0, *range(2, cols), 1][: cols]:
        blocks = stages[s]
        outs = run_stage(hops, rows, cols, s, outs, lhs, [*blocks, *map(moves.other, blocks)], orbitals)
    return outs


def solution(mesh):
    rows, cols = mesh.shape["row"], mesh.shape["col"]
    whole = P(AXES, None, None)
    return jax.shard_map(
        functools.partial(shards, rows, cols),
        mesh=mesh,
        in_specs=(whole, whole, P(None, "row", "col")),
        out_specs=(whole, whole),
        check_vma=False,
    )
```

time: 208 us -> 110 us (0.53)
  waiting for transfers between devices: 138 us -> 63.6 us
  matrix products: 26.9 us -> 0 us
  Pallas kernels: 0 us -> 17.9 us
  starting transfers between devices: 0.08 us -> 17.3 us
  between operations: 14.1 us -> 1.03 us
  local copies, waits for them, and re-layouts: 21.6 us -> 9.37 us
  other arithmetic: 7.14 us -> 0.38 us
    all_gather x2 -> x0, waiting for transfers between devices: 138 us -> none  [the longest x1 87.5 us: shards(): shard_piece = lax.all_gather(strip, 'row', axis=1, tiled=True)]
    ppermute x0 -> x31, waiting for transfers between devices: none -> 63.6 us  [the longest x10 49.2 us: ring(): return lax.ppermute(value, AXES, pairs)]
    dot_general x2 -> x0, matrix products: 26.9 us -> none  [the longest x1 14.3 us: shards(): jnp.dot(imag_cols, lower_half, preferred_element_type=jnp.float32)]
    pallas_call x0 -> x4, Pallas kernels: none -> 17.9 us  [run_stage(): pl.pallas_call(functools.partial(stage_kernel, hops, rows, cols, stage, f...]
    ppermute x0 -> x31, starting transfers between devices: none -> 17.3 us  [the longest x10 12.1 us: ring(): return lax.ppermute(value, AXES, pairs)]
    squeeze x1 -> x0, local copies, waits for them, and re-layouts: 11.8 us -> none  [shards(): upper_half = jnp.concatenate([shard_piece[0], shard_piece[1]], 1)]
    neg x1 -> x0, other arithmetic: 7.14 us -> none  [shards(): lower_half = jnp.concatenate([-shard_piece[1], shard_piece[0]], 1)]
    slice x3 -> x2, local copies, waits for them, and re-layouts: 6.8 us -> 6.65 us  [shards(): real = jnp.concatenate([orbitals[:, 0], applied[:, 0]], 0)]
  transfers between devices with their start and end apart: 2 -> 31, of which waited for: 2 -> 10; matrix products, arithmetic and copies ran while one was open for 1% -> 9% of each run, Pallas kernels for 0% -> 12%
where the time goes in v1:
time: 110 us
  waiting for transfers between devices  63.6 us (58%)
  Pallas kernels  17.9 us (16%)
  starting transfers between devices  17.3 us (16%)
  local copies, waits for them, and re-layouts  9.37 us (9%)
    ppermute x10, waiting for transfers between devices, ring(): return lax.ppermute(value, AXES, pairs)  49.2 us
    pallas_call x4, Pallas kernels, run_stage(): pl.pallas_call(functools.partial(stage_kernel, hops, rows, cols, stage, f...  17.9 us
    ppermute x5, waiting for transfers between devices, up(): return lax.ppermute(value, AXES, pairs)  14.4 us
    ppermute x10, starting transfers between devices, ring(): return lax.ppermute(value, AXES, pairs)  12.1 us
    slice x2, local copies, waits for them, and re-layouts, shards(): real = jnp.concatenate([orbitals[:, 0], applied[:, 0]], 0)  6.65 us
    ppermute x16, starting transfers between devices, other(): return lax.ppermute(value, AXES, pairs)  2.82 us
    ppermute x5, starting transfers between devices, up(): return lax.ppermute(value, AXES, pairs)  2.35 us
    unnamed x9, local copies, waits for them, and re-layouts  2.27 us
  transfers between devices with their start and end apart: 31, of which 10 were waited for; matrix products, arithmetic and copies ran while one was open for 9% of the time, Pallas kernels for 12%

profile of v1, /device:TPU:0, one launch (start us, length us, event | category | flops | bytes accessed | tf_op | source)
XLA Modules:
  0.0 109.5 jit_solution(14811429944020070466)
XLA Ops:
  0.6 3.0 %collective-permute-start.1 = (bf16[2,256,512]{2,1,0:T(8,128)(2,1)}, bf16[2,256,512]{2,1,0:T(8,128)(2,1)S(1)}, u32[]{:S(2)}, u32[]{:S(2)}) collective-permute-start(bf16[2,256,512]{2,1,0:T(8,128)(2,1)} %refs_0_.1), channel_id=1, source_target_pairs={{0,16},{1,17},{2,18},{3,19},{4,12},{5,13},{6,14},{7,15},{16,24},{1... | collective-permute-start | bytes 1572872 | tf_op jit(solution)/shard_map/ppermute | solution.py:33
  3.7 0.0 collective-permute-start.2
  3.7 2.0 %collective-permute-start = (bf16[2,256,512]{2,1,0:T(8,128)(2,1)}, bf16[2,256,512]{2,1,0:T(8,128)(2,1)S(1)}, u32[]{:S(2)}, u32[]{:S(2)}) collective-permute-start(bf16[2,256,512]{2,1,0:T(8,128)(2,1)} %refs_0_.1), channel_id=1, source_target_pairs={{0,1},{1,2},{2,3},{3,0},{4,5},{5,6},{6,7},{7,4},{16,17},{17,18},{1... | collective-permute-start | bytes 1572872 | tf_op jit(solution)/shard_map/ppermute | solution.py:37
  5.7 10.3 %collective-permute-done.1.refs_1_ = bf16[2,256,512]{2,1,0:T(8,128)(2,1)S(1)} collective-permute-done((bf16[2,256,512]{2,1,0:T(8,128)(2,1)}, bf16[2,256,512]{2,1,0:T(8,128)(2,1)S(1)}, u32[]{:S(2)}, u32[]{:S(2)}) %collective-permute-start.1) | collective-permute-done | bytes 524320 | tf_op jit(solution)/shard_map/ppermute | solution.py:33
  16.1 0.0 collective-permute-done.2.refs_3_
  16.1 3.3 %collective-permute-done.refs_0_ = bf16[2,256,512]{2,1,0:T(8,128)(2,1)S(1)} collective-permute-done((bf16[2,256,512]{2,1,0:T(8,128)(2,1)}, bf16[2,256,512]{2,1,0:T(8,128)(2,1)S(1)}, u32[]{:S(2)}, u32[]{:S(2)}) %collective-permute-start) | collective-permute-done | bytes 524320 | tf_op jit(solution)/shard_map/ppermute | solution.py:37
  19.4 1.5 %collective-permute-start.6 = (bf16[2,256,512]{2,1,0:T(8,128)(2,1)S(1)}, bf16[2,256,512]{2,1,0:T(8,128)(2,1)S(1)}, u32[]{:S(2)}, u32[]{:S(2)}) collective-permute-start(bf16[2,256,512]{2,1,0:T(8,128)(2,1)S(1)} %collective-permute-done.1.refs_1_), channel_id=1, source_target_pairs={{0,16},{1,17},{2,18},{3,19},{4,12},{5,13},{6,14},{7,15},{16,24},{1... | collective-permute-start | bytes 1572872 | tf_op jit(solution)/shard_map/ppermute | solution.py:33
  20.9 0.5 collective-permute-start.8
  21.4 12.2 %collective-permute-done.6.refs_2_ = bf16[2,256,512]{2,1,0:T(8,128)(2,1)S(1)} collective-permute-done((bf16[2,256,512]{2,1,0:T(8,128)(2,1)S(1)}, bf16[2,256,512]{2,1,0:T(8,128)(2,1)S(1)}, u32[]{:S(2)}, u32[]{:S(2)}) %collective-permute-start.6) | collective-permute-done | bytes 524320 | tf_op jit(solution)/shard_map/ppermute | solution.py:33
  33.6 1.0 collective-permute-done.3.refs_0_
  34.7 0.7 collective-permute-start.13
  35.4 4.4 %fusion.3 = (bf16[192,1,2048]{2,1,0:T(2,128)(2,1)S(1)}, bf16[192,1,2048]{2,1,0:T(2,128)(2,1)S(1)}) fusion(bf16[192,2,2048]{2,1,0:T(2,128)(2,1)} %param.4), kind=kLoop, calls=%fused_computation.10 | loop fusion | bytes 3145728 | tf_op jit(solution)/shard_map/slice | solution.py:108
  39.8 0.1 collective-permute-start.28
  39.9 0.5 collective-permute-start.30
  40.4 1.3 %collective-permute-start.14 = (bf16[2,256,512]{2,1,0:T(8,128)(2,1)S(1)}, bf16[2,256,512]{2,1,0:T(8,128)(2,1)S(1)}, u32[]{:S(2)}, u32[]{:S(2)}) collective-permute-start(bf16[2,256,512]{2,1,0:T(8,128)(2,1)S(1)} %collective-permute-done.3.refs_0_), channel_id=1, source_target_pairs={{0,8},{1,9},{2,10},{3,11},{4,20},{5,21},{6,22},{7,23},{16,0},{17,1... | collective-permute-start | bytes 1572872 | tf_op jit(solution)/shard_map/ppermute | solution.py:33
  41.7 2.8 %collective-permute-done.13.refs_1_ = bf16[2,256,512]{2,1,0:T(8,128)(2,1)S(1)} collective-permute-done((bf16[2,256,512]{2,1,0:T(8,128)(2,1)S(1)}, bf16[2,256,512]{2,1,0:T(8,128)(2,1)S(1)}, u32[]{:S(2)}, u32[]{:S(2)}) %collective-permute-start.13) | collective-permute-done | bytes 524320 | tf_op jit(solution)/shard_map/ppermute | solution.py:33
  44.5 2.2 %fusion.4 = (bf16[192,1,2048]{2,1,0:T(2,128)(2,1)S(1)}, bf16[192,1,2048]{2,1,0:T(2,128)(2,1)S(1)}) fusion(bf16[192,2,2048]{2,1,0:T(2,128)(2,1)S(1)} %copy-done.1), kind=kLoop, calls=%fused_computation.11 | loop fusion | bytes 3145728 | tf_op jit(solution)/shard_map/slice | solution.py:108
  46.8 0.5 copy.31
  47.2 0.5 copy.32
  47.7 1.9 %collective-permute-done.14.refs_3_ = bf16[2,256,512]{2,1,0:T(8,128)(2,1)S(1)} collective-permute-done((bf16[2,256,512]{2,1,0:T(8,128)(2,1)S(1)}, bf16[2,256,512]{2,1,0:T(8,128)(2,1)S(1)}, u32[]{:S(2)}, u32[]{:S(2)}) %collective-permute-start.14) | collective-permute-done | bytes 524320 | tf_op jit(solution)/shard_map/ppermute | solution.py:33
  49.6 0.0 collective-permute-start.29
  49.6 7.6 %collective-permute-done.4.refs_0_ = bf16[2,256,512]{2,1,0:T(8,128)(2,1)S(1)} collective-permute-done((bf16[2,256,512]{2,1,0:T(8,128)(2,1)S(1)}, bf16[2,256,512]{2,1,0:T(8,128)(2,1)S(1)}, u32[]{:S(2)}, u32[]{:S(2)}) %collective-permute-start.4) | collective-permute-done | bytes 524320 | tf_op jit(solution)/shard_map/ppermute | solution.py:37
  57.2 1.4 %collective-permute-start.15 = (bf16[2,256,512]{2,1,0:T(8,128)(2,1)S(1)}, bf16[2,256,512]{2,1,0:T(8,128)(2,1)S(1)}, u32[]{:S(2)}, u32[]{:S(2)}) collective-permute-start(bf16[2,256,512]{2,1,0:T(8,128)(2,1)S(1)} %collective-permute-done.4.refs_0_), channel_id=1, source_target_pairs={{0,16},{1,17},{2,18},{3,19},{4,12},{5,13},{6,14},{7,15},{16,24},{1... | collective-permute-start | bytes 1572872 | tf_op jit(solution)/shard_map/ppermute | solution.py:33
  58.7 0.5 collective-permute-start.22
  59.2 0.4 fusion
  59.6 0.1 collective-permute-start.5
  59.6 0.5 fusion.2
  60.1 1.6 %collective-permute-start.17 = (bf16[2,256,512]{2,1,0:T(8,128)(2,1)S(1)}, bf16[2,256,512]{2,1,0:T(8,128)(2,1)S(1)}, u32[]{:S(2)}, u32[]{:S(2)}) collective-permute-start(bf16[2,256,512]{2,1,0:T(8,128)(2,1)S(1)} %collective-permute-done.4.refs_0_), channel_id=1, source_target_pairs={{0,8},{1,9},{2,10},{3,11},{4,20},{5,21},{6,22},{7,23},{16,0},{17,1... | collective-permute-start | bytes 1572872 | tf_op jit(solution)/shard_map/ppermute | solution.py:33
  61.7 16.0 %collective-permute-done.22.refs_2_ = bf16[2,256,512]{2,1,0:T(8,128)(2,1)S(1)} collective-permute-done((bf16[2,256,512]{2,1,0:T(8,128)(2,1)S(1)}, bf16[2,256,512]{2,1,0:T(8,128)(2,1)S(1)}, u32[]{:S(2)}, u32[]{:S(2)}) %collective-permute-start.22) | collective-permute-done | bytes 524320 | tf_op jit(solution)/shard_map/ppermute | solution.py:33
  77.7 0.5 collective-permute-start.18
  78.2 0.5 fusion.1
  78.6 1.5 %collective-permute-start.16 = (bf16[2,256,512]{2,1,0:T(8,128)(2,1)S(1)}, bf16[2,256,512]{2,1,0:T(8,128)(2,1)S(1)}, u32[]{:S(2)}, u32[]{:S(2)}) collective-permute-start(bf16[2,256,512]{2,1,0:T(8,128)(2,1)S(1)} %collective-permute-done.15.refs_1_), channel_id=1, source_target_pairs={{0,16},{1,17},{2,18},{3,19},{4,12},{5,13},{6,14},{7,15},{16,24},{1... | collective-permute-start | bytes 1572872 | tf_op jit(solution)/shard_map/ppermute | solution.py:33
  80.1 0.5 constant_dynamic-update-slice_fusion.1
  80.6 0.0 copy-start
  80.6 0.2 collective-permute-start.7
  80.8 0.1 collective-permute-start.19
  80.9 0.5 collective-permute-start.25
  81.4 0.1 collective-permute-start.21
  81.5 0.5 constant_dynamic-update-slice_fusion.lhs
  82.0 5.9 %collective-permute-done.16.refs_2_ = bf16[2,256,512]{2,1,0:T(8,128)(2,1)S(1)} collective-permute-done((bf16[2,256,512]{2,1,0:T(8,128)(2,1)S(1)}, bf16[2,256,512]{2,1,0:T(8,128)(2,1)S(1)}, u32[]{:S(2)}, u32[]{:S(2)}) %collective-permute-start.16) | collective-permute-done | bytes 524320 | tf_op jit(solution)/shard_map/ppermute | solution.py:33
  87.9 4.5 %shard_map.50 = (bf16[192,2,2048]{2,1,0:T(2,128)(2,1)}, bf16[192,2,2048]{2,1,0:T(2,128)(2,1)}) custom-call(bf16[1152,2048]{1,0:T(8,128)(2,1)S(1)} %constant_dynamic-update-slice_fusion.lhs, bf16[2,256,512]{2,1,0:T(8,128)(2,1)S(1)} %copy-done, bf16[2,256,512]{2,1,0:T(8,128)(2,1)S(1)} %collective-permute-done.1.refs_1_, ...), custom_call_target="tpu_custom_call" | custom-call | flops 3221225472 | bytes 8388608 | tf_op jit(solution)/shard_map/pallas_call | solution.py:90
  92.4 0.6 collective-permute-start.9
  92.9 0.1 collective-permute-start.12
  93.0 0.4 collective-permute-start.10
  93.4 2.4 %collective-permute-done.7.refs_2_ = bf16[2,256,512]{2,1,0:T(8,128)(2,1)S(1)} collective-permute-done((bf16[2,256,512]{2,1,0:T(8,128)(2,1)S(1)}, bf16[2,256,512]{2,1,0:T(8,128)(2,1)S(1)}, u32[]{:S(2)}, u32[]{:S(2)}) %collective-permute-start.7) | collective-permute-done | bytes 524320 | tf_op jit(solution)/shard_map/ppermute | solution.py:37
  95.9 4.5 %shard_map.51 = (bf16[192,2,2048]{2,1,0:T(2,128)(2,1)}, bf16[192,2,2048]{2,1,0:T(2,128)(2,1)}) custom-call(bf16[1152,2048]{1,0:T(8,128)(2,1)S(1)} %constant_dynamic-update-slice_fusion.lhs, bf16[2,256,512]{2,1,0:T(8,128)(2,1)S(1)} %collective-permute-done.3.refs_0_, ...), custom_call_target="tpu_custom_call", output_to_operand_aliasing={{0}: (9, {}), {1}: (10, {})} | custom-call | flops 3221225472 | bytes 8388608 | tf_op jit(solution)/shard_map/pallas_call | solution.py:90
  100.4 4.5 %shard_map.52 = (bf16[192,2,2048]{2,1,0:T(2,128)(2,1)}, bf16[192,2,2048]{2,1,0:T(2,128)(2,1)}) custom-call(bf16[1152,2048]{1,0:T(8,128)(2,1)S(1)} %constant_dynamic-update-slice_fusion.lhs, bf16[2,256,512]{2,1,0:T(8,128)(2,1)S(1)} %collective-permute-done.4.refs_0_, ...), custom_call_target="tpu_custom_call", output_to_operand_aliasing={{0}: (9, {}), {1}: (10, {})} | custom-call | flops 3221225472 | bytes 8388608 | tf_op jit(solution)/shard_map/pallas_call | solution.py:90
  104.9 4.5 %shard_map.53 = (bf16[192,2,2048]{2,1,0:T(2,128)(2,1)}, bf16[192,2,2048]{2,1,0:T(2,128)(2,1)}) custom-call(bf16[1152,2048]{1,0:T(8,128)(2,1)S(1)} %constant_dynamic-update-slice_fusion.lhs, bf16[2,256,512]{2,1,0:T(8,128)(2,1)S(1)} %collective-permute-done.refs_0_, ...), custom_call_target="tpu_custom_call", output_to_operand_aliasing={{0}: (9, {}), {1}: (10, {})} | custom-call | flops 3221225472 | bytes 8388608 | tf_op jit(solution)/shard_map/pallas_call | solution.py:90
  (31 shorter events, 0.1 us)
Async XLA Ops:
  0.6 43.9 %copy-start.1 = (bf16[192,2,2048]{2,1,0:T(2,128)(2,1)S(1)}, bf16[192,2,2048]{2,1,0:T(2,128)(2,1)}, u32[]{:S(2)}) copy-start(bf16[192,2,2048]{2,1,0:T(2,128)(2,1)} %param.3) | copy-start | bytes 4718596
  0.6 15.4 %collective-permute-start.1 = (bf16[2,256,512]{2,1,0:T(8,128)(2,1)}, bf16[2,256,512]{2,1,0:T(8,128)(2,1)S(1)}, u32[]{:S(2)}, u32[]{:S(2)}) collective-permute-start(bf16[2,256,512]{2,1,0:T(8,128)(2,1)} %refs_0_.1), channel_id=1, source_target_pairs={{0,16},{1,17},{2,18},{3,19},{4,12},{5,13},{6,14},{7,15},{16,24},{1... | collective-permute-start | bytes 1572872 | tf_op jit(solution)/shard_map/ppermute | solution.py:33
  3.7 12.4 %collective-permute-start.2 = (bf16[2,256,512]{2,1,0:T(8,128)(2,1)}, bf16[2,256,512]{2,1,0:T(8,128)(2,1)S(1)}, u32[]{:S(2)}, u32[]{:S(2)}) collective-permute-start(bf16[2,256,512]{2,1,0:T(8,128)(2,1)} %refs_0_.1), channel_id=1, source_target_pairs={{0,8},{1,9},{2,10},{3,11},{4,20},{5,21},{6,22},{7,23},{16,0},{17,1... | collective-permute-start | bytes 1572872 | tf_op jit(solution)/shard_map/ppermute | solution.py:33
  3.7 15.7 %collective-permute-start = (bf16[2,256,512]{2,1,0:T(8,128)(2,1)}, bf16[2,256,512]{2,1,0:T(8,128)(2,1)S(1)}, u32[]{:S(2)}, u32[]{:S(2)}) collective-permute-start(bf16[2,256,512]{2,1,0:T(8,128)(2,1)} %refs_0_.1), channel_id=1, source_target_pairs={{0,1},{1,2},{2,3},{3,0},{4,5},{5,6},{6,7},{7,4},{16,17},{17,18},{1... | collective-permute-start | bytes 1572872 | tf_op jit(solution)/shard_map/ppermute | solution.py:37
  19.4 14.3 %collective-permute-start.6 = (bf16[2,256,512]{2,1,0:T(8,128)(2,1)S(1)}, bf16[2,256,512]{2,1,0:T(8,128)(2,1)S(1)}, u32[]{:S(2)}, u32[]{:S(2)}) collective-permute-start(bf16[2,256,512]{2,1,0:T(8,128)(2,1)S(1)} %collective-permute-done.1.refs_1_), channel_id=1, source_target_pairs={{0,16},{1,17},{2,18},{3,19},{4,12},{5,13},{6,14},{7,15},{16,24},{1... | collective-permute-start | bytes 1572872 | tf_op jit(solution)/shard_map/ppermute | solution.py:33
  20.9 13.8 %collective-permute-start.3 = (bf16[2,256,512]{2,1,0:T(8,128)(2,1)S(1)}, bf16[2,256,512]{2,1,0:T(8,128)(2,1)S(1)}, u32[]{:S(2)}, u32[]{:S(2)}) collective-permute-start(bf16[2,256,512]{2,1,0:T(8,128)(2,1)S(1)} %collective-permute-done.refs_0_), channel_id=1, source_target_pairs={{0,1},{1,2},{2,3},{3,0},{4,5},{5,6},{6,7},{7,4},{16,17},{17,18},{1... | collective-permute-start | bytes 1572872 | tf_op jit(solution)/shard_map/ppermute | solution.py:37
  20.9 13.8 %collective-permute-start.8 = (bf16[2,256,512]{2,1,0:T(8,128)(2,1)S(1)}, bf16[2,256,512]{2,1,0:T(8,128)(2,1)S(1)}, u32[]{:S(2)}, u32[]{:S(2)}) collective-permute-start(bf16[2,256,512]{2,1,0:T(8,128)(2,1)S(1)} %collective-permute-done.refs_0_), channel_id=1, source_target_pairs={{0,8},{1,9},{2,10},{3,11},{4,20},{5,21},{6,22},{7,23},{16,0},{17,1... | collective-permute-start | bytes 1572872 | tf_op jit(solution)/shard_map/ppermute | solution.py:33
  21.4 35.8 %collective-permute-start.27 = (bf16[2,256,512]{2,1,0:T(8,128)(2,1)}, bf16[2,256,512]{2,1,0:T(8,128)(2,1)S(1)}, u32[]{:S(2)}, u32[]{:S(2)}) collective-permute-start(bf16[2,256,512]{2,1,0:T(8,128)(2,1)} %refs_0_.1), channel_id=1, source_target_pairs={{0,4},{1,5},{2,6},{3,7},{4,0},{5,1},{6,2},{7,3},{16,20},{17,21},{1... | collective-permute-start | bytes 1572872 | tf_op jit(solution)/shard_map/ppermute | solution.py:41
  34.7 9.9 %collective-permute-start.13 = (bf16[2,256,512]{2,1,0:T(8,128)(2,1)S(1)}, bf16[2,256,512]{2,1,0:T(8,128)(2,1)S(1)}, u32[]{:S(2)}, u32[]{:S(2)}) collective-permute-start(bf16[2,256,512]{2,1,0:T(8,128)(2,1)S(1)} %collective-permute-done.3.refs_0_), channel_id=1, source_target_pairs={{0,16},{1,17},{2,18},{3,19},{4,12},{5,13},{6,14},{7,15},{16,24},{1... | collective-permute-start | bytes 1572872 | tf_op jit(solution)/shard_map/ppermute | solution.py:33
  39.8 18.8 %collective-permute-start.28 = (bf16[2,256,512]{2,1,0:T(8,128)(2,1)S(1)}, bf16[2,256,512]{2,1,0:T(8,128)(2,1)S(1)}, u32[]{:S(2)}, u32[]{:S(2)}) collective-permute-start(bf16[2,256,512]{2,1,0:T(8,128)(2,1)S(1)} %collective-permute-done.1.refs_1_), channel_id=1, source_target_pairs={{0,4},{1,5},{2,6},{3,7},{4,0},{5,1},{6,2},{7,3},{16,20},{17,21},{1... | collective-permute-start | bytes 1572872 | tf_op jit(solution)/shard_map/ppermute | solution.py:41
  39.9 19.7 %collective-permute-start.30 = (bf16[2,256,512]{2,1,0:T(8,128)(2,1)S(1)}, bf16[2,256,512]{2,1,0:T(8,128)(2,1)S(1)}, u32[]{:S(2)}, u32[]{:S(2)}) collective-permute-start(bf16[2,256,512]{2,1,0:T(8,128)(2,1)S(1)} %collective-permute-done.2.refs_3_), channel_id=1, source_target_pairs={{0,4},{1,5},{2,6},{3,7},{4,0},{5,1},{6,2},{7,3},{16,20},{17,21},{1... | collective-permute-start | bytes 1572872 | tf_op jit(solution)/shard_map/ppermute | solution.py:41
  40.4 9.2 %collective-permute-start.14 = (bf16[2,256,512]{2,1,0:T(8,128)(2,1)S(1)}, bf16[2,256,512]{2,1,0:T(8,128)(2,1)S(1)}, u32[]{:S(2)}, u32[]{:S(2)}) collective-permute-start(bf16[2,256,512]{2,1,0:T(8,128)(2,1)S(1)} %collective-permute-done.3.refs_0_), channel_id=1, source_target_pairs={{0,8},{1,9},{2,10},{3,11},{4,20},{5,21},{6,22},{7,23},{16,0},{17,1... | collective-permute-start | bytes 1572872 | tf_op jit(solution)/shard_map/ppermute | solution.py:33
  44.5 12.7 %collective-permute-start.4 = (bf16[2,256,512]{2,1,0:T(8,128)(2,1)S(1)}, bf16[2,256,512]{2,1,0:T(8,128)(2,1)S(1)}, u32[]{:S(2)}, u32[]{:S(2)}) collective-permute-start(bf16[2,256,512]{2,1,0:T(8,128)(2,1)S(1)} %collective-permute-done.3.refs_0_), channel_id=1, source_target_pairs={{0,1},{1,2},{2,3},{3,0},{4,5},{5,6},{6,7},{7,4},{16,17},{17,18},{1... | collective-permute-start | bytes 1572872 | tf_op jit(solution)/shard_map/ppermute | solution.py:37
  49.6 10.5 %collective-permute-start.29 = (bf16[2,256,512]{2,1,0:T(8,128)(2,1)S(1)}, bf16[2,256,512]{2,1,0:T(8,128)(2,1)S(1)}, u32[]{:S(2)}, u32[]{:S(2)}) collective-permute-start(bf16[2,256,512]{2,1,0:T(8,128)(2,1)S(1)} %collective-permute-done.6.refs_2_), channel_id=1, source_target_pairs={{0,4},{1,5},{2,6},{3,7},{4,0},{5,1},{6,2},{7,3},{16,20},{17,21},{1... | collective-permute-start | bytes 1572872 | tf_op jit(solution)/shard_map/ppermute | solution.py:41
  57.2 4.5 %collective-permute-start.23 = (bf16[2,256,512]{2,1,0:T(8,128)(2,1)S(1)}, bf16[2,256,512]{2,1,0:T(8,128)(2,1)S(1)}, u32[]{:S(2)}, u32[]{:S(2)}) collective-permute-start(bf16[2,256,512]{2,1,0:T(8,128)(2,1)S(1)} %collective-permute-done.3.refs_0_), channel_id=1, source_target_pairs={{0,4},{1,5},{2,6},{3,7},{4,0},{5,1},{6,2},{7,3},{16,20},{17,21},{1... | collective-permute-start | bytes 1572872 | tf_op jit(solution)/shard_map/ppermute | solution.py:41
  57.2 20.4 %collective-permute-start.15 = (bf16[2,256,512]{2,1,0:T(8,128)(2,1)S(1)}, bf16[2,256,512]{2,1,0:T(8,128)(2,1)S(1)}, u32[]{:S(2)}, u32[]{:S(2)}) collective-permute-start(bf16[2,256,512]{2,1,0:T(8,128)(2,1)S(1)} %collective-permute-done.4.refs_0_), channel_id=1, source_target_pairs={{0,16},{1,17},{2,18},{3,19},{4,12},{5,13},{6,14},{7,15},{16,24},{1... | collective-permute-start | bytes 1572872 | tf_op jit(solution)/shard_map/ppermute | solution.py:33
  58.7 19.0 %collective-permute-start.22 = (bf16[2,256,512]{2,1,0:T(8,128)(2,1)S(1)}, bf16[2,256,512]{2,1,0:T(8,128)(2,1)S(1)}, u32[]{:S(2)}, u32[]{:S(2)}) collective-permute-start(bf16[2,256,512]{2,1,0:T(8,128)(2,1)S(1)} %collective-permute-done.13.refs_1_), channel_id=1, source_target_pairs={{0,16},{1,17},{2,18},{3,19},{4,12},{5,13},{6,14},{7,15},{16,24},{1... | collective-permute-start | bytes 1572872 | tf_op jit(solution)/shard_map/ppermute | solution.py:33
  59.6 19.1 %collective-permute-start.5 = (bf16[2,256,512]{2,1,0:T(8,128)(2,1)S(1)}, bf16[2,256,512]{2,1,0:T(8,128)(2,1)S(1)}, u32[]{:S(2)}, u32[]{:S(2)}) collective-permute-start(bf16[2,256,512]{2,1,0:T(8,128)(2,1)S(1)} %collective-permute-done.1.refs_1_), channel_id=1, source_target_pairs={{0,1},{1,2},{2,3},{3,0},{4,5},{5,6},{6,7},{7,4},{16,17},{17,18},{1... | collective-permute-start | bytes 1572872 | tf_op jit(solution)/shard_map/ppermute | solution.py:37
  60.1 20.8 %collective-permute-start.17 = (bf16[2,256,512]{2,1,0:T(8,128)(2,1)S(1)}, bf16[2,256,512]{2,1,0:T(8,128)(2,1)S(1)}, u32[]{:S(2)}, u32[]{:S(2)}) collective-permute-start(bf16[2,256,512]{2,1,0:T(8,128)(2,1)S(1)} %collective-permute-done.4.refs_0_), channel_id=1, source_target_pairs={{0,8},{1,9},{2,10},{3,11},{4,20},{5,21},{6,22},{7,23},{16,0},{17,1... | collective-permute-start | bytes 1572872 | tf_op jit(solution)/shard_map/ppermute | solution.py:33
  61.7 18.9 %collective-permute-start.24 = (bf16[2,256,512]{2,1,0:T(8,128)(2,1)S(1)}, bf16[2,256,512]{2,1,0:T(8,128)(2,1)S(1)}, u32[]{:S(2)}, u32[]{:S(2)}) collective-permute-start(bf16[2,256,512]{2,1,0:T(8,128)(2,1)S(1)} %collective-permute-done.13.refs_1_), channel_id=1, source_target_pairs={{0,4},{1,5},{2,6},{3,7},{4,0},{5,1},{6,2},{7,3},{16,20},{17,21},{1... | collective-permute-start | bytes 1572872 | tf_op jit(solution)/shard_map/ppermute | solution.py:41
  77.6 3.2 %collective-permute-start.26 = (bf16[2,256,512]{2,1,0:T(8,128)(2,1)S(1)}, bf16[2,256,512]{2,1,0:T(8,128)(2,1)S(1)}, u32[]{:S(2)}, u32[]{:S(2)}) collective-permute-start(bf16[2,256,512]{2,1,0:T(8,128)(2,1)S(1)} %collective-permute-done.14.refs_3_), channel_id=1, source_target_pairs={{0,4},{1,5},{2,6},{3,7},{4,0},{5,1},{6,2},{7,3},{16,20},{17,21},{1... | collective-permute-start | bytes 1572872 | tf_op jit(solution)/shard_map/ppermute | solution.py:41
  77.7 3.8 %collective-permute-start.18 = (bf16[2,256,512]{2,1,0:T(8,128)(2,1)S(1)}, bf16[2,256,512]{2,1,0:T(8,128)(2,1)S(1)}, u32[]{:S(2)}, u32[]{:S(2)}) collective-permute-start(bf16[2,256,512]{2,1,0:T(8,128)(2,1)S(1)} %collective-permute-done.4.refs_0_), channel_id=1, source_target_pairs={{0,4},{1,5},{2,6},{3,7},{4,0},{5,1},{6,2},{7,3},{16,20},{17,21},{1... | collective-permute-start | bytes 1572872 | tf_op jit(solution)/shard_map/ppermute | solution.py:41
  78.6 9.2 %collective-permute-start.16 = (bf16[2,256,512]{2,1,0:T(8,128)(2,1)S(1)}, bf16[2,256,512]{2,1,0:T(8,128)(2,1)S(1)}, u32[]{:S(2)}, u32[]{:S(2)}) collective-permute-start(bf16[2,256,512]{2,1,0:T(8,128)(2,1)S(1)} %collective-permute-done.15.refs_1_), channel_id=1, source_target_pairs={{0,16},{1,17},{2,18},{3,19},{4,12},{5,13},{6,14},{7,15},{16,24},{1... | collective-permute-start | bytes 1572872 | tf_op jit(solution)/shard_map/ppermute | solution.py:33
  80.6 7.3 %copy-start = (bf16[2,256,512]{2,1,0:T(8,128)(2,1)S(1)}, bf16[2,256,512]{2,1,0:T(8,128)(2,1)}, u32[]{:S(2)}) copy-start(bf16[2,256,512]{2,1,0:T(8,128)(2,1)} %refs_0_.1) | copy-start | bytes 1572868
  80.6 15.3 %collective-permute-start.7 = (bf16[2,256,512]{2,1,0:T(8,128)(2,1)S(1)}, bf16[2,256,512]{2,1,0:T(8,128)(2,1)S(1)}, u32[]{:S(2)}, u32[]{:S(2)}) collective-permute-start(bf16[2,256,512]{2,1,0:T(8,128)(2,1)S(1)} %collective-permute-done.6.refs_2_), channel_id=1, source_target_pairs={{0,1},{1,2},{2,3},{3,0},{4,5},{5,6},{6,7},{7,4},{16,17},{17,18},{1... | collective-permute-start | bytes 1572872 | tf_op jit(solution)/shard_map/ppermute | solution.py:37
  80.8 12.1 %collective-permute-start.19 = (bf16[2,256,512]{2,1,0:T(8,128)(2,1)S(1)}, bf16[2,256,512]{2,1,0:T(8,128)(2,1)S(1)}, u32[]{:S(2)}, u32[]{:S(2)}) collective-permute-start(bf16[2,256,512]{2,1,0:T(8,128)(2,1)S(1)} %collective-permute-done.15.refs_1_), channel_id=1, source_target_pairs={{0,4},{1,5},{2,6},{3,7},{4,0},{5,1},{6,2},{7,3},{16,20},{17,21},{1... | collective-permute-start | bytes 1572872 | tf_op jit(solution)/shard_map/ppermute | solution.py:41
  80.9 11.4 %collective-permute-start.25 = (bf16[2,256,512]{2,1,0:T(8,128)(2,1)S(1)}, bf16[2,256,512]{2,1,0:T(8,128)(2,1)S(1)}, u32[]{:S(2)}, u32[]{:S(2)}) collective-permute-start(bf16[2,256,512]{2,1,0:T(8,128)(2,1)S(1)} %collective-permute-done.22.refs_2_), channel_id=1, source_target_pairs={{0,4},{1,5},{2,6},{3,7},{4,0},{5,1},{6,2},{7,3},{16,20},{17,21},{1... | collective-permute-start | bytes 1572872 | tf_op jit(solution)/shard_map/ppermute | solution.py:41
  81.4 11.6 %collective-permute-start.21 = (bf16[2,256,512]{2,1,0:T(8,128)(2,1)S(1)}, bf16[2,256,512]{2,1,0:T(8,128)(2,1)S(1)}, u32[]{:S(2)}, u32[]{:S(2)}) collective-permute-start(bf16[2,256,512]{2,1,0:T(8,128)(2,1)S(1)} %collective-permute-done.17.refs_3_), channel_id=1, source_target_pairs={{0,4},{1,5},{2,6},{3,7},{4,0},{5,1},{6,2},{7,3},{16,20},{17,21},{1... | collective-permute-start | bytes 1572872 | tf_op jit(solution)/shard_map/ppermute | solution.py:41
  87.9 12.5 %collective-permute-start.20 = (bf16[2,256,512]{2,1,0:T(8,128)(2,1)S(1)}, bf16[2,256,512]{2,1,0:T(8,128)(2,1)S(1)}, u32[]{:S(2)}, u32[]{:S(2)}) collective-permute-start(bf16[2,256,512]{2,1,0:T(8,128)(2,1)S(1)} %collective-permute-done.16.refs_2_), channel_id=1, source_target_pairs={{0,4},{1,5},{2,6},{3,7},{4,0},{5,1},{6,2},{7,3},{16,20},{17,21},{1... | collective-permute-start | bytes 1572872 | tf_op jit(solution)/shard_map/ppermute | solution.py:41
  92.4 12.5 %collective-permute-start.9 = (bf16[2,256,512]{2,1,0:T(8,128)(2,1)S(1)}, bf16[2,256,512]{2,1,0:T(8,128)(2,1)S(1)}, u32[]{:S(2)}, u32[]{:S(2)}) collective-permute-start(bf16[2,256,512]{2,1,0:T(8,128)(2,1)S(1)} %collective-permute-done.refs_0_), channel_id=1, source_target_pairs={{0,4},{1,5},{2,6},{3,7},{4,0},{5,1},{6,2},{7,3},{16,20},{17,21},{1... | collective-permute-start | bytes 1572872 | tf_op jit(solution)/shard_map/ppermute | solution.py:41
  92.9 11.9 %collective-permute-start.12 = (bf16[2,256,512]{2,1,0:T(8,128)(2,1)S(1)}, bf16[2,256,512]{2,1,0:T(8,128)(2,1)S(1)}, u32[]{:S(2)}, u32[]{:S(2)}) collective-permute-start(bf16[2,256,512]{2,1,0:T(8,128)(2,1)S(1)} %collective-permute-done.8.refs_3_), channel_id=1, source_target_pairs={{0,4},{1,5},{2,6},{3,7},{4,0},{5,1},{6,2},{7,3},{16,20},{17,21},{1... | collective-permute-start | bytes 1572872 | tf_op jit(solution)/shard_map/ppermute | solution.py:41
  93.0 11.8 %collective-permute-start.10 = (bf16[2,256,512]{2,1,0:T(8,128)(2,1)S(1)}, bf16[2,256,512]{2,1,0:T(8,128)(2,1)S(1)}, u32[]{:S(2)}, u32[]{:S(2)}) collective-permute-start(bf16[2,256,512]{2,1,0:T(8,128)(2,1)S(1)} %collective-permute-done.5.refs_1_), channel_id=1, source_target_pairs={{0,4},{1,5},{2,6},{3,7},{4,0},{5,1},{6,2},{7,3},{16,20},{17,21},{1... | collective-permute-start | bytes 1572872 | tf_op jit(solution)/shard_map/ppermute | solution.py:41
  95.9 9.0 %collective-permute-start.11 = (bf16[2,256,512]{2,1,0:T(8,128)(2,1)S(1)}, bf16[2,256,512]{2,1,0:T(8,128)(2,1)S(1)}, u32[]{:S(2)}, u32[]{:S(2)}) collective-permute-start(bf16[2,256,512]{2,1,0:T(8,128)(2,1)S(1)} %collective-permute-done.7.refs_2_), channel_id=1, source_target_pairs={{0,4},{1,5},{2,6},{3,7},{4,0},{5,1},{6,2},{7,3},{16,20},{17,21},{1... | collective-permute-start | bytes 1572872 | tf_op jit(solution)/shard_map/ppermute | solution.py:41

commit v2 on v0

v2 whole, which is shorter than its diff:
```python
import functools

import jax
import jax.numpy as jnp
from jax import lax
from jax.experimental import pallas as pl
from jax.experimental.pallas import tpu as pltpu
from jax.sharding import PartitionSpec as P

AXES = ("row", "col")


def chip_at(place, chips):
    place = place % chips
    return 2 * place if 2 * place < chips else 2 * (chips - 1 - place) + 1


class Moves:
    def __init__(self, rows, cols):
        self.chips, self.cols = rows // 2, cols

    def every(self):
        for place in range(self.chips):
            for core in range(2):
                for layer in range(self.cols):
                    yield place, core, layer

    def device(self, place, core, layer):
        return (chip_at(place, self.chips) * 2 + core) * self.cols + layer % self.cols

    def ring(self, value, step):
        pairs = [(self.device(p, k, z), self.device(p + (step if k == 0 else -step), k, z)) for p, k, z in self.every()]
        return lax.ppermute(value, AXES, pairs)

    def along(self, value, step):
        pairs = [(self.device(p, k, z), self.device(p, k, z + step)) for p, k, z in self.every()]
        return lax.ppermute(value, AXES, pairs)

    def other(self, value):
        pairs = [(self.device(p, k, z), self.device(p, 1 - k, z)) for p, k, z in self.every()]
        return lax.ppermute(value, AXES, pairs)


def after(value, *earlier):
    return lax.optimization_barrier((value,) + earlier)[0]


class Part:
    def __init__(self, stage, terms, begun=None, finish=True):
        self.stage, self.terms, self.begun, self.finish = stage, terms, begun, finish


def parts_kernel(plan, rows, cols, n_arrays, n_outs, fresh, first, second, *refs):
    refs = list(refs)
    arrays = [refs.pop(0) for _ in range(n_arrays)]
    begun = [refs.pop(0) if has else None for _, _, has, _ in plan]
    if n_outs and not fresh:
        del refs[:2]
    outs = [refs.pop(0) for _ in range(n_outs)]
    sums = [None if finish else refs.pop(0) for _, _, _, finish in plan]
    chips = rows // 2
    depth, width = arrays[0].shape[1:]
    g, bands = first.shape[0], first.shape[1] // 2
    row, layer = lax.axis_index("row"), lax.axis_index("col")
    chip, core = row // 2, row % 2
    place = jnp.where(chip % 2 == 0, chip // 2, chips - 1 - chip // 2)
    copies = []
    for i, (stage, terms, _, finish) in enumerate(plan):
        total = jnp.zeros((4 * g, width), jnp.float32) if begun[i] is None else begun[i][...]
        for hop, mine, array, number in terms:
            owner_core = core if mine else 1 - core
            at = (place + chips + jnp.where(owner_core == 0, -hop, hop)) % chips
            owner = jnp.where(2 * at < chips, 2 * at, 2 * (chips - 1 - at) + 1) * 2 + owner_core
            real = pl.ds(pl.multiple_of(owner * depth, depth), depth)
            imag = pl.ds(pl.multiple_of(bands + owner * depth, depth), depth)
            left = [jnp.concatenate([x[:, real], -x[:, imag]], 1) for x in (first, second)]
            left += [jnp.concatenate([x[:, imag], x[:, real]], 1) for x in (first, second)]
            right = arrays[array][2 * number : 2 * number + 2].reshape(2 * depth, width)
            total += jnp.dot(jnp.concatenate(left, 0), right, preferred_element_type=jnp.float32)
        if not finish:
            sums[i][...] = total
            continue
        rounded = total.astype(outs[0].dtype)
        columns = pl.ds(pl.multiple_of(((layer + cols - stage) % cols) * width, width), width)
        for half in range(2):
            tile, sem = refs.pop(0), refs.pop(0)
            tile[:, 0, :] = rounded[half * g : (half + 1) * g]
            tile[:, 1, :] = rounded[(2 + half) * g : (3 + half) * g]
            copy = pltpu.make_async_copy(tile, outs[half].at[:, :, columns], sem)
            copy.start()
            copies.append(copy)
    for copy in copies:
        copy.wait()


def run_parts(parts, rows, cols, lefts, like, outs=None):
    g = like.shape[0]
    fresh = outs is None
    finishing = sum(p.finish for p in parts)
    vmem, hbm = pl.BlockSpec(memory_space=pltpu.VMEM), pl.BlockSpec(memory_space=pl.ANY)
    arrays = list({id(t[2]): t[2] for p in parts for t in p.terms}.values())
    index = {id(a): i for i, a in enumerate(arrays)}
    depth, width = arrays[0].shape[1:]
    operands = [*lefts, *arrays, *(p.begun for p in parts if p.begun is not None)]
    in_specs = [vmem] * len(operands)
    out_shape, out_specs, scratch, aliases = [], [], [], {}
    if finishing:
        if not fresh:
            aliases = {len(operands): 0, len(operands) + 1: 1}
            operands, in_specs = [*operands, *outs], [*in_specs, hbm, hbm]
        out_shape, out_specs = [jax.ShapeDtypeStruct(like.shape, like.dtype)] * 2, [hbm, hbm]
        scratch = [pltpu.VMEM((g, 2, width), like.dtype), pltpu.SemaphoreType.DMA] * 2 * finishing
    sums = len(parts) - finishing
    out_shape += [jax.ShapeDtypeStruct((4 * g, width), jnp.float32)] * sums
    out_specs += [vmem] * sums
    count = sum(len(p.terms) for p in parts)
    plan = [(p.stage, [(h, m, index[id(a)], n) for h, m, a, n in p.terms], p.begun is not None, p.finish) for p in parts]
    result = pl.pallas_call(
        functools.partial(parts_kernel, plan, rows, cols, len(arrays), 2 if finishing else 0, fresh),
        out_shape=out_shape,
        in_specs=in_specs,
        out_specs=out_specs,
        scratch_shapes=scratch,
        input_output_aliases=aliases,
        compiler_params=pltpu.CompilerParams(vmem_limit_bytes=28 * 2**20),
        cost_estimate=pl.CostEstimate(flops=2 * 8 * g * depth * width * count, bytes_accessed=2**20 * count, transcendentals=0),
    )(*operands)
    return (tuple(result[:2]), result[2:]) if finishing else (outs, result)


def shards(rows, cols, orbitals, applied, ritz):
    moves = Moves(rows, cols)
    chips = rows // 2
    ahead, back = chips // 2, (chips - 1) // 2
    hops = [*range(ahead + 1), *(-h for h in range(1, back + 1))]
    lefts = [x.reshape(x.shape[0], -1) for x in (orbitals, applied)]
    run = functools.partial(run_parts, rows=rows, cols=cols, lefts=lefts, like=orbitals)

    final = cols + chips - 3
    distances = [*range(cols - 1), -1]
    mine, theirs = {(0, 0): (ritz, 0)}, {}

    def bundle(keys, gate):
        values = [lax.slice_in_dim(a, 2 * n, 2 * n + 2) if a.shape[0] > 2 else a for a, n in (mine[key] for key in keys)]
        if gate:
            values = [after(v, *gate) for v in values]
        return jnp.concatenate(values, 0) if len(values) > 1 else values[0]

    def move(how, into, sources, keys, gate, name):
        if not keys:
            return ()
        with jax.named_scope(name):
            value = how(bundle(sources, gate))
        into.update({key: (value, number) for number, key in enumerate(keys)})
        return (value,)

    def part(layer, hops, begun=None, finish=True):
        return Part(layer, [(h, whose is mine, *whose[layer, h]) for whose in (mine, theirs) for h in hops], begun, finish)

    def complete(layer):
        return [*range(chips - 1), -1] if layer in (0, -1) else [*range(chips)]

    state = {"outs": None}
    sums, used = {}, {d: [] for d in distances}

    def products(keys):
        parts = []
        for d in distances:
            hops = [h for h in complete(d) if (d, h) in keys and h not in used[d]]
            if hops:
                used[d] += hops
                parts.append(part(d, hops, sums.pop(d, None), len(used[d]) == len(complete(d))))
        parts.sort(key=lambda p: p.finish)
        state["outs"], kept = run(parts, outs=state["outs"])
        unfinished = [p for p in parts if not p.finish]
        sums.update({p.stage: s for p, s in zip(unfinished, kept, strict=True)})
        return kept[0] if unfinished else state["outs"][0]

    def tiny(value, number):
        at = 16 * (number % (ritz.shape[1] // 16))
        with jax.named_scope("token"):
            return moves.other(after(lax.slice(ritz, (0, at, 0), (1, at + 16, 128)), value))

    along_gate = gate = ()
    fresh = [(0, 0)]
    for r in range(1, final + 1):
        if r < cols - 1:
            layer, hop, step = r, 0, 1
        else:
            layer, hop, step = -1, r - (cols - 1), -1
        source = (layer - step, hop)
        z = move(lambda v: moves.along(v, step), mine, [source], [(layer, hop)], along_gate, f"along{layer}_{hop}")
        ring = [(d, r - d) for d in range(cols - 1) if 1 <= r - d <= (chips - 2 if d == 0 else chips - 1)]
        p = move(lambda v: moves.ring(v, 1), mine, [(d, h - 1) for d, h in ring], ring, gate, f"ring{r}")
        back = {1: [(0, -1)], final: [(-1, -1)]}.get(r, [])
        m = move(lambda v: moves.ring(v, -1), mine, [(d, 0) for d, _ in back], back, gate, f"back{r}")
        e = move(moves.other, theirs, fresh, fresh, gate, f"core{r}")
        fresh_before, fresh = fresh, [*ring, (layer, hop), *back]
        token = ()
        held = set(theirs) - set(fresh_before)
        if r >= chips:
            ran = products(held)
            if r == final:
                ran = products(set(theirs))
            token = (tiny(ran, r),)
        along_gate = (*p, *m, *e, *token, *(lefts if r == 1 else ()))
        gate = (*along_gate, *z)
    move(moves.other, theirs, fresh, fresh, token, "core_last")
    products(set(theirs))
    return state["outs"]


def solution(mesh):
    rows, cols = mesh.shape["row"], mesh.shape["col"]
    whole = P(AXES, None, None)
    return jax.shard_map(
        functools.partial(shards, rows, cols),
        mesh=mesh,
        in_specs=(whole, whole, P(None, "row", "col")),
        out_specs=(whole, whole),
        check_vma=False,
    )
```

time: 208 us -> 92 us (0.44)
  waiting for transfers between devices: 138 us -> 49.3 us
  matrix products: 26.9 us -> 0 us
  starting transfers between devices: 0.08 us -> 19.7 us
  local copies, waits for them, and re-layouts: 21.6 us -> 3.56 us
  Pallas kernels: 0 us -> 17.2 us
  between operations: 14.1 us -> 0.96 us
  other arithmetic: 7.14 us -> 1.13 us
    all_gather x2 -> x0, waiting for transfers between devices: 138 us -> none  [the longest x1 87.5 us: shards(): shard_piece = lax.all_gather(strip, 'row', axis=1, tiled=True)]
    ppermute x0 -> x20, waiting for transfers between devices: none -> 49.3 us  [the longest x7 30 us: ring(): return lax.ppermute(value, AXES, pairs)]
    dot_general x2 -> x0, matrix products: 26.9 us -> none  [the longest x1 14.3 us: shards(): jnp.dot(imag_cols, lower_half, preferred_element_type=jnp.float32)]
    ppermute x0 -> x20, starting transfers between devices: none -> 19.7 us  [the longest x5 11.5 us: along(): return lax.ppermute(value, AXES, pairs)]
    pallas_call x0 -> x4, Pallas kernels: none -> 17.2 us  [run_parts(): pl.pallas_call(functools.partial(parts_kernel, plan, rows, cols, len(arra...]
    squeeze x1 -> x0, local copies, waits for them, and re-layouts: 11.8 us -> none  [shards(): upper_half = jnp.concatenate([shard_piece[0], shard_piece[1]], 1)]
    neg x1 -> x0, other arithmetic: 7.14 us -> none  [shards(): lower_half = jnp.concatenate([-shard_piece[1], shard_piece[0]], 1)]
    slice x3 -> x4, local copies, waits for them, and re-layouts: 6.8 us -> 0.21 us  [the longest x3 0.21 us: bundle(): lax.slice_in_dim(a, 2 * n, 2 * n + 2)]
  transfers between devices with their start and end apart: 2 -> 20, of which waited for: 2 -> 12; matrix products, arithmetic and copies ran while one was open for 1% -> 4% of each run, Pallas kernels for 0% -> 14%
where the time goes in v2:
time: 92 us; the launch traced here: 91.9 us
  waiting for transfers between devices  49.3 us (54%)
  starting transfers between devices  19.7 us (21%)
  Pallas kernels  17.2 us (19%)
  local copies, waits for them, and re-layouts  3.56 us (4%)
  other arithmetic  1.13 us (1%)
  between operations  0.96 us (1%)
    ppermute x7, waiting for transfers between devices, ring(): return lax.ppermute(value, AXES, pairs)  30 us
    pallas_call x4, Pallas kernels, run_parts(): pl.pallas_call(functools.partial(parts_kernel, plan, rows, cols, len(arra...  17.2 us
    ppermute x5, waiting for transfers between devices, along(): return lax.ppermute(value, AXES, pairs)  14.7 us
    ppermute x5, starting transfers between devices, along(): return lax.ppermute(value, AXES, pairs)  11.5 us
    ppermute x7, starting transfers between devices, ring(): return lax.ppermute(value, AXES, pairs)  7.24 us
    ppermute x8, waiting for transfers between devices, other(): return lax.ppermute(value, AXES, pairs)  4.55 us
    unnamed x6, local copies, waits for them, and re-layouts  3.35 us
  transfers between devices with their start and end apart: 20, of which 12 were waited for; matrix products, arithmetic and copies ran while one was open for 4% of the time, Pallas kernels for 14%

profile of v2, /device:TPU:0, one launch (start us, length us, event | category | flops | bytes accessed | tf_op | source)
XLA Modules:
  0.0 91.9 jit_solution(8425161824152244082)
XLA Ops:
  0.6 3.1 %collective-permute-start.3 = (bf16[2,256,512]{2,1,0:T(8,128)(2,1)}, bf16[2,256,512]{2,1,0:T(8,128)(2,1)S(1)}, u32[]{:S(2)}, u32[]{:S(2)}) collective-permute-start(bf16[2,256,512]{2,1,0:T(8,128)(2,1)} %refs_5_.1), channel_id=1, source_target_pairs={{0,1},{1,2},{2,3},{3,0},{4,5},{5,6},{6,7},{7,4},{16,17},{17,18},{1... | collective-permute-start | bytes 1572872 | tf_op jit(solution)/shard_map/along1_0/ppermute | solution.py:37
  3.7 1.5 %collective-permute-start.1 = (bf16[2,256,512]{2,1,0:T(8,128)(2,1)}, bf16[2,256,512]{2,1,0:T(8,128)(2,1)S(1)}, u32[]{:S(2)}, u32[]{:S(2)}) collective-permute-start(bf16[2,256,512]{2,1,0:T(8,128)(2,1)} %refs_5_.1), channel_id=1, source_target_pairs={{0,8},{1,9},{2,10},{3,11},{4,20},{5,21},{6,22},{7,23},{16,0},{17,1... | collective-permute-start | bytes 1572872 | tf_op jit(solution)/shard_map/back1/ppermute | solution.py:33
  5.2 0.5 collective-permute-start
  5.7 2.2 %copy.9 = bf16[24,8,2,2048]{3,1,2,0:T(8,128)(2,1)S(1)} copy(bf16[24,8,2,2048]{3,2,1,0:T(2,128)(2,1)} %bitcast.12) | data formatting | bytes 3145728
  7.9 0.6 copy.10
  8.6 9.3 %collective-permute-done.3.refs_0_ = bf16[2,256,512]{2,1,0:T(8,128)(2,1)S(1)} collective-permute-done((bf16[2,256,512]{2,1,0:T(8,128)(2,1)}, bf16[2,256,512]{2,1,0:T(8,128)(2,1)S(1)}, u32[]{:S(2)}, u32[]{:S(2)}) %collective-permute-start.3) | collective-permute-done | bytes 524320 | tf_op jit(solution)/shard_map/along1_0/ppermute | solution.py:37
  17.9 0.1 collective-permute-done.1.refs_7_
  18.0 0.3 collective-permute-done.refs_6_
  18.3 0.2 pad_maximum_fusion
  18.4 0.3 collective-permute-start.5
  18.8 0.1 pad_maximum_fusion.5
  18.9 1.6 %collective-permute-start.4 = (bf16[4,256,512]{2,1,0:T(8,128)(2,1)S(1)}, bf16[4,256,512]{2,1,0:T(8,128)(2,1)S(1)}, u32[]{:S(2)}, u32[]{:S(2)}) collective-permute-start(bf16[4,256,512]{2,1,0:T(8,128)(2,1)S(1)} %pad_maximum_fusion.5), channel_id=1, source_target_pairs={{0,16},{1,17},{2,18},{3,19},{4,12},{5,13},{6,14},{7,15},{16,24},{1... | collective-permute-start | bytes 3145736 | tf_op jit(solution)/shard_map/ring2/ppermute | solution.py:33
  20.4 1.6 %collective-permute-start.6 = (bf16[2,256,512]{2,1,0:T(8,128)(2,1)S(1)}, bf16[2,256,512]{2,1,0:T(8,128)(2,1)S(1)}, u32[]{:S(2)}, u32[]{:S(2)}) collective-permute-start(bf16[2,256,512]{2,1,0:T(8,128)(2,1)S(1)} %collective-permute-done.3.refs_0_), channel_id=1, source_target_pairs={{0,1},{1,2},{2,3},{3,0},{4,5},{5,6},{6,7},{7,4},{16,17},{17,18},{1... | collective-permute-start | bytes 1572872 | tf_op jit(solution)/shard_map/along2_0/ppermute | solution.py:37
  22.0 11.7 %collective-permute-done.4.refs_1_ = bf16[4,256,512]{2,1,0:T(8,128)(2,1)S(1)} collective-permute-done((bf16[4,256,512]{2,1,0:T(8,128)(2,1)S(1)}, bf16[4,256,512]{2,1,0:T(8,128)(2,1)S(1)}, u32[]{:S(2)}, u32[]{:S(2)}) %collective-permute-start.4) | collective-permute-done | bytes 1048608 | tf_op jit(solution)/shard_map/ring2/ppermute | solution.py:33
  33.7 0.1 fusion.2
  33.8 2.5 %collective-permute-done.6.refs_4_ = bf16[2,256,512]{2,1,0:T(8,128)(2,1)S(1)} collective-permute-done((bf16[2,256,512]{2,1,0:T(8,128)(2,1)S(1)}, bf16[2,256,512]{2,1,0:T(8,128)(2,1)S(1)}, u32[]{:S(2)}, u32[]{:S(2)}) %collective-permute-start.6) | collective-permute-done | bytes 524320 | tf_op jit(solution)/shard_map/along2_0/ppermute | solution.py:37
  36.3 0.2 pad_maximum_fusion.1
  36.4 0.1 collective-permute-start.8
  36.5 0.1 pad_maximum_fusion.6
  36.6 0.3 collective-permute-start.7
  37.0 0.5 copy-done
  37.5 0.5 collective-permute-start.9
  38.0 13.5 %collective-permute-done.7.refs_0_ = bf16[4,256,512]{2,1,0:T(8,128)(2,1)S(1)} collective-permute-done((bf16[4,256,512]{2,1,0:T(8,128)(2,1)S(1)}, bf16[4,256,512]{2,1,0:T(8,128)(2,1)S(1)}, u32[]{:S(2)}, u32[]{:S(2)}) %collective-permute-start.7) | collective-permute-done | bytes 1048608 | tf_op jit(solution)/shard_map/ring3/ppermute | solution.py:33
  51.5 0.1 fusion.1
  51.5 0.3 collective-permute-done.9.refs_2_
  51.8 0.2 pad_maximum_fusion.2
  52.0 0.1 collective-permute-start.11
  52.1 0.1 pad_maximum_fusion.7
  52.2 1.0 %collective-permute-start.10 = (bf16[4,256,512]{2,1,0:T(8,128)(2,1)S(1)}, bf16[4,256,512]{2,1,0:T(8,128)(2,1)S(1)}, u32[]{:S(2)}, u32[]{:S(2)}) collective-permute-start(bf16[4,256,512]{2,1,0:T(8,128)(2,1)S(1)} %pad_maximum_fusion.7), channel_id=1, source_target_pairs={{0,16},{1,17},{2,18},{3,19},{4,12},{5,13},{6,14},{7,15},{16,24},{1... | collective-permute-start | bytes 3145736 | tf_op jit(solution)/shard_map/ring4/ppermute | solution.py:33
  53.2 2.3 %collective-permute-start.13 = (bf16[2,256,512]{2,1,0:T(8,128)(2,1)S(1)}, bf16[2,256,512]{2,1,0:T(8,128)(2,1)S(1)}, u32[]{:S(2)}, u32[]{:S(2)}) collective-permute-start(bf16[2,256,512]{2,1,0:T(8,128)(2,1)S(1)} %collective-permute-done.refs_6_), channel_id=1, source_target_pairs={{0,3},{1,0},{2,1},{3,2},{4,7},{5,4},{6,5},{7,6},{16,19},{17,16},{1... | collective-permute-start | bytes 1572872 | tf_op jit(solution)/shard_map/along-1_1/ppermute | solution.py:37
  55.5 6.9 %shard_map.50 = (bf16[192,2,2048]{2,1,0:T(2,128)(2,1)}, bf16[192,2,2048]{2,1,0:T(2,128)(2,1)}, f32[768,512]{1,0:T(8,128)S(1)}, f32[768,512]{1,0:T(8,128)S(1)}) custom-call(bf16[192,4096]{1,0:T(8,128)(2,1)S(1)} %bitcast.4, bf16[192,4096]{1,0:T(8,128)(2,1)S(1)} %bitcast.8, bf16[2,256,512]{2,1,0:T(8,128)(2,1)S(1)} %collective-permute-done.3.refs_0_, ...), custom_call_target="tpu_custom_call" | custom-call | flops 5637144576 | bytes 14680064 | tf_op jit(solution)/shard_map/pallas_call | solution.py:118
  62.3 0.3 collective-permute-start.12
  62.6 4.4 %collective-permute-done.10.refs_0_ = bf16[4,256,512]{2,1,0:T(8,128)(2,1)S(1)} collective-permute-done((bf16[4,256,512]{2,1,0:T(8,128)(2,1)S(1)}, bf16[4,256,512]{2,1,0:T(8,128)(2,1)S(1)}, u32[]{:S(2)}, u32[]{:S(2)}) %collective-permute-start.10) | collective-permute-done | bytes 1048608 | tf_op jit(solution)/shard_map/ring4/ppermute | solution.py:33
  67.1 0.2 collective-permute-done.13.refs_2_
  67.3 0.2 pad_maximum_fusion.3
  67.5 0.1 collective-permute-start.15
  67.5 0.8 collective-permute-start.18
  68.4 4.1 %collective-permute-start.17 = (bf16[2,256,512]{2,1,0:T(8,128)(2,1)S(1)}, bf16[2,256,512]{2,1,0:T(8,128)(2,1)S(1)}, u32[]{:S(2)}, u32[]{:S(2)}) collective-permute-start(bf16[2,256,512]{2,1,0:T(8,128)(2,1)S(1)} %get-tuple-element.61), channel_id=1, source_target_pairs={{0,3},{1,0},{2,1},{3,2},{4,7},{5,4},{6,5},{7,6},{16,19},{17,16},{1... | collective-permute-start | bytes 1572872 | tf_op jit(solution)/shard_map/along-1_2/ppermute | solution.py:37
  72.4 1.5 %collective-permute-start.14 = (bf16[2,256,512]{2,1,0:T(8,128)(2,1)S(1)}, bf16[2,256,512]{2,1,0:T(8,128)(2,1)S(1)}, u32[]{:S(2)}, u32[]{:S(2)}) collective-permute-start(bf16[2,256,512]{2,1,0:T(8,128)(2,1)S(1)} %get-tuple-element.49), channel_id=1, source_target_pairs={{0,16},{1,17},{2,18},{3,19},{4,12},{5,13},{6,14},{7,15},{16,24},{1... | collective-permute-start | bytes 1572872 | tf_op jit(solution)/shard_map/ring5/ppermute | solution.py:33
  73.9 2.6 %shard_map.51 = (f32[768,512]{1,0:T(8,128)S(1)}, f32[768,512]{1,0:T(8,128)S(1)}, f32[768,512]{1,0:T(8,128)S(1)}) custom-call(bf16[192,4096]{1,0:T(8,128)(2,1)S(1)} %bitcast.5, bf16[192,4096]{1,0:T(8,128)(2,1)S(1)} %bitcast.9, bf16[4,256,512]{2,1,0:T(8,128)(2,1)S(1)} %collective-permute-done.7.refs_0_, ...), custom_call_target="tpu_custom_call" | custom-call | flops 2415919104 | bytes 6291456 | tf_op jit(solution)/shard_map/pallas_call | solution.py:118
  76.5 3.7 %shard_map.52 = (bf16[192,2,2048]{2,1,0:T(2,128)(2,1)}, bf16[192,2,2048]{2,1,0:T(2,128)(2,1)}, f32[768,512]{1,0:T(8,128)S(1)}, f32[768,512]{1,0:T(8,128)S(1)}) custom-call(bf16[192,4096]{1,0:T(8,128)(2,1)S(1)} %bitcast.6, bf16[192,4096]{1,0:T(8,128)(2,1)S(1)} %bitcast.10, ...), custom_call_target="tpu_custom_call", output_to_operand_aliasing={{0}: (8, {}), {1}: (9, {})} | custom-call | flops 2415919104 | bytes 6291456 | tf_op jit(solution)/shard_map/pallas_call | solution.py:118
  80.2 0.1 collective-permute-start.16
  80.3 1.1 %collective-permute-done.16 = bf16[1,16,128]{2,1,0:T(8,128)(2,1)S(1)} collective-permute-done((bf16[1,16,128]{2,1,0:T(8,128)(2,1)S(1)}, bf16[1,16,128]{2,1,0:T(8,128)(2,1)S(1)}, u32[]{:S(2)}, u32[]{:S(2)}) %collective-permute-start.16) | collective-permute-done | bytes 4128 | tf_op jit(solution)/shard_map/token/ppermute | solution.py:41
  81.5 2.5 %collective-permute-done.17.refs_2_ = bf16[2,256,512]{2,1,0:T(8,128)(2,1)S(1)} collective-permute-done((bf16[2,256,512]{2,1,0:T(8,128)(2,1)S(1)}, bf16[2,256,512]{2,1,0:T(8,128)(2,1)S(1)}, u32[]{:S(2)}, u32[]{:S(2)}) %collective-permute-start.17) | collective-permute-done | bytes 524320 | tf_op jit(solution)/shard_map/along-1_2/ppermute | solution.py:37
  84.0 0.2 pad_maximum_fusion.4
  84.2 0.1 collective-permute-start.19
  84.3 3.4 %collective-permute-done.19.refs_1_ = bf16[6,256,512]{2,1,0:T(8,128)(2,1)S(1)} collective-permute-done((bf16[6,256,512]{2,1,0:T(8,128)(2,1)S(1)}, bf16[6,256,512]{2,1,0:T(8,128)(2,1)S(1)}, u32[]{:S(2)}, u32[]{:S(2)}) %collective-permute-start.19) | collective-permute-done | bytes 1572896 | tf_op jit(solution)/shard_map/core_last/ppermute | solution.py:41
  87.7 4.1 %shard_map.53 = (bf16[192,2,2048]{2,1,0:T(2,128)(2,1)}, bf16[192,2,2048]{2,1,0:T(2,128)(2,1)}) custom-call(bf16[192,4096]{1,0:T(8,128)(2,1)S(1)} %bitcast.7, bf16[192,4096]{1,0:T(8,128)(2,1)S(1)} %bitcast.11, bf16[2,256,512]{2,1,0:T(8,128)(2,1)S(1)} %collective-permute-done.14.refs_0_, ...), custom_call_target="tpu_custom_call", output_to_operand_aliasing={{0}: (8, {}), {1}: (9, {})} | custom-call | flops 2415919104 | bytes 6291456 | tf_op jit(solution)/shard_map/pallas_call | solution.py:118
  (14 shorter events, 0.1 us)
Async XLA Ops:
  0.6 17.2 %collective-permute-start.3 = (bf16[2,256,512]{2,1,0:T(8,128)(2,1)}, bf16[2,256,512]{2,1,0:T(8,128)(2,1)S(1)}, u32[]{:S(2)}, u32[]{:S(2)}) collective-permute-start(bf16[2,256,512]{2,1,0:T(8,128)(2,1)} %refs_5_.1), channel_id=1, source_target_pairs={{0,1},{1,2},{2,3},{3,0},{4,5},{5,6},{6,7},{7,4},{16,17},{17,18},{1... | collective-permute-start | bytes 1572872 | tf_op jit(solution)/shard_map/along1_0/ppermute | solution.py:37
  3.7 14.2 %collective-permute-start.2 = (bf16[2,256,512]{2,1,0:T(8,128)(2,1)}, bf16[2,256,512]{2,1,0:T(8,128)(2,1)S(1)}, u32[]{:S(2)}, u32[]{:S(2)}) collective-permute-start(bf16[2,256,512]{2,1,0:T(8,128)(2,1)} %refs_5_.1), channel_id=1, source_target_pairs={{0,4},{1,5},{2,6},{3,7},{4,0},{5,1},{6,2},{7,3},{16,20},{17,21},{1... | collective-permute-start | bytes 1572872 | tf_op jit(solution)/shard_map/core1/ppermute | solution.py:41
  3.7 14.3 %collective-permute-start.1 = (bf16[2,256,512]{2,1,0:T(8,128)(2,1)}, bf16[2,256,512]{2,1,0:T(8,128)(2,1)S(1)}, u32[]{:S(2)}, u32[]{:S(2)}) collective-permute-start(bf16[2,256,512]{2,1,0:T(8,128)(2,1)} %refs_5_.1), channel_id=1, source_target_pairs={{0,8},{1,9},{2,10},{3,11},{4,20},{5,21},{6,22},{7,23},{16,0},{17,1... | collective-permute-start | bytes 1572872 | tf_op jit(solution)/shard_map/back1/ppermute | solution.py:33
  5.2 13.1 %collective-permute-start = (bf16[2,256,512]{2,1,0:T(8,128)(2,1)}, bf16[2,256,512]{2,1,0:T(8,128)(2,1)S(1)}, u32[]{:S(2)}, u32[]{:S(2)}) collective-permute-start(bf16[2,256,512]{2,1,0:T(8,128)(2,1)} %refs_5_.1), channel_id=1, source_target_pairs={{0,16},{1,17},{2,18},{3,19},{4,12},{5,13},{6,14},{7,15},{16,24},{1... | collective-permute-start | bytes 1572872 | tf_op jit(solution)/shard_map/ring1/ppermute | solution.py:33
  5.7 2.2 %copy-start.1 = (bf16[192,2,2048]{2,1,0:T(2,128)(2,1)S(1)}, bf16[192,2,2048]{2,1,0:T(2,128)(2,1)}, u32[]{:S(2)}) copy-start(bf16[192,2,2048]{2,1,0:T(2,128)(2,1)} %param.4) | copy-start | bytes 4718596
  18.4 17.8 %collective-permute-start.5 = (bf16[6,256,512]{2,1,0:T(8,128)(2,1)S(1)}, bf16[6,256,512]{2,1,0:T(8,128)(2,1)S(1)}, u32[]{:S(2)}, u32[]{:S(2)}) collective-permute-start(bf16[6,256,512]{2,1,0:T(8,128)(2,1)S(1)} %pad_maximum_fusion), channel_id=1, source_target_pairs={{0,4},{1,5},{2,6},{3,7},{4,0},{5,1},{6,2},{7,3},{16,20},{17,21},{1... | collective-permute-start | bytes 4718600 | tf_op jit(solution)/shard_map/core2/ppermute | solution.py:41
  18.9 14.9 %collective-permute-start.4 = (bf16[4,256,512]{2,1,0:T(8,128)(2,1)S(1)}, bf16[4,256,512]{2,1,0:T(8,128)(2,1)S(1)}, u32[]{:S(2)}, u32[]{:S(2)}) collective-permute-start(bf16[4,256,512]{2,1,0:T(8,128)(2,1)S(1)} %pad_maximum_fusion.5), channel_id=1, source_target_pairs={{0,16},{1,17},{2,18},{3,19},{4,12},{5,13},{6,14},{7,15},{16,24},{1... | collective-permute-start | bytes 3145736 | tf_op jit(solution)/shard_map/ring2/ppermute | solution.py:33
  20.4 15.8 %collective-permute-start.6 = (bf16[2,256,512]{2,1,0:T(8,128)(2,1)S(1)}, bf16[2,256,512]{2,1,0:T(8,128)(2,1)S(1)}, u32[]{:S(2)}, u32[]{:S(2)}) collective-permute-start(bf16[2,256,512]{2,1,0:T(8,128)(2,1)S(1)} %collective-permute-done.3.refs_0_), channel_id=1, source_target_pairs={{0,1},{1,2},{2,3},{3,0},{4,5},{5,6},{6,7},{7,4},{16,17},{17,18},{1... | collective-permute-start | bytes 1572872 | tf_op jit(solution)/shard_map/along2_0/ppermute | solution.py:37
  36.4 1.0 %copy-start = (bf16[2,256,512]{2,1,0:T(8,128)(2,1)S(1)}, bf16[2,256,512]{2,1,0:T(8,128)(2,1)}, u32[]{:S(2)}) copy-start(bf16[2,256,512]{2,1,0:T(8,128)(2,1)} %refs_5_.1) | copy-start | bytes 1572868
  36.4 15.4 %collective-permute-start.8 = (bf16[6,256,512]{2,1,0:T(8,128)(2,1)S(1)}, bf16[6,256,512]{2,1,0:T(8,128)(2,1)S(1)}, u32[]{:S(2)}, u32[]{:S(2)}) collective-permute-start(bf16[6,256,512]{2,1,0:T(8,128)(2,1)S(1)} %pad_maximum_fusion.1), channel_id=1, source_target_pairs={{0,4},{1,5},{2,6},{3,7},{4,0},{5,1},{6,2},{7,3},{16,20},{17,21},{1... | collective-permute-start | bytes 4718600 | tf_op jit(solution)/shard_map/core3/ppermute | solution.py:41
  36.6 14.9 %collective-permute-start.7 = (bf16[4,256,512]{2,1,0:T(8,128)(2,1)S(1)}, bf16[4,256,512]{2,1,0:T(8,128)(2,1)S(1)}, u32[]{:S(2)}, u32[]{:S(2)}) collective-permute-start(bf16[4,256,512]{2,1,0:T(8,128)(2,1)S(1)} %pad_maximum_fusion.6), channel_id=1, source_target_pairs={{0,16},{1,17},{2,18},{3,19},{4,12},{5,13},{6,14},{7,15},{16,24},{1... | collective-permute-start | bytes 3145736 | tf_op jit(solution)/shard_map/ring3/ppermute | solution.py:33
  37.5 14.3 %collective-permute-start.9 = (bf16[2,256,512]{2,1,0:T(8,128)(2,1)S(1)}, bf16[2,256,512]{2,1,0:T(8,128)(2,1)S(1)}, u32[]{:S(2)}, u32[]{:S(2)}) collective-permute-start(bf16[2,256,512]{2,1,0:T(8,128)(2,1)S(1)} %copy-done), channel_id=1, source_target_pairs={{0,3},{1,0},{2,1},{3,2},{4,7},{5,4},{6,5},{7,6},{16,19},{17,16},{1... | collective-permute-start | bytes 1572872 | tf_op jit(solution)/shard_map/along-1_0/ppermute | solution.py:37
  52.0 15.3 %collective-permute-start.11 = (bf16[6,256,512]{2,1,0:T(8,128)(2,1)S(1)}, bf16[6,256,512]{2,1,0:T(8,128)(2,1)S(1)}, u32[]{:S(2)}, u32[]{:S(2)}) collective-permute-start(bf16[6,256,512]{2,1,0:T(8,128)(2,1)S(1)} %pad_maximum_fusion.2), channel_id=1, source_target_pairs={{0,4},{1,5},{2,6},{3,7},{4,0},{5,1},{6,2},{7,3},{16,20},{17,21},{1... | collective-permute-start | bytes 4718600 | tf_op jit(solution)/shard_map/core4/ppermute | solution.py:41
  52.2 14.9 %collective-permute-start.10 = (bf16[4,256,512]{2,1,0:T(8,128)(2,1)S(1)}, bf16[4,256,512]{2,1,0:T(8,128)(2,1)S(1)}, u32[]{:S(2)}, u32[]{:S(2)}) collective-permute-start(bf16[4,256,512]{2,1,0:T(8,128)(2,1)S(1)} %pad_maximum_fusion.7), channel_id=1, source_target_pairs={{0,16},{1,17},{2,18},{3,19},{4,12},{5,13},{6,14},{7,15},{16,24},{1... | collective-permute-start | bytes 3145736 | tf_op jit(solution)/shard_map/ring4/ppermute | solution.py:33
  53.2 14.1 %collective-permute-start.13 = (bf16[2,256,512]{2,1,0:T(8,128)(2,1)S(1)}, bf16[2,256,512]{2,1,0:T(8,128)(2,1)S(1)}, u32[]{:S(2)}, u32[]{:S(2)}) collective-permute-start(bf16[2,256,512]{2,1,0:T(8,128)(2,1)S(1)} %collective-permute-done.refs_6_), channel_id=1, source_target_pairs={{0,3},{1,0},{2,1},{3,2},{4,7},{5,4},{6,5},{7,6},{16,19},{17,16},{1... | collective-permute-start | bytes 1572872 | tf_op jit(solution)/shard_map/along-1_1/ppermute | solution.py:37
  62.3 4.8 %collective-permute-start.12 = (bf16[1,16,128]{2,1,0:T(8,128)(2,1)S(1)}, bf16[1,16,128]{2,1,0:T(8,128)(2,1)S(1)}, u32[]{:S(2)}, u32[]{:S(2)}) collective-permute-start(bf16[1,16,128]{2,1,0:T(8,128)(2,1)S(1)} %get-tuple-element.47), channel_id=1, source_target_pairs={{0,4},{1,5},{2,6},{3,7},{4,0},{5,1},{6,2},{7,3},{16,20},{17,21},{1... | collective-permute-start | bytes 12296 | tf_op jit(solution)/shard_map/token/ppermute | solution.py:41
  67.5 9.1 %collective-permute-start.15 = (bf16[6,256,512]{2,1,0:T(8,128)(2,1)S(1)}, bf16[6,256,512]{2,1,0:T(8,128)(2,1)S(1)}, u32[]{:S(2)}, u32[]{:S(2)}) collective-permute-start(bf16[6,256,512]{2,1,0:T(8,128)(2,1)S(1)} %pad_maximum_fusion.3), channel_id=1, source_target_pairs={{0,4},{1,5},{2,6},{3,7},{4,0},{5,1},{6,2},{7,3},{16,20},{17,21},{1... | collective-permute-start | bytes 4718600 | tf_op jit(solution)/shard_map/core5/ppermute | solution.py:41
  67.5 12.8 %collective-permute-start.18 = (bf16[2,256,512]{2,1,0:T(8,128)(2,1)S(1)}, bf16[2,256,512]{2,1,0:T(8,128)(2,1)S(1)}, u32[]{:S(2)}, u32[]{:S(2)}) collective-permute-start(bf16[2,256,512]{2,1,0:T(8,128)(2,1)S(1)} %collective-permute-done.9.refs_2_), channel_id=1, source_target_pairs={{0,8},{1,9},{2,10},{3,11},{4,20},{5,21},{6,22},{7,23},{16,0},{17,1... | collective-permute-start | bytes 1572872 | tf_op jit(solution)/shard_map/back5/ppermute | solution.py:33
  68.4 15.6 %collective-permute-start.17 = (bf16[2,256,512]{2,1,0:T(8,128)(2,1)S(1)}, bf16[2,256,512]{2,1,0:T(8,128)(2,1)S(1)}, u32[]{:S(2)}, u32[]{:S(2)}) collective-permute-start(bf16[2,256,512]{2,1,0:T(8,128)(2,1)S(1)} %get-tuple-element.61), channel_id=1, source_target_pairs={{0,3},{1,0},{2,1},{3,2},{4,7},{5,4},{6,5},{7,6},{16,19},{17,16},{1... | collective-permute-start | bytes 1572872 | tf_op jit(solution)/shard_map/along-1_2/ppermute | solution.py:37
  72.4 11.6 %collective-permute-start.14 = (bf16[2,256,512]{2,1,0:T(8,128)(2,1)S(1)}, bf16[2,256,512]{2,1,0:T(8,128)(2,1)S(1)}, u32[]{:S(2)}, u32[]{:S(2)}) collective-permute-start(bf16[2,256,512]{2,1,0:T(8,128)(2,1)S(1)} %get-tuple-element.49), channel_id=1, source_target_pairs={{0,16},{1,17},{2,18},{3,19},{4,12},{5,13},{6,14},{7,15},{16,24},{1... | collective-permute-start | bytes 1572872 | tf_op jit(solution)/shard_map/ring5/ppermute | solution.py:33
  80.2 1.2 %collective-permute-start.16 = (bf16[1,16,128]{2,1,0:T(8,128)(2,1)S(1)}, bf16[1,16,128]{2,1,0:T(8,128)(2,1)S(1)}, u32[]{:S(2)}, u32[]{:S(2)}) collective-permute-start(bf16[1,16,128]{2,1,0:T(8,128)(2,1)S(1)} %get-tuple-element.59), channel_id=1, source_target_pairs={{0,4},{1,5},{2,6},{3,7},{4,0},{5,1},{6,2},{7,3},{16,20},{17,21},{1... | collective-permute-start | bytes 12296 | tf_op jit(solution)/shard_map/token/ppermute | solution.py:41
  84.2 3.5 %collective-permute-start.19 = (bf16[6,256,512]{2,1,0:T(8,128)(2,1)S(1)}, bf16[6,256,512]{2,1,0:T(8,128)(2,1)S(1)}, u32[]{:S(2)}, u32[]{:S(2)}) collective-permute-start(bf16[6,256,512]{2,1,0:T(8,128)(2,1)S(1)} %pad_maximum_fusion.4), channel_id=1, source_target_pairs={{0,4},{1,5},{2,6},{3,7},{4,0},{5,1},{6,2},{7,3},{16,20},{17,21},{1... | collective-permute-start | bytes 4718600 | tf_op jit(solution)/shard_map/core_last/ppermute | solution.py:41

commit v3 on v2

--- a/solution.py
+++ b/solution.py
@@ -205,7 +205,10 @@
             token = (tiny(ran, r),)
         along_gate = (*p, *m, *e, *token, *(lefts if r == 1 else ()))
         gate = (*along_gate, *z)
-    move(moves.other, theirs, fresh, fresh, token, "core_last")
+    for key in [key for key in fresh if key != (layer, hop)]:
+        move(moves.other, theirs, [key], [key], token, f"core_last{key[0]}_{key[1]}")
+    products(set(theirs))
+    move(moves.other, theirs, [(layer, hop)], [(layer, hop)], (), "core_end")
     products(set(theirs))
     return state["outs"]
 

time: 92 us -> 89.6 us (0.974)
  starting transfers between devices: 19.7 us -> 18.2 us
  waiting for transfers between devices: 49.3 us -> 47.9 us
    ppermute x8 -> x10, waiting for transfers between devices: 4.55 us -> 0.1 us  [other(): return lax.ppermute(value, AXES, pairs)]
    ppermute x7, waiting for transfers between devices: 30 us -> 34 us  [ring(): return lax.ppermute(value, AXES, pairs)]
    ppermute x5, starting transfers between devices: 11.5 us -> 10.4 us  [along(): return lax.ppermute(value, AXES, pairs)]
    pallas_call x4 -> x5, Pallas kernels: 17.2 us -> 18 us  [run_parts(): pl.pallas_call(functools.partial(parts_kernel, plan, rows, cols, len(arra...]
  transfers between devices with their start and end apart: 20 -> 22, of which waited for: 12 -> 9; matrix products, arithmetic and copies ran while one was open for 4% -> 4% of each run, Pallas kernels for 14% -> 18%
where the time goes in v3:
time: 89.6 us; the launch traced here: 89.5 us
  waiting for transfers between devices  47.9 us (53%)
  starting transfers between devices  18.2 us (20%)
  Pallas kernels  18 us (20%)
  local copies, waits for them, and re-layouts  3.33 us (4%)
  between operations  1 us (1%)
  other arithmetic  0.97 us (1%)
    ppermute x7, waiting for transfers between devices, ring(): return lax.ppermute(value, AXES, pairs)  34 us
    pallas_call x5, Pallas kernels, run_parts(): pl.pallas_call(functools.partial(parts_kernel, plan, rows, cols, len(arra...  18 us
    ppermute x5, waiting for transfers between devices, along(): return lax.ppermute(value, AXES, pairs)  13.9 us
    ppermute x5, starting transfers between devices, along(): return lax.ppermute(value, AXES, pairs)  10.4 us
    ppermute x7, starting transfers between devices, ring(): return lax.ppermute(value, AXES, pairs)  6.82 us
    unnamed x6, local copies, waits for them, and re-layouts  3.12 us
  transfers between devices with their start and end apart: 22, of which 9 were waited for; matrix products, arithmetic and copies ran while one was open for 4% of the time, Pallas kernels for 18%

profile of v3, /device:TPU:0, one launch (start us, length us, event | category | flops | bytes accessed | tf_op | source)
XLA Modules:
  0.0 89.5 jit_solution(14939476486798206826)
XLA Ops:
  0.6 3.1 %collective-permute-start.3 = (bf16[2,256,512]{2,1,0:T(8,128)(2,1)}, bf16[2,256,512]{2,1,0:T(8,128)(2,1)S(1)}, u32[]{:S(2)}, u32[]{:S(2)}) collective-permute-start(bf16[2,256,512]{2,1,0:T(8,128)(2,1)} %refs_5_.1), channel_id=1, source_target_pairs={{0,1},{1,2},{2,3},{3,0},{4,5},{5,6},{6,7},{7,4},{16,17},{17,18},{1... | collective-permute-start | bytes 1572872 | tf_op jit(solution)/shard_map/along1_0/ppermute | solution.py:37
  3.7 1.5 %collective-permute-start = (bf16[2,256,512]{2,1,0:T(8,128)(2,1)}, bf16[2,256,512]{2,1,0:T(8,128)(2,1)S(1)}, u32[]{:S(2)}, u32[]{:S(2)}) collective-permute-start(bf16[2,256,512]{2,1,0:T(8,128)(2,1)} %refs_5_.1), channel_id=1, source_target_pairs={{0,16},{1,17},{2,18},{3,19},{4,12},{5,13},{6,14},{7,15},{16,24},{1... | collective-permute-start | bytes 1572872 | tf_op jit(solution)/shard_map/ring1/ppermute | solution.py:33
  5.2 0.5 collective-permute-start.1
  5.7 2.2 %copy.11 = bf16[24,8,2,2048]{3,1,2,0:T(8,128)(2,1)S(1)} copy(bf16[24,8,2,2048]{3,2,1,0:T(2,128)(2,1)} %bitcast.14) | data formatting | bytes 3145728
  7.9 0.6 copy.12
  8.6 9.3 %collective-permute-done.3.refs_0_ = bf16[2,256,512]{2,1,0:T(8,128)(2,1)S(1)} collective-permute-done((bf16[2,256,512]{2,1,0:T(8,128)(2,1)}, bf16[2,256,512]{2,1,0:T(8,128)(2,1)S(1)}, u32[]{:S(2)}, u32[]{:S(2)}) %collective-permute-start.3) | collective-permute-done | bytes 524320 | tf_op jit(solution)/shard_map/along1_0/ppermute | solution.py:37
  17.9 0.6 collective-permute-done.refs_6_
  18.5 0.2 pad_maximum_fusion
  18.7 0.1 collective-permute-start.5
  18.8 0.1 pad_maximum_fusion.4
  18.9 0.9 %collective-permute-start.4 = (bf16[4,256,512]{2,1,0:T(8,128)(2,1)S(1)}, bf16[4,256,512]{2,1,0:T(8,128)(2,1)S(1)}, u32[]{:S(2)}, u32[]{:S(2)}) collective-permute-start(bf16[4,256,512]{2,1,0:T(8,128)(2,1)S(1)} %pad_maximum_fusion.4), channel_id=1, source_target_pairs={{0,16},{1,17},{2,18},{3,19},{4,12},{5,13},{6,14},{7,15},{16,24},{1... | collective-permute-start | bytes 3145736 | tf_op jit(solution)/shard_map/ring2/ppermute | solution.py:33
  19.8 1.2 %collective-permute-start.6 = (bf16[2,256,512]{2,1,0:T(8,128)(2,1)S(1)}, bf16[2,256,512]{2,1,0:T(8,128)(2,1)S(1)}, u32[]{:S(2)}, u32[]{:S(2)}) collective-permute-start(bf16[2,256,512]{2,1,0:T(8,128)(2,1)S(1)} %collective-permute-done.3.refs_0_), channel_id=1, source_target_pairs={{0,1},{1,2},{2,3},{3,0},{4,5},{5,6},{6,7},{7,4},{16,17},{17,18},{1... | collective-permute-start | bytes 1572872 | tf_op jit(solution)/shard_map/along2_0/ppermute | solution.py:37
  21.0 12.7 %collective-permute-done.4.refs_1_ = bf16[4,256,512]{2,1,0:T(8,128)(2,1)S(1)} collective-permute-done((bf16[4,256,512]{2,1,0:T(8,128)(2,1)S(1)}, bf16[4,256,512]{2,1,0:T(8,128)(2,1)S(1)}, u32[]{:S(2)}, u32[]{:S(2)}) %collective-permute-start.4) | collective-permute-done | bytes 1048608 | tf_op jit(solution)/shard_map/ring2/ppermute | solution.py:33
  33.7 0.1 fusion.2
  33.8 2.5 %collective-permute-done.6.refs_4_ = bf16[2,256,512]{2,1,0:T(8,128)(2,1)S(1)} collective-permute-done((bf16[2,256,512]{2,1,0:T(8,128)(2,1)S(1)}, bf16[2,256,512]{2,1,0:T(8,128)(2,1)S(1)}, u32[]{:S(2)}, u32[]{:S(2)}) %collective-permute-start.6) | collective-permute-done | bytes 524320 | tf_op jit(solution)/shard_map/along2_0/ppermute | solution.py:37
  36.3 0.2 pad_maximum_fusion.1
  36.5 0.1 collective-permute-start.8
  36.6 0.1 pad_maximum_fusion.5
  36.7 0.6 collective-permute-start.7
  37.2 0.3 copy-done
  37.5 0.2 collective-permute-start.9
  37.7 13.8 %collective-permute-done.7.refs_0_ = bf16[4,256,512]{2,1,0:T(8,128)(2,1)S(1)} collective-permute-done((bf16[4,256,512]{2,1,0:T(8,128)(2,1)S(1)}, bf16[4,256,512]{2,1,0:T(8,128)(2,1)S(1)}, u32[]{:S(2)}, u32[]{:S(2)}) %collective-permute-start.7) | collective-permute-done | bytes 1048608 | tf_op jit(solution)/shard_map/ring3/ppermute | solution.py:33
  51.5 0.1 fusion.1
  51.6 0.0 collective-permute-done.9.refs_2_
  51.6 0.2 pad_maximum_fusion.2
  51.8 0.1 collective-permute-start.11
  51.9 0.1 pad_maximum_fusion.6
  52.0 1.2 %collective-permute-start.10 = (bf16[4,256,512]{2,1,0:T(8,128)(2,1)S(1)}, bf16[4,256,512]{2,1,0:T(8,128)(2,1)S(1)}, u32[]{:S(2)}, u32[]{:S(2)}) collective-permute-start(bf16[4,256,512]{2,1,0:T(8,128)(2,1)S(1)} %pad_maximum_fusion.6), channel_id=1, source_target_pairs={{0,16},{1,17},{2,18},{3,19},{4,12},{5,13},{6,14},{7,15},{16,24},{1... | collective-permute-start | bytes 3145736 | tf_op jit(solution)/shard_map/ring4/ppermute | solution.py:33
  53.2 2.1 %collective-permute-start.15 = (bf16[2,256,512]{2,1,0:T(8,128)(2,1)S(1)}, bf16[2,256,512]{2,1,0:T(8,128)(2,1)S(1)}, u32[]{:S(2)}, u32[]{:S(2)}) collective-permute-start(bf16[2,256,512]{2,1,0:T(8,128)(2,1)S(1)} %collective-permute-done.refs_6_), channel_id=1, source_target_pairs={{0,3},{1,0},{2,1},{3,2},{4,7},{5,4},{6,5},{7,6},{16,19},{17,16},{1... | collective-permute-start | bytes 1572872 | tf_op jit(solution)/shard_map/along-1_1/ppermute | solution.py:37
  55.3 6.9 %shard_map.50 = (bf16[192,2,2048]{2,1,0:T(2,128)(2,1)}, bf16[192,2,2048]{2,1,0:T(2,128)(2,1)}, f32[768,512]{1,0:T(8,128)S(1)}, f32[768,512]{1,0:T(8,128)S(1)}) custom-call(bf16[192,4096]{1,0:T(8,128)(2,1)S(1)} %bitcast.4, bf16[192,4096]{1,0:T(8,128)(2,1)S(1)} %bitcast.9, bf16[2,256,512]{2,1,0:T(8,128)(2,1)S(1)} %collective-permute-done.3.refs_0_, ...), custom_call_target="tpu_custom_call" | custom-call | flops 5637144576 | bytes 14680064 | tf_op jit(solution)/shard_map/pallas_call | solution.py:118
  62.2 0.1 collective-permute-start.12
  62.2 4.6 %collective-permute-done.10.refs_0_ = bf16[4,256,512]{2,1,0:T(8,128)(2,1)S(1)} collective-permute-done((bf16[4,256,512]{2,1,0:T(8,128)(2,1)S(1)}, bf16[4,256,512]{2,1,0:T(8,128)(2,1)S(1)}, u32[]{:S(2)}, u32[]{:S(2)}) %collective-permute-start.10) | collective-permute-done | bytes 1048608 | tf_op jit(solution)/shard_map/ring4/ppermute | solution.py:33
  66.8 0.1 fusion
  66.9 0.0 collective-permute-done.15.refs_2_
  66.9 0.2 pad_maximum_fusion.3
  67.1 0.1 collective-permute-start.17
  67.2 0.9 %collective-permute-start.16 = (bf16[2,256,512]{2,1,0:T(8,128)(2,1)S(1)}, bf16[2,256,512]{2,1,0:T(8,128)(2,1)S(1)}, u32[]{:S(2)}, u32[]{:S(2)}) collective-permute-start(bf16[2,256,512]{2,1,0:T(8,128)(2,1)S(1)} %collective-permute-done.9.refs_2_), channel_id=1, source_target_pairs={{0,8},{1,9},{2,10},{3,11},{4,20},{5,21},{6,22},{7,23},{16,0},{17,1... | collective-permute-start | bytes 1572872 | tf_op jit(solution)/shard_map/back5/ppermute | solution.py:33
  68.1 1.2 %collective-permute-start.20 = (bf16[2,256,512]{2,1,0:T(8,128)(2,1)S(1)}, bf16[2,256,512]{2,1,0:T(8,128)(2,1)S(1)}, u32[]{:S(2)}, u32[]{:S(2)}) collective-permute-start(bf16[2,256,512]{2,1,0:T(8,128)(2,1)S(1)} %get-tuple-element.54), channel_id=1, source_target_pairs={{0,16},{1,17},{2,18},{3,19},{4,12},{5,13},{6,14},{7,15},{16,24},{1... | collective-permute-start | bytes 1572872 | tf_op jit(solution)/shard_map/ring5/ppermute | solution.py:33
  69.3 3.8 %collective-permute-start.13 = (bf16[2,256,512]{2,1,0:T(8,128)(2,1)S(1)}, bf16[2,256,512]{2,1,0:T(8,128)(2,1)S(1)}, u32[]{:S(2)}, u32[]{:S(2)}) collective-permute-start(bf16[2,256,512]{2,1,0:T(8,128)(2,1)S(1)} %get-tuple-element.50), channel_id=1, source_target_pairs={{0,3},{1,0},{2,1},{3,2},{4,7},{5,4},{6,5},{7,6},{16,19},{17,16},{1... | collective-permute-start | bytes 1572872 | tf_op jit(solution)/shard_map/along-1_2/ppermute | solution.py:37
  73.1 2.6 %shard_map.51 = (f32[768,512]{1,0:T(8,128)S(1)}, f32[768,512]{1,0:T(8,128)S(1)}, f32[768,512]{1,0:T(8,128)S(1)}) custom-call(bf16[192,4096]{1,0:T(8,128)(2,1)S(1)} %bitcast.5, bf16[192,4096]{1,0:T(8,128)(2,1)S(1)} %bitcast.10, bf16[4,256,512]{2,1,0:T(8,128)(2,1)S(1)} %collective-permute-done.7.refs_0_, ...), custom_call_target="tpu_custom_call" | custom-call | flops 2415919104 | bytes 6291456 | tf_op jit(solution)/shard_map/pallas_call | solution.py:118
  75.7 3.7 %shard_map.52 = (bf16[192,2,2048]{2,1,0:T(2,128)(2,1)}, bf16[192,2,2048]{2,1,0:T(2,128)(2,1)}, f32[768,512]{1,0:T(8,128)S(1)}, f32[768,512]{1,0:T(8,128)S(1)}) custom-call(bf16[192,4096]{1,0:T(8,128)(2,1)S(1)} %bitcast.6, bf16[192,4096]{1,0:T(8,128)(2,1)S(1)} %bitcast.11, ...), custom_call_target="tpu_custom_call", output_to_operand_aliasing={{0}: (8, {}), {1}: (9, {})} | custom-call | flops 2415919104 | bytes 6291456 | tf_op jit(solution)/shard_map/pallas_call | solution.py:118
  79.4 0.1 collective-permute-start.18
  79.5 2.3 %collective-permute-done.16.refs_0_ = bf16[2,256,512]{2,1,0:T(8,128)(2,1)S(1)} collective-permute-done((bf16[2,256,512]{2,1,0:T(8,128)(2,1)S(1)}, bf16[2,256,512]{2,1,0:T(8,128)(2,1)S(1)}, u32[]{:S(2)}, u32[]{:S(2)}) %collective-permute-start.16) | collective-permute-done | bytes 524320 | tf_op jit(solution)/shard_map/back5/ppermute | solution.py:33
  81.8 0.5 collective-permute-start.21
  82.3 2.1 %collective-permute-done.13.refs_0_ = bf16[2,256,512]{2,1,0:T(8,128)(2,1)S(1)} collective-permute-done((bf16[2,256,512]{2,1,0:T(8,128)(2,1)S(1)}, bf16[2,256,512]{2,1,0:T(8,128)(2,1)S(1)}, u32[]{:S(2)}, u32[]{:S(2)}) %collective-permute-start.13) | collective-permute-done | bytes 524320 | tf_op jit(solution)/shard_map/along-1_2/ppermute | solution.py:37
  84.3 0.1 collective-permute-done.21.refs_3_
  84.4 2.8 %shard_map.53 = (bf16[192,2,2048]{2,1,0:T(2,128)(2,1)}, bf16[192,2,2048]{2,1,0:T(2,128)(2,1)}, f32[768,512]{1,0:T(8,128)S(1)}) custom-call(bf16[192,4096]{1,0:T(8,128)(2,1)S(1)} %bitcast.7, bf16[192,4096]{1,0:T(8,128)(2,1)S(1)} %bitcast.12, bf16[2,256,512]{2,1,0:T(8,128)(2,1)S(1)} %collective-permute-done.16.refs_0_, ...), custom_call_target="tpu_custom_call", output_to_operand_aliasing={{0}: (8, {}), {1}: (9, {})} | custom-call | flops 1610612736 | bytes 4194304 | tf_op jit(solution)/shard_map/pallas_call | solution.py:118
  87.3 2.0 %shard_map.54 = (bf16[192,2,2048]{2,1,0:T(2,128)(2,1)}, bf16[192,2,2048]{2,1,0:T(2,128)(2,1)}) custom-call(bf16[192,4096]{1,0:T(8,128)(2,1)S(1)} %bitcast.8, bf16[192,4096]{1,0:T(8,128)(2,1)S(1)} %bitcast.13, bf16[2,256,512]{2,1,0:T(8,128)(2,1)S(1)} %collective-permute-done.13.refs_0_, ...), custom_call_target="tpu_custom_call", output_to_operand_aliasing={{0}: (5, {}), {1}: (6, {})} | custom-call | flops 805306368 | bytes 2097152 | tf_op jit(solution)/shard_map/pallas_call | solution.py:118
  (18 shorter events, 0.0 us)
Async XLA Ops:
  0.6 17.2 %collective-permute-start.3 = (bf16[2,256,512]{2,1,0:T(8,128)(2,1)}, bf16[2,256,512]{2,1,0:T(8,128)(2,1)S(1)}, u32[]{:S(2)}, u32[]{:S(2)}) collective-permute-start(bf16[2,256,512]{2,1,0:T(8,128)(2,1)} %refs_5_.1), channel_id=1, source_target_pairs={{0,1},{1,2},{2,3},{3,0},{4,5},{5,6},{6,7},{7,4},{16,17},{17,18},{1... | collective-permute-start | bytes 1572872 | tf_op jit(solution)/shard_map/along1_0/ppermute | solution.py:37
  3.7 14.8 %collective-permute-start = (bf16[2,256,512]{2,1,0:T(8,128)(2,1)}, bf16[2,256,512]{2,1,0:T(8,128)(2,1)S(1)}, u32[]{:S(2)}, u32[]{:S(2)}) collective-permute-start(bf16[2,256,512]{2,1,0:T(8,128)(2,1)} %refs_5_.1), channel_id=1, source_target_pairs={{0,16},{1,17},{2,18},{3,19},{4,12},{5,13},{6,14},{7,15},{16,24},{1... | collective-permute-start | bytes 1572872 | tf_op jit(solution)/shard_map/ring1/ppermute | solution.py:33
  5.2 13.3 %collective-permute-start.1 = (bf16[2,256,512]{2,1,0:T(8,128)(2,1)}, bf16[2,256,512]{2,1,0:T(8,128)(2,1)S(1)}, u32[]{:S(2)}, u32[]{:S(2)}) collective-permute-start(bf16[2,256,512]{2,1,0:T(8,128)(2,1)} %refs_5_.1), channel_id=1, source_target_pairs={{0,8},{1,9},{2,10},{3,11},{4,20},{5,21},{6,22},{7,23},{16,0},{17,1... | collective-permute-start | bytes 1572872 | tf_op jit(solution)/shard_map/back1/ppermute | solution.py:33
  5.7 12.8 %collective-permute-start.2 = (bf16[2,256,512]{2,1,0:T(8,128)(2,1)}, bf16[2,256,512]{2,1,0:T(8,128)(2,1)S(1)}, u32[]{:S(2)}, u32[]{:S(2)}) collective-permute-start(bf16[2,256,512]{2,1,0:T(8,128)(2,1)} %refs_5_.1), channel_id=1, source_target_pairs={{0,4},{1,5},{2,6},{3,7},{4,0},{5,1},{6,2},{7,3},{16,20},{17,21},{1... | collective-permute-start | bytes 1572872 | tf_op jit(solution)/shard_map/core1/ppermute | solution.py:41
  5.7 2.2 %copy-start.1 = (bf16[192,2,2048]{2,1,0:T(2,128)(2,1)S(1)}, bf16[192,2,2048]{2,1,0:T(2,128)(2,1)}, u32[]{:S(2)}) copy-start(bf16[192,2,2048]{2,1,0:T(2,128)(2,1)} %param.4) | copy-start | bytes 4718596
  18.7 17.6 %collective-permute-start.5 = (bf16[6,256,512]{2,1,0:T(8,128)(2,1)S(1)}, bf16[6,256,512]{2,1,0:T(8,128)(2,1)S(1)}, u32[]{:S(2)}, u32[]{:S(2)}) collective-permute-start(bf16[6,256,512]{2,1,0:T(8,128)(2,1)S(1)} %pad_maximum_fusion), channel_id=1, source_target_pairs={{0,4},{1,5},{2,6},{3,7},{4,0},{5,1},{6,2},{7,3},{16,20},{17,21},{1... | collective-permute-start | bytes 4718600 | tf_op jit(solution)/shard_map/core2/ppermute | solution.py:41
  18.9 14.9 %collective-permute-start.4 = (bf16[4,256,512]{2,1,0:T(8,128)(2,1)S(1)}, bf16[4,256,512]{2,1,0:T(8,128)(2,1)S(1)}, u32[]{:S(2)}, u32[]{:S(2)}) collective-permute-start(bf16[4,256,512]{2,1,0:T(8,128)(2,1)S(1)} %pad_maximum_fusion.4), channel_id=1, source_target_pairs={{0,16},{1,17},{2,18},{3,19},{4,12},{5,13},{6,14},{7,15},{16,24},{1... | collective-permute-start | bytes 3145736 | tf_op jit(solution)/shard_map/ring2/ppermute | solution.py:33
  19.8 16.5 %collective-permute-start.6 = (bf16[2,256,512]{2,1,0:T(8,128)(2,1)S(1)}, bf16[2,256,512]{2,1,0:T(8,128)(2,1)S(1)}, u32[]{:S(2)}, u32[]{:S(2)}) collective-permute-start(bf16[2,256,512]{2,1,0:T(8,128)(2,1)S(1)} %collective-permute-done.3.refs_0_), channel_id=1, source_target_pairs={{0,1},{1,2},{2,3},{3,0},{4,5},{5,6},{6,7},{7,4},{16,17},{17,18},{1... | collective-permute-start | bytes 1572872 | tf_op jit(solution)/shard_map/along2_0/ppermute | solution.py:37
  36.5 1.0 %copy-start = (bf16[2,256,512]{2,1,0:T(8,128)(2,1)S(1)}, bf16[2,256,512]{2,1,0:T(8,128)(2,1)}, u32[]{:S(2)}) copy-start(bf16[2,256,512]{2,1,0:T(8,128)(2,1)} %refs_5_.1) | copy-start | bytes 1572868
  36.5 15.1 %collective-permute-start.8 = (bf16[6,256,512]{2,1,0:T(8,128)(2,1)S(1)}, bf16[6,256,512]{2,1,0:T(8,128)(2,1)S(1)}, u32[]{:S(2)}, u32[]{:S(2)}) collective-permute-start(bf16[6,256,512]{2,1,0:T(8,128)(2,1)S(1)} %pad_maximum_fusion.1), channel_id=1, source_target_pairs={{0,4},{1,5},{2,6},{3,7},{4,0},{5,1},{6,2},{7,3},{16,20},{17,21},{1... | collective-permute-start | bytes 4718600 | tf_op jit(solution)/shard_map/core3/ppermute | solution.py:41
  36.7 14.9 %collective-permute-start.7 = (bf16[4,256,512]{2,1,0:T(8,128)(2,1)S(1)}, bf16[4,256,512]{2,1,0:T(8,128)(2,1)S(1)}, u32[]{:S(2)}, u32[]{:S(2)}) collective-permute-start(bf16[4,256,512]{2,1,0:T(8,128)(2,1)S(1)} %pad_maximum_fusion.5), channel_id=1, source_target_pairs={{0,16},{1,17},{2,18},{3,19},{4,12},{5,13},{6,14},{7,15},{16,24},{1... | collective-permute-start | bytes 3145736 | tf_op jit(solution)/shard_map/ring3/ppermute | solution.py:33
  37.5 14.1 %collective-permute-start.9 = (bf16[2,256,512]{2,1,0:T(8,128)(2,1)S(1)}, bf16[2,256,512]{2,1,0:T(8,128)(2,1)S(1)}, u32[]{:S(2)}, u32[]{:S(2)}) collective-permute-start(bf16[2,256,512]{2,1,0:T(8,128)(2,1)S(1)} %copy-done), channel_id=1, source_target_pairs={{0,3},{1,0},{2,1},{3,2},{4,7},{5,4},{6,5},{7,6},{16,19},{17,16},{1... | collective-permute-start | bytes 1572872 | tf_op jit(solution)/shard_map/along-1_0/ppermute | solution.py:37
  51.8 15.1 %collective-permute-start.11 = (bf16[6,256,512]{2,1,0:T(8,128)(2,1)S(1)}, bf16[6,256,512]{2,1,0:T(8,128)(2,1)S(1)}, u32[]{:S(2)}, u32[]{:S(2)}) collective-permute-start(bf16[6,256,512]{2,1,0:T(8,128)(2,1)S(1)} %pad_maximum_fusion.2), channel_id=1, source_target_pairs={{0,4},{1,5},{2,6},{3,7},{4,0},{5,1},{6,2},{7,3},{16,20},{17,21},{1... | collective-permute-start | bytes 4718600 | tf_op jit(solution)/shard_map/core4/ppermute | solution.py:41
  52.0 14.9 %collective-permute-start.10 = (bf16[4,256,512]{2,1,0:T(8,128)(2,1)S(1)}, bf16[4,256,512]{2,1,0:T(8,128)(2,1)S(1)}, u32[]{:S(2)}, u32[]{:S(2)}) collective-permute-start(bf16[4,256,512]{2,1,0:T(8,128)(2,1)S(1)} %pad_maximum_fusion.6), channel_id=1, source_target_pairs={{0,16},{1,17},{2,18},{3,19},{4,12},{5,13},{6,14},{7,15},{16,24},{1... | collective-permute-start | bytes 3145736 | tf_op jit(solution)/shard_map/ring4/ppermute | solution.py:33
  53.2 13.7 %collective-permute-start.15 = (bf16[2,256,512]{2,1,0:T(8,128)(2,1)S(1)}, bf16[2,256,512]{2,1,0:T(8,128)(2,1)S(1)}, u32[]{:S(2)}, u32[]{:S(2)}) collective-permute-start(bf16[2,256,512]{2,1,0:T(8,128)(2,1)S(1)} %collective-permute-done.refs_6_), channel_id=1, source_target_pairs={{0,3},{1,0},{2,1},{3,2},{4,7},{5,4},{6,5},{7,6},{16,19},{17,16},{1... | collective-permute-start | bytes 1572872 | tf_op jit(solution)/shard_map/along-1_1/ppermute | solution.py:37
  62.2 4.7 %collective-permute-start.12 = (bf16[1,16,128]{2,1,0:T(8,128)(2,1)S(1)}, bf16[1,16,128]{2,1,0:T(8,128)(2,1)S(1)}, u32[]{:S(2)}, u32[]{:S(2)}) collective-permute-start(bf16[1,16,128]{2,1,0:T(8,128)(2,1)S(1)} %get-tuple-element.49), channel_id=1, source_target_pairs={{0,4},{1,5},{2,6},{3,7},{4,0},{5,1},{6,2},{7,3},{16,20},{17,21},{1... | collective-permute-start | bytes 12296 | tf_op jit(solution)/shard_map/token/ppermute | solution.py:41
  67.1 8.6 %collective-permute-start.17 = (bf16[6,256,512]{2,1,0:T(8,128)(2,1)S(1)}, bf16[6,256,512]{2,1,0:T(8,128)(2,1)S(1)}, u32[]{:S(2)}, u32[]{:S(2)}) collective-permute-start(bf16[6,256,512]{2,1,0:T(8,128)(2,1)S(1)} %pad_maximum_fusion.3), channel_id=1, source_target_pairs={{0,4},{1,5},{2,6},{3,7},{4,0},{5,1},{6,2},{7,3},{16,20},{17,21},{1... | collective-permute-start | bytes 4718600 | tf_op jit(solution)/shard_map/core5/ppermute | solution.py:41
  67.2 14.6 %collective-permute-start.16 = (bf16[2,256,512]{2,1,0:T(8,128)(2,1)S(1)}, bf16[2,256,512]{2,1,0:T(8,128)(2,1)S(1)}, u32[]{:S(2)}, u32[]{:S(2)}) collective-permute-start(bf16[2,256,512]{2,1,0:T(8,128)(2,1)S(1)} %collective-permute-done.9.refs_2_), channel_id=1, source_target_pairs={{0,8},{1,9},{2,10},{3,11},{4,20},{5,21},{6,22},{7,23},{16,0},{17,1... | collective-permute-start | bytes 1572872 | tf_op jit(solution)/shard_map/back5/ppermute | solution.py:33
  68.1 13.7 %collective-permute-start.20 = (bf16[2,256,512]{2,1,0:T(8,128)(2,1)S(1)}, bf16[2,256,512]{2,1,0:T(8,128)(2,1)S(1)}, u32[]{:S(2)}, u32[]{:S(2)}) collective-permute-start(bf16[2,256,512]{2,1,0:T(8,128)(2,1)S(1)} %get-tuple-element.54), channel_id=1, source_target_pairs={{0,16},{1,17},{2,18},{3,19},{4,12},{5,13},{6,14},{7,15},{16,24},{1... | collective-permute-start | bytes 1572872 | tf_op jit(solution)/shard_map/ring5/ppermute | solution.py:33
  69.3 15.1 %collective-permute-start.13 = (bf16[2,256,512]{2,1,0:T(8,128)(2,1)S(1)}, bf16[2,256,512]{2,1,0:T(8,128)(2,1)S(1)}, u32[]{:S(2)}, u32[]{:S(2)}) collective-permute-start(bf16[2,256,512]{2,1,0:T(8,128)(2,1)S(1)} %get-tuple-element.50), channel_id=1, source_target_pairs={{0,3},{1,0},{2,1},{3,2},{4,7},{5,4},{6,5},{7,6},{16,19},{17,16},{1... | collective-permute-start | bytes 1572872 | tf_op jit(solution)/shard_map/along-1_2/ppermute | solution.py:37
  79.4 2.3 %collective-permute-start.18 = (bf16[1,16,128]{2,1,0:T(8,128)(2,1)S(1)}, bf16[1,16,128]{2,1,0:T(8,128)(2,1)S(1)}, u32[]{:S(2)}, u32[]{:S(2)}) collective-permute-start(bf16[1,16,128]{2,1,0:T(8,128)(2,1)S(1)} %get-tuple-element.63), channel_id=1, source_target_pairs={{0,4},{1,5},{2,6},{3,7},{4,0},{5,1},{6,2},{7,3},{16,20},{17,21},{1... | collective-permute-start | bytes 12296 | tf_op jit(solution)/shard_map/token/ppermute | solution.py:41
  81.8 2.6 %collective-permute-start.19 = (bf16[2,256,512]{2,1,0:T(8,128)(2,1)S(1)}, bf16[2,256,512]{2,1,0:T(8,128)(2,1)S(1)}, u32[]{:S(2)}, u32[]{:S(2)}) collective-permute-start(bf16[2,256,512]{2,1,0:T(8,128)(2,1)S(1)} %collective-permute-done.16.refs_0_), channel_id=1, source_target_pairs={{0,4},{1,5},{2,6},{3,7},{4,0},{5,1},{6,2},{7,3},{16,20},{17,21},{1... | collective-permute-start | bytes 1572872 | tf_op jit(solution)/shard_map/core_last-1_-1/ppermute | solution.py:41
  81.8 2.7 %collective-permute-start.21 = (bf16[2,256,512]{2,1,0:T(8,128)(2,1)S(1)}, bf16[2,256,512]{2,1,0:T(8,128)(2,1)S(1)}, u32[]{:S(2)}, u32[]{:S(2)}) collective-permute-start(bf16[2,256,512]{2,1,0:T(8,128)(2,1)S(1)} %collective-permute-done.20.refs_2_), channel_id=1, source_target_pairs={{0,4},{1,5},{2,6},{3,7},{4,0},{5,1},{6,2},{7,3},{16,20},{17,21},{1... | collective-permute-start | bytes 1572872 | tf_op jit(solution)/shard_map/core_last2_3/ppermute | solution.py:41
  84.3 2.9 %collective-permute-start.14 = (bf16[2,256,512]{2,1,0:T(8,128)(2,1)S(1)}, bf16[2,256,512]{2,1,0:T(8,128)(2,1)S(1)}, u32[]{:S(2)}, u32[]{:S(2)}) collective-permute-start(bf16[2,256,512]{2,1,0:T(8,128)(2,1)S(1)} %collective-permute-done.13.refs_0_), channel_id=1, source_target_pairs={{0,4},{1,5},{2,6},{3,7},{4,0},{5,1},{6,2},{7,3},{16,20},{17,21},{1... | collective-permute-start | bytes 1572872 | tf_op jit(solution)/shard_map/core_end/ppermute | solution.py:41

commit v4 on v3

--- a/solution.py
+++ b/solution.py
@@ -128,14 +128,96 @@
     return (tuple(result[:2]), result[2:]) if finishing else (outs, result)
 
 
-def shards(rows, cols, orbitals, applied, ritz):
-    moves = Moves(rows, cols)
-    chips = rows // 2
-    ahead, back = chips // 2, (chips - 1) // 2
-    hops = [*range(ahead + 1), *(-h for h in range(1, back + 1))]
-    lefts = [x.reshape(x.shape[0], -1) for x in (orbitals, applied)]
-    run = functools.partial(run_parts, rows=rows, cols=cols, lefts=lefts, like=orbitals)
-
+def few_rounds(moves, run, lefts, ritz):
+    distances = [0, 1, 2, -1]
+    mine, theirs = {(0, 0): (ritz, 0)}, {}
+    full = {0: [0, 1, 2, -1], 1: [0, 1, 2, -1], 2: [0, 1, 2, -1], -1: [0, 1, 2, -1]}
+
+    def bundle(keys, gate):
+        values = [lax.slice_in_dim(a, 2 * n, 2 * n + 2) if a.shape[0] > 2 else a for a, n in (mine[key] for key in keys)]
+        values = [after(v, *gate) for v in values]
+        return jnp.concatenate(values, 0) if len(values) > 1 else values[0]
+
+    def move(how, step, pairs, *gate):
+        with jax.named_scope(how + "_".join(f"{d}:{h}" for _, (d, h) in pairs)):
+            value = getattr(moves, how)(bundle([source for source, _ in pairs], gate), step)
+        mine.update({key: (value, number) for number, (_, key) in enumerate(pairs)})
+        return value
+
+    def swap(keys, *gate):
+        with jax.named_scope("core" + "_".join(f"{d}:{h}" for d, h in keys)):
+            value = moves.other(bundle(keys, gate))
+        theirs.update({key: (value, number) for number, key in enumerate(keys)})
+        return value
+
+    def part(layer, hops, begun=None, finish=True):
+        return Part(layer, [(h, whose is mine, *whose[layer, h]) for whose in (mine, theirs) for h in hops], begun, finish)
+
+    state = {"outs": None, "tokens": 0}
+    sums, used = {}, {d: [] for d in distances}
+
+    def products(keys):
+        parts = []
+        for d in distances:
+            hops = [h for h in full[d] if (d, h) in keys and h not in used[d]]
+            if hops:
+                used[d] += hops
+                parts.append(part(d, hops, sums.pop(d, None), len(used[d]) == len(full[d])))
+        parts.sort(key=lambda p: p.finish)
+        state["outs"], kept = run(parts, outs=state["outs"])
+        unfinished = [p for p in parts if not p.finish]
+        sums.update({p.stage: s for p, s in zip(unfinished, kept, strict=True)})
+        return kept[0] if unfinished else state["outs"][0]
+
+    def token(value):
+        at = 16 * state["tokens"]
+        state["tokens"] += 1
+        with jax.named_scope("token"):
+            return moves.other(after(lax.slice(ritz, (0, at, 0), (1, at + 16, 128)), value))
+
+    cut = ritz.shape[1] // 2
+
+    def down(value, name, *gate):
+        with jax.named_scope(name):
+            return moves.along(after(value, *gate), -1)
+
+    z1 = move("along", 1, [((0, 0), (1, 0))])
+    p1 = move("ring", 1, [((0, 0), (0, 1))])
+    m1 = move("ring", -1, [((0, 0), (0, -1))])
+    e1 = swap([(0, 0)])
+    gate = (p1, m1, z1, e1, *lefts)
+    z2 = move("along", 1, [((1, 0), (2, 0))], *gate)
+    p2 = move("ring", 1, [((0, 1), (0, 2)), ((1, 0), (1, 1))], *gate)
+    m2 = move("ring", -1, [((1, 0), (1, -1))], *gate)
+    upper = down(ritz[:, :cut], "along_upper", *gate)
+    e2 = swap([(0, 1), (0, -1), (1, 0)], *gate)
+    gate = (p2, m2, e2, z2, upper)
+    p3 = move("ring", 1, [((1, 1), (1, 2)), ((2, 0), (2, 1))], *gate)
+    m3 = move("ring", -1, [((2, 0), (2, -1))], *gate)
+    lower = down(jnp.concatenate([ritz[:, cut:], mine[0, 1][0]], 1), "along_lower", *gate)
+    e3 = swap([(0, 2), (1, 1), (1, -1), (2, 0)], *gate)
+    products([(0, 0), (0, 1), (0, -1), (1, 0)])
+    t = token(products([(0, 2), (1, 1), (1, -1), (2, 0)]))
+    mine[-1, 0] = jnp.concatenate([upper, lower[:, : ritz.shape[1] - cut]], 1), 0
+    mine[-1, 1] = lower[:, ritz.shape[1] - cut :], 0
+    gate = (p3, m3, e3, t)
+    z5 = move("along", -1, [((0, 2), (-1, 2))], *gate)
+    gate = (*gate, lower)
+    p4 = move("ring", 1, [((2, 1), (2, 2))], *gate)
+    m4 = move("ring", -1, [((-1, 0), (-1, -1))], *gate)
+    e4 = swap([(1, 2), (2, 1), (2, -1)], *gate)
+    e4b = swap([(-1, 0), (-1, 1)], *gate)
+    t = token(products([(1, 2), (2, 1), (2, -1), (-1, 0), (-1, 1)]))
+    swap([(2, 2)], t, e4)
+    swap([(-1, -1)], t, e4)
+    products([(2, 2), (-1, -1)])
+    swap([(-1, 2)])
+    products([(-1, 2)])
+    return state["outs"]
+
+
+def any_rounds(moves, run, lefts, ritz):
+    chips, cols = moves.chips, moves.cols
     final = cols + chips - 3
     distances = [*range(cols - 1), -1]
     mine, theirs = {(0, 0): (ritz, 0)}, {}
@@ -213,6 +295,13 @@
     return state["outs"]
 
 
+def shards(rows, cols, orbitals, applied, ritz):
+    moves = Moves(rows, cols)
+    lefts = [x.reshape(x.shape[0], -1) for x in (orbitals, applied)]
+    run = functools.partial(run_parts, rows=rows, cols=cols, lefts=lefts, like=orbitals)
+    return (few_rounds if (moves.chips, cols) == (4, 4) else any_rounds)(moves, run, lefts, ritz)
+
+
 def solution(mesh):
     rows, cols = mesh.shape["row"], mesh.shape["col"]
     whole = P(AXES, None, None)

time: 89.6 us -> 87.3 us (0.974)
  waiting for transfers between devices: 47.9 us -> 42.1 us
  starting transfers between devices: 18.2 us -> 21.9 us
    ppermute x7 -> x8, waiting for transfers between devices: 34 us -> 26.9 us  [ring(): return lax.ppermute(value, AXES, pairs)]
    ppermute x7 -> x8, starting transfers between devices: 6.82 us -> 8.26 us  [ring(): return lax.ppermute(value, AXES, pairs)]
    ppermute x5, starting transfers between devices: 10.4 us -> 11.6 us  [along(): return lax.ppermute(value, AXES, pairs)]
    ppermute x10, starting transfers between devices: 0.94 us -> 2.05 us  [other(): return lax.ppermute(value, AXES, pairs)]
    ppermute x10, waiting for transfers between devices: 0.1 us -> 1.03 us  [other(): return lax.ppermute(value, AXES, pairs)]
  transfers between devices with their start and end apart: 22 -> 23, of which waited for: 9 -> 9; matrix products, arithmetic and copies ran while one was open for 4% -> 4% of each run, Pallas kernels for 18% -> 18%
where the time goes in v4:
time: 87.3 us; the launch traced here: 87.1 us
  waiting for transfers between devices  42.1 us (48%)
  starting transfers between devices  21.9 us (25%)
  Pallas kernels  18.1 us (21%)
  local copies, waits for them, and re-layouts  3.06 us (4%)
  between operations  1 us (1%)
  other arithmetic  0.97 us (1%)
    ppermute x8, waiting for transfers between devices, ring(): return lax.ppermute(value, AXES, pairs)  26.9 us
    pallas_call x5, Pallas kernels, run_parts(): pl.pallas_call(functools.partial(parts_kernel, plan, rows, cols, len(arra...  18.1 us
    ppermute x5, waiting for transfers between devices, along(): return lax.ppermute(value, AXES, pairs)  14.1 us
    ppermute x5, starting transfers between devices, along(): return lax.ppermute(value, AXES, pairs)  11.6 us
    ppermute x8, starting transfers between devices, ring(): return lax.ppermute(value, AXES, pairs)  8.26 us
    unnamed x6, local copies, waits for them, and re-layouts  2.83 us
    ppermute x10, starting transfers between devices, other(): return lax.ppermute(value, AXES, pairs)  2.05 us
  transfers between devices with their start and end apart: 23, of which 9 were waited for; matrix products, arithmetic and copies ran while one was open for 4% of the time, Pallas kernels for 18%

profile of v4, /device:TPU:0, one launch (start us, length us, event | category | flops | bytes accessed | tf_op | source)
XLA Modules:
  0.0 87.1 jit_solution(6694491097913557279)
XLA Ops:
  0.6 0.5 collective-permute-start.3
  1.1 2.6 %collective-permute-start.2 = (bf16[2,256,512]{2,1,0:T(8,128)(2,1)}, bf16[2,256,512]{2,1,0:T(8,128)(2,1)S(1)}, u32[]{:S(2)}, u32[]{:S(2)}) collective-permute-start(bf16[2,256,512]{2,1,0:T(8,128)(2,1)} %refs_0_.1), channel_id=1, source_target_pairs={{0,1},{1,2},{2,3},{3,0},{4,5},{5,6},{6,7},{7,4},{16,17},{17,18},{1... | collective-permute-start | bytes 1572872 | tf_op jit(solution)/shard_map/along1:0/ppermute | solution.py:37
  3.8 1.5 %collective-permute-start.1 = (bf16[2,256,512]{2,1,0:T(8,128)(2,1)}, bf16[2,256,512]{2,1,0:T(8,128)(2,1)S(1)}, u32[]{:S(2)}, u32[]{:S(2)}) collective-permute-start(bf16[2,256,512]{2,1,0:T(8,128)(2,1)} %refs_0_.1), channel_id=1, source_target_pairs={{0,8},{1,9},{2,10},{3,11},{4,20},{5,21},{6,22},{7,23},{16,0},{17,1... | collective-permute-start | bytes 1572872 | tf_op jit(solution)/shard_map/ring0:-1/ppermute | solution.py:33
  5.3 0.5 collective-permute-start
  5.8 2.2 %copy.11 = bf16[24,8,2,2048]{3,1,2,0:T(8,128)(2,1)S(1)} copy(bf16[24,8,2,2048]{3,2,1,0:T(2,128)(2,1)} %bitcast.14) | data formatting | bytes 3145728
  8.0 0.6 copy.12
  8.7 9.9 %collective-permute-done.2.refs_5_ = bf16[2,256,512]{2,1,0:T(8,128)(2,1)S(1)} collective-permute-done((bf16[2,256,512]{2,1,0:T(8,128)(2,1)}, bf16[2,256,512]{2,1,0:T(8,128)(2,1)S(1)}, u32[]{:S(2)}, u32[]{:S(2)}) %collective-permute-start.2) | collective-permute-done | bytes 524320 | tf_op jit(solution)/shard_map/along1:0/ppermute | solution.py:37
  18.6 0.2 pad_maximum_fusion.1
  18.7 0.0 copy-start
  18.7 0.2 collective-permute-start.6
  18.9 0.1 pad_maximum_fusion.3
  19.0 1.6 %collective-permute-start.4 = (bf16[4,256,512]{2,1,0:T(8,128)(2,1)S(1)}, bf16[4,256,512]{2,1,0:T(8,128)(2,1)S(1)}, u32[]{:S(2)}, u32[]{:S(2)}) collective-permute-start(bf16[4,256,512]{2,1,0:T(8,128)(2,1)S(1)} %pad_maximum_fusion.3), channel_id=1, source_target_pairs={{0,16},{1,17},{2,18},{3,19},{4,12},{5,13},{6,14},{7,15},{16,24},{1... | collective-permute-start | bytes 3145736 | tf_op jit(solution)/shard_map/ring0:2_1:1/ppermute | solution.py:33
  20.6 1.5 %collective-permute-start.7 = (bf16[2,256,512]{2,1,0:T(8,128)(2,1)S(1)}, bf16[2,256,512]{2,1,0:T(8,128)(2,1)S(1)}, u32[]{:S(2)}, u32[]{:S(2)}) collective-permute-start(bf16[2,256,512]{2,1,0:T(8,128)(2,1)S(1)} %collective-permute-done.2.refs_5_), channel_id=1, source_target_pairs={{0,1},{1,2},{2,3},{3,0},{4,5},{5,6},{6,7},{7,4},{16,17},{17,18},{1... | collective-permute-start | bytes 1572872 | tf_op jit(solution)/shard_map/along2:0/ppermute | solution.py:37
  22.1 0.5 collective-permute-start.5
  22.7 2.3 %collective-permute-start.8 = (bf16[2,128,512]{2,1,0:T(8,128)(2,1)S(1)}, bf16[2,128,512]{2,1,0:T(8,128)(2,1)S(1)}, u32[]{:S(2)}, u32[]{:S(2)}) collective-permute-start(bf16[2,128,512]{2,1,0:T(8,128)(2,1)S(1)} %get-tuple-element.37), channel_id=1, source_target_pairs={{0,3},{1,0},{2,1},{3,2},{4,7},{5,4},{6,5},{7,6},{16,19},{17,16},{1... | collective-permute-start | bytes 786440 | tf_op jit(solution)/shard_map/along_upper/ppermute | solution.py:37
  25.0 14.5 %collective-permute-done.4.refs_0_ = bf16[4,256,512]{2,1,0:T(8,128)(2,1)S(1)} collective-permute-done((bf16[4,256,512]{2,1,0:T(8,128)(2,1)S(1)}, bf16[4,256,512]{2,1,0:T(8,128)(2,1)S(1)}, u32[]{:S(2)}, u32[]{:S(2)}) %collective-permute-start.4) | collective-permute-done | bytes 1048608 | tf_op jit(solution)/shard_map/ring0:2_1:1/ppermute | solution.py:33
  39.5 0.1 fusion.1
  39.6 2.1 %collective-permute-done.8 = bf16[2,128,512]{2,1,0:T(8,128)(2,1)S(1)} collective-permute-done((bf16[2,128,512]{2,1,0:T(8,128)(2,1)S(1)}, bf16[2,128,512]{2,1,0:T(8,128)(2,1)S(1)}, u32[]{:S(2)}, u32[]{:S(2)}) %collective-permute-start.8) | collective-permute-done | bytes 262176 | tf_op jit(solution)/shard_map/along_upper/ppermute | solution.py:37
  41.7 0.3 pad_maximum_fusion
  41.9 0.1 collective-permute-start.11
  42.0 0.1 pad_maximum_fusion.4
  42.1 0.8 collective-permute-start.9
  43.0 0.1 pad_maximum_fusion.6
  43.0 1.3 %collective-permute-start.10 = (bf16[2,256,512]{2,1,0:T(8,128)(2,1)S(1)}, bf16[2,256,512]{2,1,0:T(8,128)(2,1)S(1)}, u32[]{:S(2)}, u32[]{:S(2)}) collective-permute-start(bf16[2,256,512]{2,1,0:T(8,128)(2,1)S(1)} %collective-permute-done.7.refs_3_), channel_id=1, source_target_pairs={{0,8},{1,9},{2,10},{3,11},{4,20},{5,21},{6,22},{7,23},{16,0},{17,1... | collective-permute-start | bytes 1572872 | tf_op jit(solution)/shard_map/ring2:-1/ppermute | solution.py:33
  44.3 1.7 %collective-permute-start.15 = (bf16[2,384,512]{2,1,0:T(8,128)(2,1)S(1)}, bf16[2,384,512]{2,1,0:T(8,128)(2,1)S(1)}, u32[]{:S(2)}, u32[]{:S(2)}) collective-permute-start(bf16[2,384,512]{2,1,0:T(8,128)(2,1)S(1)} %pad_maximum_fusion.6), channel_id=1, source_target_pairs={{0,3},{1,0},{2,1},{3,2},{4,7},{5,4},{6,5},{7,6},{16,19},{17,16},{1... | collective-permute-start | bytes 2359304 | tf_op jit(solution)/shard_map/along_lower/ppermute | solution.py:37
  46.0 3.4 %shard_map.50 = (f32[768,512]{1,0:T(8,128)S(1)}, f32[768,512]{1,0:T(8,128)S(1)}) custom-call(bf16[192,4096]{1,0:T(8,128)(2,1)S(1)} %bitcast.4, bf16[192,4096]{1,0:T(8,128)(2,1)S(1)} %bitcast.9, bf16[2,256,512]{2,1,0:T(8,128)(2,1)S(1)} %copy-done, bf16[2,256,512]{2,1,0:T(8,128)(2,1)S(1)} %collective-permute-done.refs_1_, ...), custom_call_target="tpu_custom_call" | custom-call | flops 3221225472 | bytes 8388608 | tf_op jit(solution)/shard_map/pallas_call | solution.py:118
  49.4 4.5 %shard_map.51 = (bf16[192,2,2048]{2,1,0:T(2,128)(2,1)}, bf16[192,2,2048]{2,1,0:T(2,128)(2,1)}, f32[768,512]{1,0:T(8,128)S(1)}, f32[768,512]{1,0:T(8,128)S(1)}) custom-call(bf16[192,4096]{1,0:T(8,128)(2,1)S(1)} %bitcast.5, bf16[192,4096]{1,0:T(8,128)(2,1)S(1)} %bitcast.10, bf16[4,256,512]{2,1,0:T(8,128)(2,1)S(1)} %collective-permute-done.4.refs_0_, ...), custom_call_target="tpu_custom_call" | custom-call | flops 3221225472 | bytes 8388608 | tf_op jit(solution)/shard_map/pallas_call | solution.py:118
  53.9 0.1 collective-permute-start.12
  54.0 8.6 %collective-permute-done.9.refs_0_ = bf16[4,256,512]{2,1,0:T(8,128)(2,1)S(1)} collective-permute-done((bf16[4,256,512]{2,1,0:T(8,128)(2,1)S(1)}, bf16[4,256,512]{2,1,0:T(8,128)(2,1)S(1)}, u32[]{:S(2)}, u32[]{:S(2)}) %collective-permute-start.9) | collective-permute-done | bytes 1048608 | tf_op jit(solution)/shard_map/ring1:2_2:1/ppermute | solution.py:33
  62.6 0.1 fusion
  62.7 1.0 %collective-permute-done.15 = bf16[2,384,512]{2,1,0:T(8,128)(2,1)S(1)} collective-permute-done((bf16[2,384,512]{2,1,0:T(8,128)(2,1)S(1)}, bf16[2,384,512]{2,1,0:T(8,128)(2,1)S(1)}, u32[]{:S(2)}, u32[]{:S(2)}) %collective-permute-start.15) | collective-permute-done | bytes 786464 | tf_op jit(solution)/shard_map/along_lower/ppermute | solution.py:37
  63.7 0.2 pad_maximum_fusion.2
  63.9 0.1 collective-permute-start.17
  64.1 0.1 pad_maximum_fusion.5
  64.2 0.6 collective-permute-start.18
  64.7 0.8 collective-permute-start.21
  65.5 1.2 %collective-permute-start.16 = (bf16[2,256,512]{2,1,0:T(8,128)(2,1)S(1)}, bf16[2,256,512]{2,1,0:T(8,128)(2,1)S(1)}, u32[]{:S(2)}, u32[]{:S(2)}) collective-permute-start(bf16[2,256,512]{2,1,0:T(8,128)(2,1)S(1)} %pad_maximum_fusion.7.refs_3_), channel_id=1, source_target_pairs={{0,8},{1,9},{2,10},{3,11},{4,20},{5,21},{6,22},{7,23},{16,0},{17,1... | collective-permute-start | bytes 1572872 | tf_op jit(solution)/shard_map/ring-1:-1/ppermute | solution.py:33
  66.8 3.4 %collective-permute-start.13 = (bf16[2,256,512]{2,1,0:T(8,128)(2,1)S(1)}, bf16[2,256,512]{2,1,0:T(8,128)(2,1)S(1)}, u32[]{:S(2)}, u32[]{:S(2)}) collective-permute-start(bf16[2,256,512]{2,1,0:T(8,128)(2,1)S(1)} %get-tuple-element.46), channel_id=1, source_target_pairs={{0,3},{1,0},{2,1},{3,2},{4,7},{5,4},{6,5},{7,6},{16,19},{17,16},{1... | collective-permute-start | bytes 1572872 | tf_op jit(solution)/shard_map/along-1:2/ppermute | solution.py:37
  70.2 5.3 %shard_map.52 = (bf16[192,2,2048]{2,1,0:T(2,128)(2,1)}, bf16[192,2,2048]{2,1,0:T(2,128)(2,1)}, f32[768,512]{1,0:T(8,128)S(1)}, f32[768,512]{1,0:T(8,128)S(1)}) custom-call(bf16[192,4096]{1,0:T(8,128)(2,1)S(1)} %bitcast.6, bf16[192,4096]{1,0:T(8,128)(2,1)S(1)} %bitcast.11, ...), custom_call_target="tpu_custom_call", output_to_operand_aliasing={{0}: (10, {}), {1}: (11, {})} | custom-call | flops 4026531840 | bytes 10485760 | tf_op jit(solution)/shard_map/pallas_call | solution.py:118
  75.5 0.1 collective-permute-start.19
  75.6 3.8 %collective-permute-done.21.refs_2_ = bf16[2,256,512]{2,1,0:T(8,128)(2,1)S(1)} collective-permute-done((bf16[2,256,512]{2,1,0:T(8,128)(2,1)S(1)}, bf16[2,256,512]{2,1,0:T(8,128)(2,1)S(1)}, u32[]{:S(2)}, u32[]{:S(2)}) %collective-permute-start.21) | collective-permute-done | bytes 524320 | tf_op jit(solution)/shard_map/ring2:2/ppermute | solution.py:33
  79.4 0.2 collective-permute-start.20
  79.6 0.3 collective-permute-start.22
  79.9 1.1 %collective-permute-done.13.refs_0_ = bf16[2,256,512]{2,1,0:T(8,128)(2,1)S(1)} collective-permute-done((bf16[2,256,512]{2,1,0:T(8,128)(2,1)S(1)}, bf16[2,256,512]{2,1,0:T(8,128)(2,1)S(1)}, u32[]{:S(2)}, u32[]{:S(2)}) %collective-permute-start.13) | collective-permute-done | bytes 524320 | tf_op jit(solution)/shard_map/along-1:2/ppermute | solution.py:37
  81.1 0.3 collective-permute-done.20.refs_1_
  81.3 0.7 collective-permute-done.22.refs_3_
  82.1 2.9 %shard_map.53 = (bf16[192,2,2048]{2,1,0:T(2,128)(2,1)}, bf16[192,2,2048]{2,1,0:T(2,128)(2,1)}, f32[768,512]{1,0:T(8,128)S(1)}) custom-call(bf16[192,4096]{1,0:T(8,128)(2,1)S(1)} %bitcast.7, bf16[192,4096]{1,0:T(8,128)(2,1)S(1)} %bitcast.12, bf16[2,256,512]{2,1,0:T(8,128)(2,1)S(1)} %collective-permute-done.16.refs_0_, ...), custom_call_target="tpu_custom_call", output_to_operand_aliasing={{0}: (8, {}), {1}: (9, {})} | custom-call | flops 1610612736 | bytes 4194304 | tf_op jit(solution)/shard_map/pallas_call | solution.py:118
  84.9 2.0 %shard_map.54 = (bf16[192,2,2048]{2,1,0:T(2,128)(2,1)}, bf16[192,2,2048]{2,1,0:T(2,128)(2,1)}) custom-call(bf16[192,4096]{1,0:T(8,128)(2,1)S(1)} %bitcast.8, bf16[192,4096]{1,0:T(8,128)(2,1)S(1)} %bitcast.13, bf16[2,256,512]{2,1,0:T(8,128)(2,1)S(1)} %collective-permute-done.13.refs_0_, ...), custom_call_target="tpu_custom_call", output_to_operand_aliasing={{0}: (5, {}), {1}: (6, {})} | custom-call | flops 805306368 | bytes 2097152 | tf_op jit(solution)/shard_map/pallas_call | solution.py:118
  (23 shorter events, 0.2 us)
Async XLA Ops:
  0.6 8.0 %collective-permute-start.3 = (bf16[2,256,512]{2,1,0:T(8,128)(2,1)}, bf16[2,256,512]{2,1,0:T(8,128)(2,1)S(1)}, u32[]{:S(2)}, u32[]{:S(2)}) collective-permute-start(bf16[2,256,512]{2,1,0:T(8,128)(2,1)} %refs_0_.1), channel_id=1, source_target_pairs={{0,4},{1,5},{2,6},{3,7},{4,0},{5,1},{6,2},{7,3},{16,20},{17,21},{1... | collective-permute-start | bytes 1572872 | tf_op jit(solution)/shard_map/core0:0/ppermute | solution.py:41
  1.1 17.4 %collective-permute-start.2 = (bf16[2,256,512]{2,1,0:T(8,128)(2,1)}, bf16[2,256,512]{2,1,0:T(8,128)(2,1)S(1)}, u32[]{:S(2)}, u32[]{:S(2)}) collective-permute-start(bf16[2,256,512]{2,1,0:T(8,128)(2,1)} %refs_0_.1), channel_id=1, source_target_pairs={{0,1},{1,2},{2,3},{3,0},{4,5},{5,6},{6,7},{7,4},{16,17},{17,18},{1... | collective-permute-start | bytes 1572872 | tf_op jit(solution)/shard_map/along1:0/ppermute | solution.py:37
  3.8 14.8 %collective-permute-start.1 = (bf16[2,256,512]{2,1,0:T(8,128)(2,1)}, bf16[2,256,512]{2,1,0:T(8,128)(2,1)S(1)}, u32[]{:S(2)}, u32[]{:S(2)}) collective-permute-start(bf16[2,256,512]{2,1,0:T(8,128)(2,1)} %refs_0_.1), channel_id=1, source_target_pairs={{0,8},{1,9},{2,10},{3,11},{4,20},{5,21},{6,22},{7,23},{16,0},{17,1... | collective-permute-start | bytes 1572872 | tf_op jit(solution)/shard_map/ring0:-1/ppermute | solution.py:33
  5.3 13.3 %collective-permute-start = (bf16[2,256,512]{2,1,0:T(8,128)(2,1)}, bf16[2,256,512]{2,1,0:T(8,128)(2,1)S(1)}, u32[]{:S(2)}, u32[]{:S(2)}) collective-permute-start(bf16[2,256,512]{2,1,0:T(8,128)(2,1)} %refs_0_.1), channel_id=1, source_target_pairs={{0,16},{1,17},{2,18},{3,19},{4,12},{5,13},{6,14},{7,15},{16,24},{1... | collective-permute-start | bytes 1572872 | tf_op jit(solution)/shard_map/ring0:1/ppermute | solution.py:33
  5.8 2.2 %copy-start.1 = (bf16[192,2,2048]{2,1,0:T(2,128)(2,1)S(1)}, bf16[192,2,2048]{2,1,0:T(2,128)(2,1)}, u32[]{:S(2)}) copy-start(bf16[192,2,2048]{2,1,0:T(2,128)(2,1)} %param.4) | copy-start | bytes 4718596
  18.7 3.9 %copy-start = (bf16[2,256,512]{2,1,0:T(8,128)(2,1)S(1)}, bf16[2,256,512]{2,1,0:T(8,128)(2,1)}, u32[]{:S(2)}) copy-start(bf16[2,256,512]{2,1,0:T(8,128)(2,1)} %refs_0_.1) | copy-start | bytes 1572868
  18.7 22.9 %collective-permute-start.6 = (bf16[6,256,512]{2,1,0:T(8,128)(2,1)S(1)}, bf16[6,256,512]{2,1,0:T(8,128)(2,1)S(1)}, u32[]{:S(2)}, u32[]{:S(2)}) collective-permute-start(bf16[6,256,512]{2,1,0:T(8,128)(2,1)S(1)} %pad_maximum_fusion.1), channel_id=1, source_target_pairs={{0,4},{1,5},{2,6},{3,7},{4,0},{5,1},{6,2},{7,3},{16,20},{17,21},{1... | collective-permute-start | bytes 4718600 | tf_op jit(solution)/shard_map/core0:1_0:-1_1:0/ppermute | solution.py:41
  19.0 20.5 %collective-permute-start.4 = (bf16[4,256,512]{2,1,0:T(8,128)(2,1)S(1)}, bf16[4,256,512]{2,1,0:T(8,128)(2,1)S(1)}, u32[]{:S(2)}, u32[]{:S(2)}) collective-permute-start(bf16[4,256,512]{2,1,0:T(8,128)(2,1)S(1)} %pad_maximum_fusion.3), channel_id=1, source_target_pairs={{0,16},{1,17},{2,18},{3,19},{4,12},{5,13},{6,14},{7,15},{16,24},{1... | collective-permute-start | bytes 3145736 | tf_op jit(solution)/shard_map/ring0:2_1:1/ppermute | solution.py:33
  20.6 21.1 %collective-permute-start.7 = (bf16[2,256,512]{2,1,0:T(8,128)(2,1)S(1)}, bf16[2,256,512]{2,1,0:T(8,128)(2,1)S(1)}, u32[]{:S(2)}, u32[]{:S(2)}) collective-permute-start(bf16[2,256,512]{2,1,0:T(8,128)(2,1)S(1)} %collective-permute-done.2.refs_5_), channel_id=1, source_target_pairs={{0,1},{1,2},{2,3},{3,0},{4,5},{5,6},{6,7},{7,4},{16,17},{17,18},{1... | collective-permute-start | bytes 1572872 | tf_op jit(solution)/shard_map/along2:0/ppermute | solution.py:37
  22.1 19.6 %collective-permute-start.5 = (bf16[2,256,512]{2,1,0:T(8,128)(2,1)S(1)}, bf16[2,256,512]{2,1,0:T(8,128)(2,1)S(1)}, u32[]{:S(2)}, u32[]{:S(2)}) collective-permute-start(bf16[2,256,512]{2,1,0:T(8,128)(2,1)S(1)} %collective-permute-done.2.refs_5_), channel_id=1, source_target_pairs={{0,8},{1,9},{2,10},{3,11},{4,20},{5,21},{6,22},{7,23},{16,0},{17,1... | collective-permute-start | bytes 1572872 | tf_op jit(solution)/shard_map/ring1:-1/ppermute | solution.py:33
  22.7 19.0 %collective-permute-start.8 = (bf16[2,128,512]{2,1,0:T(8,128)(2,1)S(1)}, bf16[2,128,512]{2,1,0:T(8,128)(2,1)S(1)}, u32[]{:S(2)}, u32[]{:S(2)}) collective-permute-start(bf16[2,128,512]{2,1,0:T(8,128)(2,1)S(1)} %get-tuple-element.37), channel_id=1, source_target_pairs={{0,3},{1,0},{2,1},{3,2},{4,7},{5,4},{6,5},{7,6},{16,19},{17,16},{1... | collective-permute-start | bytes 786440 | tf_op jit(solution)/shard_map/along_upper/ppermute | solution.py:37
  41.9 7.4 %collective-permute-start.11 = (bf16[8,256,512]{2,1,0:T(8,128)(2,1)S(1)}, bf16[8,256,512]{2,1,0:T(8,128)(2,1)S(1)}, u32[]{:S(2)}, u32[]{:S(2)}) collective-permute-start(bf16[8,256,512]{2,1,0:T(8,128)(2,1)S(1)} %pad_maximum_fusion), channel_id=1, source_target_pairs={{0,4},{1,5},{2,6},{3,7},{4,0},{5,1},{6,2},{7,3},{16,20},{17,21},{1... | collective-permute-start | bytes 6291464 | tf_op jit(solution)/shard_map/core0:2_1:1_1:-1_2:0/ppermute | solution.py:41
  42.1 20.5 %collective-permute-start.9 = (bf16[4,256,512]{2,1,0:T(8,128)(2,1)S(1)}, bf16[4,256,512]{2,1,0:T(8,128)(2,1)S(1)}, u32[]{:S(2)}, u32[]{:S(2)}) collective-permute-start(bf16[4,256,512]{2,1,0:T(8,128)(2,1)S(1)} %pad_maximum_fusion.4), channel_id=1, source_target_pairs={{0,16},{1,17},{2,18},{3,19},{4,12},{5,13},{6,14},{7,15},{16,24},{1... | collective-permute-start | bytes 3145736 | tf_op jit(solution)/shard_map/ring1:2_2:1/ppermute | solution.py:33
  43.0 19.6 %collective-permute-start.10 = (bf16[2,256,512]{2,1,0:T(8,128)(2,1)S(1)}, bf16[2,256,512]{2,1,0:T(8,128)(2,1)S(1)}, u32[]{:S(2)}, u32[]{:S(2)}) collective-permute-start(bf16[2,256,512]{2,1,0:T(8,128)(2,1)S(1)} %collective-permute-done.7.refs_3_), channel_id=1, source_target_pairs={{0,8},{1,9},{2,10},{3,11},{4,20},{5,21},{6,22},{7,23},{16,0},{17,1... | collective-permute-start | bytes 1572872 | tf_op jit(solution)/shard_map/ring2:-1/ppermute | solution.py:33
  44.3 19.4 %collective-permute-start.15 = (bf16[2,384,512]{2,1,0:T(8,128)(2,1)S(1)}, bf16[2,384,512]{2,1,0:T(8,128)(2,1)S(1)}, u32[]{:S(2)}, u32[]{:S(2)}) collective-permute-start(bf16[2,384,512]{2,1,0:T(8,128)(2,1)S(1)} %pad_maximum_fusion.6), channel_id=1, source_target_pairs={{0,3},{1,0},{2,1},{3,2},{4,7},{5,4},{6,5},{7,6},{16,19},{17,16},{1... | collective-permute-start | bytes 2359304 | tf_op jit(solution)/shard_map/along_lower/ppermute | solution.py:37
  53.9 9.8 %collective-permute-start.12 = (bf16[1,16,128]{2,1,0:T(8,128)(2,1)S(1)}, bf16[1,16,128]{2,1,0:T(8,128)(2,1)S(1)}, u32[]{:S(2)}, u32[]{:S(2)}) collective-permute-start(bf16[1,16,128]{2,1,0:T(8,128)(2,1)S(1)} %get-tuple-element.45), channel_id=1, source_target_pairs={{0,4},{1,5},{2,6},{3,7},{4,0},{5,1},{6,2},{7,3},{16,20},{17,21},{1... | collective-permute-start | bytes 12296 | tf_op jit(solution)/shard_map/token/ppermute | solution.py:41
  63.9 6.3 %collective-permute-start.17 = (bf16[6,256,512]{2,1,0:T(8,128)(2,1)S(1)}, bf16[6,256,512]{2,1,0:T(8,128)(2,1)S(1)}, u32[]{:S(2)}, u32[]{:S(2)}) collective-permute-start(bf16[6,256,512]{2,1,0:T(8,128)(2,1)S(1)} %pad_maximum_fusion.2), channel_id=1, source_target_pairs={{0,4},{1,5},{2,6},{3,7},{4,0},{5,1},{6,2},{7,3},{16,20},{17,21},{1... | collective-permute-start | bytes 4718600 | tf_op jit(solution)/shard_map/core1:2_2:1_2:-1/ppermute | solution.py:41
  64.2 6.0 %collective-permute-start.18 = (bf16[4,256,512]{2,1,0:T(8,128)(2,1)S(1)}, bf16[4,256,512]{2,1,0:T(8,128)(2,1)S(1)}, u32[]{:S(2)}, u32[]{:S(2)}) collective-permute-start(bf16[4,256,512]{2,1,0:T(8,128)(2,1)S(1)} %pad_maximum_fusion.5), channel_id=1, source_target_pairs={{0,4},{1,5},{2,6},{3,7},{4,0},{5,1},{6,2},{7,3},{16,20},{17,21},{1... | collective-permute-start | bytes 3145736 | tf_op jit(solution)/shard_map/core-1:0_-1:1/ppermute | solution.py:41
  64.7 14.7 %collective-permute-start.21 = (bf16[2,256,512]{2,1,0:T(8,128)(2,1)S(1)}, bf16[2,256,512]{2,1,0:T(8,128)(2,1)S(1)}, u32[]{:S(2)}, u32[]{:S(2)}) collective-permute-start(bf16[2,256,512]{2,1,0:T(8,128)(2,1)S(1)} %get-tuple-element.50), channel_id=1, source_target_pairs={{0,16},{1,17},{2,18},{3,19},{4,12},{5,13},{6,14},{7,15},{16,24},{1... | collective-permute-start | bytes 1572872 | tf_op jit(solution)/shard_map/ring2:2/ppermute | solution.py:33
  65.5 13.9 %collective-permute-start.16 = (bf16[2,256,512]{2,1,0:T(8,128)(2,1)S(1)}, bf16[2,256,512]{2,1,0:T(8,128)(2,1)S(1)}, u32[]{:S(2)}, u32[]{:S(2)}) collective-permute-start(bf16[2,256,512]{2,1,0:T(8,128)(2,1)S(1)} %pad_maximum_fusion.7.refs_3_), channel_id=1, source_target_pairs={{0,8},{1,9},{2,10},{3,11},{4,20},{5,21},{6,22},{7,23},{16,0},{17,1... | collective-permute-start | bytes 1572872 | tf_op jit(solution)/shard_map/ring-1:-1/ppermute | solution.py:33
  66.8 14.3 %collective-permute-start.13 = (bf16[2,256,512]{2,1,0:T(8,128)(2,1)S(1)}, bf16[2,256,512]{2,1,0:T(8,128)(2,1)S(1)}, u32[]{:S(2)}, u32[]{:S(2)}) collective-permute-start(bf16[2,256,512]{2,1,0:T(8,128)(2,1)S(1)} %get-tuple-element.46), channel_id=1, source_target_pairs={{0,3},{1,0},{2,1},{3,2},{4,7},{5,4},{6,5},{7,6},{16,19},{17,16},{1... | collective-permute-start | bytes 1572872 | tf_op jit(solution)/shard_map/along-1:2/ppermute | solution.py:37
  75.5 3.9 %collective-permute-start.19 = (bf16[1,16,128]{2,1,0:T(8,128)(2,1)S(1)}, bf16[1,16,128]{2,1,0:T(8,128)(2,1)S(1)}, u32[]{:S(2)}, u32[]{:S(2)}) collective-permute-start(bf16[1,16,128]{2,1,0:T(8,128)(2,1)S(1)} %get-tuple-element.57), channel_id=1, source_target_pairs={{0,4},{1,5},{2,6},{3,7},{4,0},{5,1},{6,2},{7,3},{16,20},{17,21},{1... | collective-permute-start | bytes 12296 | tf_op jit(solution)/shard_map/token/ppermute | solution.py:41
  79.4 1.9 %collective-permute-start.20 = (bf16[2,256,512]{2,1,0:T(8,128)(2,1)S(1)}, bf16[2,256,512]{2,1,0:T(8,128)(2,1)S(1)}, u32[]{:S(2)}, u32[]{:S(2)}) collective-permute-start(bf16[2,256,512]{2,1,0:T(8,128)(2,1)S(1)} %collective-permute-done.16.refs_0_), channel_id=1, source_target_pairs={{0,4},{1,5},{2,6},{3,7},{4,0},{5,1},{6,2},{7,3},{16,20},{17,21},{1... | collective-permute-start | bytes 1572872 | tf_op jit(solution)/shard_map/core-1:-1/ppermute | solution.py:41
  79.6 2.4 %collective-permute-start.22 = (bf16[2,256,512]{2,1,0:T(8,128)(2,1)S(1)}, bf16[2,256,512]{2,1,0:T(8,128)(2,1)S(1)}, u32[]{:S(2)}, u32[]{:S(2)}) collective-permute-start(bf16[2,256,512]{2,1,0:T(8,128)(2,1)S(1)} %collective-permute-done.21.refs_2_), channel_id=1, source_target_pairs={{0,4},{1,5},{2,6},{3,7},{4,0},{5,1},{6,2},{7,3},{16,20},{17,21},{1... | collective-permute-start | bytes 1572872 | tf_op jit(solution)/shard_map/core2:2/ppermute | solution.py:41
  81.1 3.9 %collective-permute-start.14 = (bf16[2,256,512]{2,1,0:T(8,128)(2,1)S(1)}, bf16[2,256,512]{2,1,0:T(8,128)(2,1)S(1)}, u32[]{:S(2)}, u32[]{:S(2)}) collective-permute-start(bf16[2,256,512]{2,1,0:T(8,128)(2,1)S(1)} %collective-permute-done.13.refs_0_), channel_id=1, source_target_pairs={{0,4},{1,5},{2,6},{3,7},{4,0},{5,1},{6,2},{7,3},{16,20},{17,21},{1... | collective-permute-start | bytes 1572872 | tf_op jit(solution)/shard_map/core-1:2/ppermute | solution.py:41

commit v5 on v4

--- a/solution.py
+++ b/solution.py
@@ -46,14 +46,14 @@
 
 
 class Part:
-    def __init__(self, stage, terms, begun=None, finish=True):
+    def __init__(self, stage, terms, begun=(), finish=True):
         self.stage, self.terms, self.begun, self.finish = stage, terms, begun, finish
 
 
 def parts_kernel(plan, rows, cols, n_arrays, n_outs, fresh, first, second, *refs):
     refs = list(refs)
     arrays = [refs.pop(0) for _ in range(n_arrays)]
-    begun = [refs.pop(0) if has else None for _, _, has, _ in plan]
+    begun = [[refs.pop(0) for _ in range(count)] for _, _, count, _ in plan]
     if n_outs and not fresh:
         del refs[:2]
     outs = [refs.pop(0) for _ in range(n_outs)]
@@ -66,7 +66,7 @@
     place = jnp.where(chip % 2 == 0, chip // 2, chips - 1 - chip // 2)
     copies = []
     for i, (stage, terms, _, finish) in enumerate(plan):
-        total = jnp.zeros((4 * g, width), jnp.float32) if begun[i] is None else begun[i][...]
+        total = jnp.zeros((4 * g, width), jnp.float32) if not begun[i] else functools.reduce(jnp.add, [b[...] for b in begun[i]])
         for hop, mine, array, number in terms:
             owner_core = core if mine else 1 - core
             at = (place + chips + jnp.where(owner_core == 0, -hop, hop)) % chips
@@ -93,7 +93,7 @@
         copy.wait()
 
 
-def run_parts(parts, rows, cols, lefts, like, outs=None):
+def run_parts(parts, rows, cols, lefts, like, outs=None, weight=1):
     g = like.shape[0]
     fresh = outs is None
     finishing = sum(p.finish for p in parts)
@@ -101,7 +101,7 @@
     arrays = list({id(t[2]): t[2] for p in parts for t in p.terms}.values())
     index = {id(a): i for i, a in enumerate(arrays)}
     depth, width = arrays[0].shape[1:]
-    operands = [*lefts, *arrays, *(p.begun for p in parts if p.begun is not None)]
+    operands = [*lefts, *arrays, *(b for p in parts for b in p.begun)]
     in_specs = [vmem] * len(operands)
     out_shape, out_specs, scratch, aliases = [], [], [], {}
     if finishing:
@@ -114,7 +114,7 @@
     out_shape += [jax.ShapeDtypeStruct((4 * g, width), jnp.float32)] * sums
     out_specs += [vmem] * sums
     count = sum(len(p.terms) for p in parts)
-    plan = [(p.stage, [(h, m, index[id(a)], n) for h, m, a, n in p.terms], p.begun is not None, p.finish) for p in parts]
+    plan = [(p.stage, [(h, m, index[id(a)], n) for h, m, a, n in p.terms], len(p.begun), p.finish) for p in parts]
     result = pl.pallas_call(
         functools.partial(parts_kernel, plan, rows, cols, len(arrays), 2 if finishing else 0, fresh),
         out_shape=out_shape,
@@ -123,7 +123,7 @@
         scratch_shapes=scratch,
         input_output_aliases=aliases,
         compiler_params=pltpu.CompilerParams(vmem_limit_bytes=28 * 2**20),
-        cost_estimate=pl.CostEstimate(flops=2 * 8 * g * depth * width * count, bytes_accessed=2**20 * count, transcendentals=0),
+        cost_estimate=pl.CostEstimate(flops=weight * 2 * 8 * g * depth * width * count, bytes_accessed=2**20 * count, transcendentals=0),
     )(*operands)
     return (tuple(result[:2]), result[2:]) if finishing else (outs, result)
 
@@ -150,23 +150,25 @@
         theirs.update({key: (value, number) for number, key in enumerate(keys)})
         return value
 
-    def part(layer, hops, begun=None, finish=True):
-        return Part(layer, [(h, whose is mine, *whose[layer, h]) for whose in (mine, theirs) for h in hops], begun, finish)
-
     state = {"outs": None, "tokens": 0}
-    sums, used = {}, {d: [] for d in distances}
-
-    def products(keys):
+    sums, used = {d: [] for d in distances}, {d: [] for d in distances}
+
+    def products(who, keys, fresh=(), more=(), weight=1):
         parts = []
         for d in distances:
-            hops = [h for h in full[d] if (d, h) in keys and h not in used[d]]
-            if hops:
-                used[d] += hops
-                parts.append(part(d, hops, sums.pop(d, None), len(used[d]) == len(full[d])))
+            terms = [(h, whose is mine, *whose[d, h]) for whose in who for e, h in keys if e == d]
+            terms += [(h, whose is mine, *whose[d, h]) for whose, e, h in more if e == d]
+            if terms:
+                used[d] += terms
+                begun = []
+                if d not in fresh:
+                    begun, sums[d] = sums[d], []
+                parts.append(Part(d, terms, begun, d not in fresh and len(used[d]) == 2 * len(full[d])))
         parts.sort(key=lambda p: p.finish)
-        state["outs"], kept = run(parts, outs=state["outs"])
+        state["outs"], kept = run(parts, outs=state["outs"], weight=weight)
         unfinished = [p for p in parts if not p.finish]
-        sums.update({p.stage: s for p, s in zip(unfinished, kept, strict=True)})
+        for p, s in zip(unfinished, kept, strict=True):
+            sums[p.stage].append(s)
         return kept[0] if unfinished else state["outs"][0]
 
     def token(value):
@@ -175,6 +177,7 @@
         with jax.named_scope("token"):
             return moves.other(after(lax.slice(ritz, (0, at, 0), (1, at + 16, 128)), value))
 
+    both = (mine, theirs)
     cut = ritz.shape[1] // 2
 
     def down(value, name, *gate):
@@ -183,21 +186,22 @@
 
     z1 = move("along", 1, [((0, 0), (1, 0))])
     p1 = move("ring", 1, [((0, 0), (0, 1))])
-    m1 = move("ring", -1, [((0, 0), (0, -1))])
-    e1 = swap([(0, 0)])
-    gate = (p1, m1, z1, e1, *lefts)
+    m1 = move("ring", -1, [((0, 0), (0, -1))], *lefts)
+    e1 = swap([(0, 0)], *lefts)
+    x2 = move("ring", 1, [((0, 1), (0, 2))], *lefts)
+    gate = (p1, z1)
     z2 = move("along", 1, [((1, 0), (2, 0))], *gate)
-    p2 = move("ring", 1, [((0, 1), (0, 2)), ((1, 0), (1, 1))], *gate)
-    m2 = move("ring", -1, [((1, 0), (1, -1))], *gate)
-    upper = down(ritz[:, :cut], "along_upper", *gate)
-    e2 = swap([(0, 1), (0, -1), (1, 0)], *gate)
-    gate = (p2, m2, e2, z2, upper)
+    s1 = move("ring", 1, [((1, 0), (1, 1))], *gate)
+    m2 = move("ring", -1, [((1, 0), (1, -1))], m1, *gate)
+    upper = down(ritz[:, :cut], "along_upper", m1, *gate)
+    gate = (lax.slice(x2, (0, 0, 0), (1, 16, 128)), s1, m2, e1, z2, upper)
     p3 = move("ring", 1, [((1, 1), (1, 2)), ((2, 0), (2, 1))], *gate)
     m3 = move("ring", -1, [((2, 0), (2, -1))], *gate)
     lower = down(jnp.concatenate([ritz[:, cut:], mine[0, 1][0]], 1), "along_lower", *gate)
-    e3 = swap([(0, 2), (1, 1), (1, -1), (2, 0)], *gate)
-    products([(0, 0), (0, 1), (0, -1), (1, 0)])
-    t = token(products([(0, 2), (1, 1), (1, -1), (2, 0)]))
+    e3 = swap([(0, 1), (0, -1), (0, 2), (1, 0)], *gate)
+    e3b = swap([(1, 1), (1, -1), (2, 0)], *gate)
+    products(both, [(0, 0), (0, 1), (0, -1), (0, 2), (1, 0)])
+    t = token(products(both, [(1, 1), (1, -1), (2, 0)]))
     mine[-1, 0] = jnp.concatenate([upper, lower[:, : ritz.shape[1] - cut]], 1), 0
     mine[-1, 1] = lower[:, ritz.shape[1] - cut :], 0
     gate = (p3, m3, e3, t)
@@ -207,12 +211,13 @@
     m4 = move("ring", -1, [((-1, 0), (-1, -1))], *gate)
     e4 = swap([(1, 2), (2, 1), (2, -1)], *gate)
     e4b = swap([(-1, 0), (-1, 1)], *gate)
-    t = token(products([(1, 2), (2, 1), (2, -1), (-1, 0), (-1, 1)]))
+    t = token(products(both, [(1, 2), (2, 1), (2, -1), (-1, 0), (-1, 1)]))
     swap([(2, 2)], t, e4)
     swap([(-1, -1)], t, e4)
-    products([(2, 2), (-1, -1)])
-    swap([(-1, 2)])
-    products([(-1, 2)])
+    swap([(-1, 2)], t, e4)
+    products([mine], [(2, 2), (-1, -1), (-1, 2)], (2, -1))
+    products([theirs], [(2, 2)])
+    products([theirs], [(-1, -1), (-1, 2)])
     return state["outs"]
 
 
@@ -237,7 +242,7 @@
         return (value,)
 
     def part(layer, hops, begun=None, finish=True):
-        return Part(layer, [(h, whose is mine, *whose[layer, h]) for whose in (mine, theirs) for h in hops], begun, finish)
+        return Part(layer, [(h, whose is mine, *whose[layer, h]) for whose in (mine, theirs) for h in hops], () if begun is None else (begun,), finish)
 
     def complete(layer):
         return [*range(chips - 1), -1] if layer in (0, -1) else [*range(chips)]

time: 87.3 us -> 84.4 us (0.967)
  waiting for transfers between devices: 42.1 us -> 37 us
  starting transfers between devices: 21.9 us -> 23.8 us
    ppermute x8 -> x9, waiting for transfers between devices: 26.9 us -> 19.7 us  [ring(): return lax.ppermute(value, AXES, pairs)]
    ppermute x5, waiting for transfers between devices: 14.1 us -> 17.1 us  [along(): return lax.ppermute(value, AXES, pairs)]
    ppermute x8 -> x9, starting transfers between devices: 8.26 us -> 10.3 us  [ring(): return lax.ppermute(value, AXES, pairs)]
    ppermute x10, waiting for transfers between devices: 1.03 us -> 0.1 us  [other(): return lax.ppermute(value, AXES, pairs)]
    pallas_call x5 -> x6, Pallas kernels: 18.1 us -> 18.3 us  [run_parts(): pl.pallas_call(functools.partial(parts_kernel, plan, rows, cols, len(arra...]
  transfers between devices with their start and end apart: 23 -> 24, of which waited for: 9 -> 10; matrix products, arithmetic and copies ran while one was open for 4% -> 4% of each run, Pallas kernels for 18% -> 19%
where the time goes in v5:
time: 84.4 us; the launch traced here: 84.2 us
  waiting for transfers between devices  37 us (44%)
  starting transfers between devices  23.8 us (28%)
  Pallas kernels  18.3 us (22%)
  local copies, waits for them, and re-layouts  3.37 us (4%)
  between operations  0.98 us (1%)
  other arithmetic  0.88 us (1%)
    ppermute x9, waiting for transfers between devices, ring(): return lax.ppermute(value, AXES, pairs)  19.7 us
    pallas_call x6, Pallas kernels, run_parts(): pl.pallas_call(functools.partial(parts_kernel, plan, rows, cols, len(arra...  18.3 us
    ppermute x5, waiting for transfers between devices, along(): return lax.ppermute(value, AXES, pairs)  17.1 us
    ppermute x5, starting transfers between devices, along(): return lax.ppermute(value, AXES, pairs)  11.3 us
    ppermute x9, starting transfers between devices, ring(): return lax.ppermute(value, AXES, pairs)  10.3 us
    unnamed x6, local copies, waits for them, and re-layouts  3.21 us
    ppermute x10, starting transfers between devices, other(): return lax.ppermute(value, AXES, pairs)  2.2 us
  transfers between devices with their start and end apart: 24, of which 10 were waited for; matrix products, arithmetic and copies ran while one was open for 4% of the time, Pallas kernels for 19%

profile of v5, /device:TPU:0, one launch (start us, length us, event | category | flops | bytes accessed | tf_op | source)
XLA Modules:
  0.0 84.2 jit_solution(9609408466895563)
XLA Ops:
  0.6 3.0 %collective-permute-start.1 = (bf16[2,256,512]{2,1,0:T(8,128)(2,1)}, bf16[2,256,512]{2,1,0:T(8,128)(2,1)S(1)}, u32[]{:S(2)}, u32[]{:S(2)}) collective-permute-start(bf16[2,256,512]{2,1,0:T(8,128)(2,1)} %refs_2_.1), channel_id=1, source_target_pairs={{0,16},{1,17},{2,18},{3,19},{4,12},{5,13},{6,14},{7,15},{16,24},{1... | collective-permute-start | bytes 1572872 | tf_op jit(solution)/shard_map/ring0:1/ppermute | solution.py:33
  3.6 1.6 %collective-permute-start.2 = (bf16[2,256,512]{2,1,0:T(8,128)(2,1)}, bf16[2,256,512]{2,1,0:T(8,128)(2,1)S(1)}, u32[]{:S(2)}, u32[]{:S(2)}) collective-permute-start(bf16[2,256,512]{2,1,0:T(8,128)(2,1)} %refs_2_.1), channel_id=1, source_target_pairs={{0,1},{1,2},{2,3},{3,0},{4,5},{5,6},{6,7},{7,4},{16,17},{17,18},{1... | collective-permute-start | bytes 1572872 | tf_op jit(solution)/shard_map/along1:0/ppermute | solution.py:37
  5.2 2.2 %copy.11 = bf16[24,8,2,2048]{3,1,2,0:T(8,128)(2,1)S(1)} copy(bf16[24,8,2,2048]{3,2,1,0:T(2,128)(2,1)} %bitcast.16) | data formatting | bytes 3145728
  7.4 0.0 copy-start
  7.4 0.6 copy.12
  8.1 0.4 copy-done
  8.5 0.5 collective-permute-start
  9.0 3.8 %collective-permute-done.1.refs_3_ = bf16[2,256,512]{2,1,0:T(8,128)(2,1)S(1)} collective-permute-done((bf16[2,256,512]{2,1,0:T(8,128)(2,1)}, bf16[2,256,512]{2,1,0:T(8,128)(2,1)S(1)}, u32[]{:S(2)}, u32[]{:S(2)}) %collective-permute-start.1) | collective-permute-done | bytes 524320 | tf_op jit(solution)/shard_map/ring0:1/ppermute | solution.py:33
  12.8 2.4 %collective-permute-start.4 = (bf16[2,256,512]{2,1,0:T(8,128)(2,1)S(1)}, bf16[2,256,512]{2,1,0:T(8,128)(2,1)S(1)}, u32[]{:S(2)}, u32[]{:S(2)}) collective-permute-start(bf16[2,256,512]{2,1,0:T(8,128)(2,1)S(1)} %collective-permute-done.1.refs_3_), channel_id=1, source_target_pairs={{0,16},{1,17},{2,18},{3,19},{4,12},{5,13},{6,14},{7,15},{16,24},{1... | collective-permute-start | bytes 1572872 | tf_op jit(solution)/shard_map/ring0:2/ppermute | solution.py:33
  15.2 3.9 %collective-permute-done.2.refs_0_ = bf16[2,256,512]{2,1,0:T(8,128)(2,1)S(1)} collective-permute-done((bf16[2,256,512]{2,1,0:T(8,128)(2,1)}, bf16[2,256,512]{2,1,0:T(8,128)(2,1)S(1)}, u32[]{:S(2)}, u32[]{:S(2)}) %collective-permute-start.2) | collective-permute-done | bytes 524320 | tf_op jit(solution)/shard_map/along1:0/ppermute | solution.py:37
  19.1 0.0 collective-permute-start.8
  19.1 0.5 collective-permute-start.5
  19.6 2.8 %collective-permute-done.refs_4_ = bf16[2,256,512]{2,1,0:T(8,128)(2,1)S(1)} collective-permute-done((bf16[2,256,512]{2,1,0:T(8,128)(2,1)S(1)}, bf16[2,256,512]{2,1,0:T(8,128)(2,1)S(1)}, u32[]{:S(2)}, u32[]{:S(2)}) %collective-permute-start) | collective-permute-done | bytes 524320 | tf_op jit(solution)/shard_map/ring0:-1/ppermute | solution.py:33
  22.4 0.0 collective-permute-start.6
  22.5 0.5 collective-permute-done.4.refs_5_
  23.0 6.3 %collective-permute-start.3 = (bf16[2,128,512]{2,1,0:T(8,128)(2,1)S(1)}, bf16[2,128,512]{2,1,0:T(8,128)(2,1)S(1)}, u32[]{:S(2)}, u32[]{:S(2)}) collective-permute-start(bf16[2,128,512]{2,1,0:T(8,128)(2,1)S(1)} %get-tuple-element.40), channel_id=1, source_target_pairs={{0,3},{1,0},{2,1},{3,2},{4,7},{5,4},{6,5},{7,6},{16,19},{17,16},{1... | collective-permute-start | bytes 786440 | tf_op jit(solution)/shard_map/along_upper/ppermute | solution.py:37
  29.2 9.8 %collective-permute-done.3 = bf16[2,128,512]{2,1,0:T(8,128)(2,1)S(1)} collective-permute-done((bf16[2,128,512]{2,1,0:T(8,128)(2,1)S(1)}, bf16[2,128,512]{2,1,0:T(8,128)(2,1)S(1)}, u32[]{:S(2)}, u32[]{:S(2)}) %collective-permute-start.3) | collective-permute-done | bytes 262176 | tf_op jit(solution)/shard_map/along_upper/ppermute | solution.py:37
  39.1 0.3 pad_maximum_fusion
  39.3 0.1 collective-permute-start.12
  39.4 0.2 pad_maximum_fusion.1
  39.6 0.5 collective-permute-start.13
  40.2 0.1 pad_maximum_fusion.3
  40.3 0.7 collective-permute-start.10
  41.0 0.1 pad_maximum_fusion.5
  41.1 2.2 %collective-permute-start.11 = (bf16[2,256,512]{2,1,0:T(8,128)(2,1)S(1)}, bf16[2,256,512]{2,1,0:T(8,128)(2,1)S(1)}, u32[]{:S(2)}, u32[]{:S(2)}) collective-permute-start(bf16[2,256,512]{2,1,0:T(8,128)(2,1)S(1)} %collective-permute-done.8.refs_3_), channel_id=1, source_target_pairs={{0,8},{1,9},{2,10},{3,11},{4,20},{5,21},{6,22},{7,23},{16,0},{17,1... | collective-permute-start | bytes 1572872 | tf_op jit(solution)/shard_map/ring2:-1/ppermute | solution.py:33
  43.2 0.3 collective-permute-start.9
  43.5 0.1 collective-permute-done.12.refs_1_
  43.6 5.2 %shard_map.50 = (bf16[192,2,2048]{2,1,0:T(2,128)(2,1)}, bf16[192,2,2048]{2,1,0:T(2,128)(2,1)}, f32[768,512]{1,0:T(8,128)S(1)}) custom-call(bf16[192,4096]{1,0:T(8,128)(2,1)S(1)} %bitcast.4, bf16[192,4096]{1,0:T(8,128)(2,1)S(1)} %bitcast.10, bf16[2,256,512]{2,1,0:T(8,128)(2,1)S(1)} %collective-permute-done.2.refs_0_, ...), custom_call_target="tpu_custom_call" | custom-call | flops 4026531840 | bytes 10485760 | tf_op jit(solution)/shard_map/pallas_call | solution.py:118
  48.8 2.6 %shard_map.51 = (f32[768,512]{1,0:T(8,128)S(1)}, f32[768,512]{1,0:T(8,128)S(1)}) custom-call(bf16[192,4096]{1,0:T(8,128)(2,1)S(1)} %bitcast.5, bf16[192,4096]{1,0:T(8,128)(2,1)S(1)} %bitcast.11, bf16[2,256,512]{2,1,0:T(8,128)(2,1)S(1)} %collective-permute-done.5.refs_0_, bf16[2,256,512]{2,1,0:T(8,128)(2,1)S(1)} %collective-permute-done.6.refs_1_, ...), custom_call_target="tpu_custom_call" | custom-call | flops 2415919104 | bytes 6291456 | tf_op jit(solution)/shard_map/pallas_call | solution.py:118
  51.5 0.2 collective-permute-start.14
  51.7 9.8 %collective-permute-done.10.refs_0_ = bf16[4,256,512]{2,1,0:T(8,128)(2,1)S(1)} collective-permute-done((bf16[4,256,512]{2,1,0:T(8,128)(2,1)S(1)}, bf16[4,256,512]{2,1,0:T(8,128)(2,1)S(1)}, u32[]{:S(2)}, u32[]{:S(2)}) %collective-permute-start.10) | collective-permute-done | bytes 1048608 | tf_op jit(solution)/shard_map/ring1:2_2:1/ppermute | solution.py:33
  61.5 0.1 fusion
  61.6 0.9 %collective-permute-done.9 = bf16[2,384,512]{2,1,0:T(8,128)(2,1)S(1)} collective-permute-done((bf16[2,384,512]{2,1,0:T(8,128)(2,1)S(1)}, bf16[2,384,512]{2,1,0:T(8,128)(2,1)S(1)}, u32[]{:S(2)}, u32[]{:S(2)}) %collective-permute-start.9) | collective-permute-done | bytes 786464 | tf_op jit(solution)/shard_map/along_lower/ppermute | solution.py:37
  62.4 0.2 pad_maximum_fusion.2
  62.6 0.1 collective-permute-start.16
  62.8 0.1 pad_maximum_fusion.4
  62.9 0.6 collective-permute-start.17
  63.5 3.1 %collective-permute-start.20 = (bf16[2,256,512]{2,1,0:T(8,128)(2,1)S(1)}, bf16[2,256,512]{2,1,0:T(8,128)(2,1)S(1)}, u32[]{:S(2)}, u32[]{:S(2)}) collective-permute-start(bf16[2,256,512]{2,1,0:T(8,128)(2,1)S(1)} %collective-permute-done.4.refs_5_), channel_id=1, source_target_pairs={{0,3},{1,0},{2,1},{3,2},{4,7},{5,4},{6,5},{7,6},{16,19},{17,16},{1... | collective-permute-start | bytes 1572872 | tf_op jit(solution)/shard_map/along-1:2/ppermute | solution.py:37
  66.6 1.0 %collective-permute-start.15 = (bf16[2,256,512]{2,1,0:T(8,128)(2,1)S(1)}, bf16[2,256,512]{2,1,0:T(8,128)(2,1)S(1)}, u32[]{:S(2)}, u32[]{:S(2)}) collective-permute-start(bf16[2,256,512]{2,1,0:T(8,128)(2,1)S(1)} %pad_maximum_fusion.6.refs_3_), channel_id=1, source_target_pairs={{0,8},{1,9},{2,10},{3,11},{4,20},{5,21},{6,22},{7,23},{16,0},{17,1... | collective-permute-start | bytes 1572872 | tf_op jit(solution)/shard_map/ring-1:-1/ppermute | solution.py:33
  67.6 0.0 collective-permute-done.17.refs_5_
  67.6 5.3 %shard_map.52 = (bf16[192,2,2048]{2,1,0:T(2,128)(2,1)}, bf16[192,2,2048]{2,1,0:T(2,128)(2,1)}, f32[768,512]{1,0:T(8,128)S(1)}, f32[768,512]{1,0:T(8,128)S(1)}) custom-call(bf16[192,4096]{1,0:T(8,128)(2,1)S(1)} %bitcast.6, bf16[192,4096]{1,0:T(8,128)(2,1)S(1)} %bitcast.12, ...), custom_call_target="tpu_custom_call", output_to_operand_aliasing={{0}: (10, {}), {1}: (11, {})} | custom-call | flops 4026531840 | bytes 10485760 | tf_op jit(solution)/shard_map/pallas_call | solution.py:118
  72.9 0.2 collective-permute-start.18
  73.1 2.8 %collective-permute-done.22.refs_0_ = bf16[2,256,512]{2,1,0:T(8,128)(2,1)S(1)} collective-permute-done((bf16[2,256,512]{2,1,0:T(8,128)(2,1)S(1)}, bf16[2,256,512]{2,1,0:T(8,128)(2,1)S(1)}, u32[]{:S(2)}, u32[]{:S(2)}) %collective-permute-start.22) | collective-permute-done | bytes 524320 | tf_op jit(solution)/shard_map/ring2:2/ppermute | solution.py:33
  75.9 2.5 %collective-permute-done.20.refs_2_ = bf16[2,256,512]{2,1,0:T(8,128)(2,1)S(1)} collective-permute-done((bf16[2,256,512]{2,1,0:T(8,128)(2,1)S(1)}, bf16[2,256,512]{2,1,0:T(8,128)(2,1)S(1)}, u32[]{:S(2)}, u32[]{:S(2)}) %collective-permute-start.20) | collective-permute-done | bytes 524320 | tf_op jit(solution)/shard_map/along-1:2/ppermute | solution.py:37
  78.4 0.5 collective-permute-start.21
  78.9 1.4 %shard_map.53 = (f32[768,512]{1,0:T(8,128)S(1)}, f32[768,512]{1,0:T(8,128)S(1)}) custom-call(bf16[192,4096]{1,0:T(8,128)(2,1)S(1)} %bitcast.7, bf16[192,4096]{1,0:T(8,128)(2,1)S(1)} %bitcast.13, bf16[2,256,512]{2,1,0:T(8,128)(2,1)S(1)} %collective-permute-done.22.refs_0_, bf16[2,256,512]{2,1,0:T(8,128)(2,1)S(1)} %collective-permute-done.15.refs_1_, ...), custom_call_target="tpu_custom_call" | custom-call | flops 1207959552 | bytes 3145728 | tf_op jit(solution)/shard_map/pallas_call | solution.py:118
  80.3 1.7 %shard_map.54 = (bf16[192,2,2048]{2,1,0:T(2,128)(2,1)}, bf16[192,2,2048]{2,1,0:T(2,128)(2,1)}) custom-call(bf16[192,4096]{1,0:T(8,128)(2,1)S(1)} %bitcast.8, bf16[192,4096]{1,0:T(8,128)(2,1)S(1)} %bitcast.14, bf16[2,256,512]{2,1,0:T(8,128)(2,1)S(1)} %collective-permute-done.23.refs_0_, ...), custom_call_target="tpu_custom_call", output_to_operand_aliasing={{0}: (5, {}), {1}: (6, {})} | custom-call | flops 402653184 | bytes 1048576 | tf_op jit(solution)/shard_map/pallas_call | solution.py:118
  82.0 2.1 %shard_map.55 = (bf16[192,2,2048]{2,1,0:T(2,128)(2,1)}, bf16[192,2,2048]{2,1,0:T(2,128)(2,1)}) custom-call(bf16[192,4096]{1,0:T(8,128)(2,1)S(1)} %bitcast.9, bf16[192,4096]{1,0:T(8,128)(2,1)S(1)} %bitcast.15, bf16[2,256,512]{2,1,0:T(8,128)(2,1)S(1)} %collective-permute-done.19.refs_0_, ...), custom_call_target="tpu_custom_call", output_to_operand_aliasing={{0}: (6, {}), {1}: (7, {})} | custom-call | flops 805306368 | bytes 2097152 | tf_op jit(solution)/shard_map/pallas_call | solution.py:118
  (24 shorter events, 0.2 us)
Async XLA Ops:
  0.6 12.2 %collective-permute-start.1 = (bf16[2,256,512]{2,1,0:T(8,128)(2,1)}, bf16[2,256,512]{2,1,0:T(8,128)(2,1)S(1)}, u32[]{:S(2)}, u32[]{:S(2)}) collective-permute-start(bf16[2,256,512]{2,1,0:T(8,128)(2,1)} %refs_2_.1), channel_id=1, source_target_pairs={{0,16},{1,17},{2,18},{3,19},{4,12},{5,13},{6,14},{7,15},{16,24},{1... | collective-permute-start | bytes 1572872 | tf_op jit(solution)/shard_map/ring0:1/ppermute | solution.py:33
  3.6 15.5 %collective-permute-start.2 = (bf16[2,256,512]{2,1,0:T(8,128)(2,1)}, bf16[2,256,512]{2,1,0:T(8,128)(2,1)S(1)}, u32[]{:S(2)}, u32[]{:S(2)}) collective-permute-start(bf16[2,256,512]{2,1,0:T(8,128)(2,1)} %refs_2_.1), channel_id=1, source_target_pairs={{0,1},{1,2},{2,3},{3,0},{4,5},{5,6},{6,7},{7,4},{16,17},{17,18},{1... | collective-permute-start | bytes 1572872 | tf_op jit(solution)/shard_map/along1:0/ppermute | solution.py:37
  5.2 2.2 %copy-start.1 = (bf16[192,2,2048]{2,1,0:T(2,128)(2,1)S(1)}, bf16[192,2,2048]{2,1,0:T(2,128)(2,1)}, u32[]{:S(2)}) copy-start(bf16[192,2,2048]{2,1,0:T(2,128)(2,1)} %param.4) | copy-start | bytes 4718596
  7.4 1.0 %copy-start = (bf16[2,256,512]{2,1,0:T(8,128)(2,1)S(1)}, bf16[2,256,512]{2,1,0:T(8,128)(2,1)}, u32[]{:S(2)}) copy-start(bf16[2,256,512]{2,1,0:T(8,128)(2,1)} %refs_2_.1) | copy-start | bytes 1572868
  8.5 14.0 %collective-permute-start = (bf16[2,256,512]{2,1,0:T(8,128)(2,1)S(1)}, bf16[2,256,512]{2,1,0:T(8,128)(2,1)S(1)}, u32[]{:S(2)}, u32[]{:S(2)}) collective-permute-start(bf16[2,256,512]{2,1,0:T(8,128)(2,1)S(1)} %copy-done), channel_id=1, source_target_pairs={{0,8},{1,9},{2,10},{3,11},{4,20},{5,21},{6,22},{7,23},{16,0},{17,1... | collective-permute-start | bytes 1572872 | tf_op jit(solution)/shard_map/ring0:-1/ppermute | solution.py:33
  12.8 10.2 %collective-permute-start.4 = (bf16[2,256,512]{2,1,0:T(8,128)(2,1)S(1)}, bf16[2,256,512]{2,1,0:T(8,128)(2,1)S(1)}, u32[]{:S(2)}, u32[]{:S(2)}) collective-permute-start(bf16[2,256,512]{2,1,0:T(8,128)(2,1)S(1)} %collective-permute-done.1.refs_3_), channel_id=1, source_target_pairs={{0,16},{1,17},{2,18},{3,19},{4,12},{5,13},{6,14},{7,15},{16,24},{1... | collective-permute-start | bytes 1572872 | tf_op jit(solution)/shard_map/ring0:2/ppermute | solution.py:33
  15.2 14.1 %collective-permute-start.7 = (bf16[2,256,512]{2,1,0:T(8,128)(2,1)S(1)}, bf16[2,256,512]{2,1,0:T(8,128)(2,1)S(1)}, u32[]{:S(2)}, u32[]{:S(2)}) collective-permute-start(bf16[2,256,512]{2,1,0:T(8,128)(2,1)S(1)} %copy-done), channel_id=1, source_target_pairs={{0,4},{1,5},{2,6},{3,7},{4,0},{5,1},{6,2},{7,3},{16,20},{17,21},{1... | collective-permute-start | bytes 1572872 | tf_op jit(solution)/shard_map/core0:0/ppermute | solution.py:41
  19.1 20.0 %collective-permute-start.8 = (bf16[2,256,512]{2,1,0:T(8,128)(2,1)S(1)}, bf16[2,256,512]{2,1,0:T(8,128)(2,1)S(1)}, u32[]{:S(2)}, u32[]{:S(2)}) collective-permute-start(bf16[2,256,512]{2,1,0:T(8,128)(2,1)S(1)} %collective-permute-done.2.refs_0_), channel_id=1, source_target_pairs={{0,1},{1,2},{2,3},{3,0},{4,5},{5,6},{6,7},{7,4},{16,17},{17,18},{1... | collective-permute-start | bytes 1572872 | tf_op jit(solution)/shard_map/along2:0/ppermute | solution.py:37
  19.1 20.0 %collective-permute-start.5 = (bf16[2,256,512]{2,1,0:T(8,128)(2,1)S(1)}, bf16[2,256,512]{2,1,0:T(8,128)(2,1)S(1)}, u32[]{:S(2)}, u32[]{:S(2)}) collective-permute-start(bf16[2,256,512]{2,1,0:T(8,128)(2,1)S(1)} %collective-permute-done.2.refs_0_), channel_id=1, source_target_pairs={{0,16},{1,17},{2,18},{3,19},{4,12},{5,13},{6,14},{7,15},{16,24},{1... | collective-permute-start | bytes 1572872 | tf_op jit(solution)/shard_map/ring1:1/ppermute | solution.py:33
  22.4 16.7 %collective-permute-start.6 = (bf16[2,256,512]{2,1,0:T(8,128)(2,1)S(1)}, bf16[2,256,512]{2,1,0:T(8,128)(2,1)S(1)}, u32[]{:S(2)}, u32[]{:S(2)}) collective-permute-start(bf16[2,256,512]{2,1,0:T(8,128)(2,1)S(1)} %collective-permute-done.2.refs_0_), channel_id=1, source_target_pairs={{0,8},{1,9},{2,10},{3,11},{4,20},{5,21},{6,22},{7,23},{16,0},{17,1... | collective-permute-start | bytes 1572872 | tf_op jit(solution)/shard_map/ring1:-1/ppermute | solution.py:33
  23.0 16.1 %collective-permute-start.3 = (bf16[2,128,512]{2,1,0:T(8,128)(2,1)S(1)}, bf16[2,128,512]{2,1,0:T(8,128)(2,1)S(1)}, u32[]{:S(2)}, u32[]{:S(2)}) collective-permute-start(bf16[2,128,512]{2,1,0:T(8,128)(2,1)S(1)} %get-tuple-element.40), channel_id=1, source_target_pairs={{0,3},{1,0},{2,1},{3,2},{4,7},{5,4},{6,5},{7,6},{16,19},{17,16},{1... | collective-permute-start | bytes 786440 | tf_op jit(solution)/shard_map/along_upper/ppermute | solution.py:37
  39.3 4.2 %collective-permute-start.12 = (bf16[8,256,512]{2,1,0:T(8,128)(2,1)S(1)}, bf16[8,256,512]{2,1,0:T(8,128)(2,1)S(1)}, u32[]{:S(2)}, u32[]{:S(2)}) collective-permute-start(bf16[8,256,512]{2,1,0:T(8,128)(2,1)S(1)} %pad_maximum_fusion), channel_id=1, source_target_pairs={{0,4},{1,5},{2,6},{3,7},{4,0},{5,1},{6,2},{7,3},{16,20},{17,21},{1... | collective-permute-start | bytes 6291464 | tf_op jit(solution)/shard_map/core0:1_0:-1_0:2_1:0/ppermute | solution.py:41
  39.6 9.2 %collective-permute-start.13 = (bf16[6,256,512]{2,1,0:T(8,128)(2,1)S(1)}, bf16[6,256,512]{2,1,0:T(8,128)(2,1)S(1)}, u32[]{:S(2)}, u32[]{:S(2)}) collective-permute-start(bf16[6,256,512]{2,1,0:T(8,128)(2,1)S(1)} %pad_maximum_fusion.1), channel_id=1, source_target_pairs={{0,4},{1,5},{2,6},{3,7},{4,0},{5,1},{6,2},{7,3},{16,20},{17,21},{1... | collective-permute-start | bytes 4718600 | tf_op jit(solution)/shard_map/core1:1_1:-1_2:0/ppermute | solution.py:41
  40.3 21.2 %collective-permute-start.10 = (bf16[4,256,512]{2,1,0:T(8,128)(2,1)S(1)}, bf16[4,256,512]{2,1,0:T(8,128)(2,1)S(1)}, u32[]{:S(2)}, u32[]{:S(2)}) collective-permute-start(bf16[4,256,512]{2,1,0:T(8,128)(2,1)S(1)} %pad_maximum_fusion.3), channel_id=1, source_target_pairs={{0,16},{1,17},{2,18},{3,19},{4,12},{5,13},{6,14},{7,15},{16,24},{1... | collective-permute-start | bytes 3145736 | tf_op jit(solution)/shard_map/ring1:2_2:1/ppermute | solution.py:33
  41.1 20.5 %collective-permute-start.11 = (bf16[2,256,512]{2,1,0:T(8,128)(2,1)S(1)}, bf16[2,256,512]{2,1,0:T(8,128)(2,1)S(1)}, u32[]{:S(2)}, u32[]{:S(2)}) collective-permute-start(bf16[2,256,512]{2,1,0:T(8,128)(2,1)S(1)} %collective-permute-done.8.refs_3_), channel_id=1, source_target_pairs={{0,8},{1,9},{2,10},{3,11},{4,20},{5,21},{6,22},{7,23},{16,0},{17,1... | collective-permute-start | bytes 1572872 | tf_op jit(solution)/shard_map/ring2:-1/ppermute | solution.py:33
  43.2 19.2 %collective-permute-start.9 = (bf16[2,384,512]{2,1,0:T(8,128)(2,1)S(1)}, bf16[2,384,512]{2,1,0:T(8,128)(2,1)S(1)}, u32[]{:S(2)}, u32[]{:S(2)}) collective-permute-start(bf16[2,384,512]{2,1,0:T(8,128)(2,1)S(1)} %pad_maximum_fusion.5), channel_id=1, source_target_pairs={{0,3},{1,0},{2,1},{3,2},{4,7},{5,4},{6,5},{7,6},{16,19},{17,16},{1... | collective-permute-start | bytes 2359304 | tf_op jit(solution)/shard_map/along_lower/ppermute | solution.py:37
  51.5 11.0 %collective-permute-start.14 = (bf16[1,16,128]{2,1,0:T(8,128)(2,1)S(1)}, bf16[1,16,128]{2,1,0:T(8,128)(2,1)S(1)}, u32[]{:S(2)}, u32[]{:S(2)}) collective-permute-start(bf16[1,16,128]{2,1,0:T(8,128)(2,1)S(1)} %get-tuple-element.54), channel_id=1, source_target_pairs={{0,4},{1,5},{2,6},{3,7},{4,0},{5,1},{6,2},{7,3},{16,20},{17,21},{1... | collective-permute-start | bytes 12296 | tf_op jit(solution)/shard_map/token/ppermute | solution.py:41
  62.6 5.0 %collective-permute-start.16 = (bf16[6,256,512]{2,1,0:T(8,128)(2,1)S(1)}, bf16[6,256,512]{2,1,0:T(8,128)(2,1)S(1)}, u32[]{:S(2)}, u32[]{:S(2)}) collective-permute-start(bf16[6,256,512]{2,1,0:T(8,128)(2,1)S(1)} %pad_maximum_fusion.2), channel_id=1, source_target_pairs={{0,4},{1,5},{2,6},{3,7},{4,0},{5,1},{6,2},{7,3},{16,20},{17,21},{1... | collective-permute-start | bytes 4718600 | tf_op jit(solution)/shard_map/core1:2_2:1_2:-1/ppermute | solution.py:41
  62.9 4.7 %collective-permute-start.17 = (bf16[4,256,512]{2,1,0:T(8,128)(2,1)S(1)}, bf16[4,256,512]{2,1,0:T(8,128)(2,1)S(1)}, u32[]{:S(2)}, u32[]{:S(2)}) collective-permute-start(bf16[4,256,512]{2,1,0:T(8,128)(2,1)S(1)} %pad_maximum_fusion.4), channel_id=1, source_target_pairs={{0,4},{1,5},{2,6},{3,7},{4,0},{5,1},{6,2},{7,3},{16,20},{17,21},{1... | collective-permute-start | bytes 3145736 | tf_op jit(solution)/shard_map/core-1:0_-1:1/ppermute | solution.py:41
  63.5 12.4 %collective-permute-start.22 = (bf16[2,256,512]{2,1,0:T(8,128)(2,1)S(1)}, bf16[2,256,512]{2,1,0:T(8,128)(2,1)S(1)}, u32[]{:S(2)}, u32[]{:S(2)}) collective-permute-start(bf16[2,256,512]{2,1,0:T(8,128)(2,1)S(1)} %get-tuple-element.57), channel_id=1, source_target_pairs={{0,16},{1,17},{2,18},{3,19},{4,12},{5,13},{6,14},{7,15},{16,24},{1... | collective-permute-start | bytes 1572872 | tf_op jit(solution)/shard_map/ring2:2/ppermute | solution.py:33
  63.5 14.9 %collective-permute-start.20 = (bf16[2,256,512]{2,1,0:T(8,128)(2,1)S(1)}, bf16[2,256,512]{2,1,0:T(8,128)(2,1)S(1)}, u32[]{:S(2)}, u32[]{:S(2)}) collective-permute-start(bf16[2,256,512]{2,1,0:T(8,128)(2,1)S(1)} %collective-permute-done.4.refs_5_), channel_id=1, source_target_pairs={{0,3},{1,0},{2,1},{3,2},{4,7},{5,4},{6,5},{7,6},{16,19},{17,16},{1... | collective-permute-start | bytes 1572872 | tf_op jit(solution)/shard_map/along-1:2/ppermute | solution.py:37
  66.6 11.8 %collective-permute-start.15 = (bf16[2,256,512]{2,1,0:T(8,128)(2,1)S(1)}, bf16[2,256,512]{2,1,0:T(8,128)(2,1)S(1)}, u32[]{:S(2)}, u32[]{:S(2)}) collective-permute-start(bf16[2,256,512]{2,1,0:T(8,128)(2,1)S(1)} %pad_maximum_fusion.6.refs_3_), channel_id=1, source_target_pairs={{0,8},{1,9},{2,10},{3,11},{4,20},{5,21},{6,22},{7,23},{16,0},{17,1... | collective-permute-start | bytes 1572872 | tf_op jit(solution)/shard_map/ring-1:-1/ppermute | solution.py:33
  72.9 3.0 %collective-permute-start.18 = (bf16[1,16,128]{2,1,0:T(8,128)(2,1)S(1)}, bf16[1,16,128]{2,1,0:T(8,128)(2,1)S(1)}, u32[]{:S(2)}, u32[]{:S(2)}) collective-permute-start(bf16[1,16,128]{2,1,0:T(8,128)(2,1)S(1)} %get-tuple-element.64), channel_id=1, source_target_pairs={{0,4},{1,5},{2,6},{3,7},{4,0},{5,1},{6,2},{7,3},{16,20},{17,21},{1... | collective-permute-start | bytes 12296 | tf_op jit(solution)/shard_map/token/ppermute | solution.py:41
  75.9 4.4 %collective-permute-start.23 = (bf16[2,256,512]{2,1,0:T(8,128)(2,1)S(1)}, bf16[2,256,512]{2,1,0:T(8,128)(2,1)S(1)}, u32[]{:S(2)}, u32[]{:S(2)}) collective-permute-start(bf16[2,256,512]{2,1,0:T(8,128)(2,1)S(1)} %collective-permute-done.22.refs_0_), channel_id=1, source_target_pairs={{0,4},{1,5},{2,6},{3,7},{4,0},{5,1},{6,2},{7,3},{16,20},{17,21},{1... | collective-permute-start | bytes 1572872 | tf_op jit(solution)/shard_map/core2:2/ppermute | solution.py:41
  78.4 3.6 %collective-permute-start.19 = (bf16[2,256,512]{2,1,0:T(8,128)(2,1)S(1)}, bf16[2,256,512]{2,1,0:T(8,128)(2,1)S(1)}, u32[]{:S(2)}, u32[]{:S(2)}) collective-permute-start(bf16[2,256,512]{2,1,0:T(8,128)(2,1)S(1)} %collective-permute-done.15.refs_1_), channel_id=1, source_target_pairs={{0,4},{1,5},{2,6},{3,7},{4,0},{5,1},{6,2},{7,3},{16,20},{17,21},{1... | collective-permute-start | bytes 1572872 | tf_op jit(solution)/shard_map/core-1:-1/ppermute | solution.py:41
  78.4 3.6 %collective-permute-start.21 = (bf16[2,256,512]{2,1,0:T(8,128)(2,1)S(1)}, bf16[2,256,512]{2,1,0:T(8,128)(2,1)S(1)}, u32[]{:S(2)}, u32[]{:S(2)}) collective-permute-start(bf16[2,256,512]{2,1,0:T(8,128)(2,1)S(1)} %collective-permute-done.20.refs_2_), channel_id=1, source_target_pairs={{0,4},{1,5},{2,6},{3,7},{4,0},{5,1},{6,2},{7,3},{16,20},{17,21},{1... | collective-permute-start | bytes 1572872 | tf_op jit(solution)/shard_map/core-1:2/ppermute | solution.py:41

commit v6 on v5

--- a/solution.py
+++ b/solution.py
@@ -205,17 +205,18 @@
     mine[-1, 0] = jnp.concatenate([upper, lower[:, : ritz.shape[1] - cut]], 1), 0
     mine[-1, 1] = lower[:, ritz.shape[1] - cut :], 0
     gate = (p3, m3, e3, t)
-    z5 = move("along", -1, [((0, 2), (-1, 2))], *gate)
+    z5 = move("along", -1, [((0, 2), (-1, 2))], m3, e3, t)
     gate = (*gate, lower)
     p4 = move("ring", 1, [((2, 1), (2, 2))], *gate)
-    m4 = move("ring", -1, [((-1, 0), (-1, -1))], *gate)
     e4 = swap([(1, 2), (2, 1), (2, -1)], *gate)
     e4b = swap([(-1, 0), (-1, 1)], *gate)
+    m4 = move("ring", -1, [((-1, 0), (-1, -1))], e4b, *gate)
     t = token(products(both, [(1, 2), (2, 1), (2, -1), (-1, 0), (-1, 1)]))
     swap([(2, 2)], t, e4)
-    swap([(-1, -1)], t, e4)
-    swap([(-1, 2)], t, e4)
-    products([mine], [(2, 2), (-1, -1), (-1, 2)], (2, -1))
+    first = products([mine], [(2, 2)])
+    swap([(-1, -1)], first, t)
+    swap([(-1, 2)], first, t)
+    products([mine], [(-1, -1), (-1, 2)])
     products([theirs], [(2, 2)])
     products([theirs], [(-1, -1), (-1, 2)])
     return state["outs"]

time: 84.4 us -> 83.9 us (level)
  waiting for transfers between devices: 37 us -> 35.7 us
    ppermute x9, waiting for transfers between devices: 19.7 us -> 17.2 us  [ring(): return lax.ppermute(value, AXES, pairs)]
    ppermute x10, waiting for transfers between devices: 0.1 us -> 1.97 us  [other(): return lax.ppermute(value, AXES, pairs)]
    pallas_call x6 -> x7, Pallas kernels: 18.3 us -> 18.4 us  [run_parts(): pl.pallas_call(functools.partial(parts_kernel, plan, rows, cols, len(arra...]
  transfers between devices with their start and end apart: 24 -> 24, of which waited for: 10 -> 12; matrix products, arithmetic and copies ran while one was open for 4% -> 4% of each run, Pallas kernels for 19% -> 19%
where the time goes in v6:
time: 83.9 us; the launch traced here: 83.8 us
  waiting for transfers between devices  35.7 us (43%)
  starting transfers between devices  24.5 us (29%)
  Pallas kernels  18.4 us (22%)
  local copies, waits for them, and re-layouts  3.37 us (4%)
  between operations  1 us (1%)
  other arithmetic  0.88 us (1%)
    pallas_call x7, Pallas kernels, run_parts(): pl.pallas_call(functools.partial(parts_kernel, plan, rows, cols, len(arra...  18.4 us
    ppermute x9, waiting for transfers between devices, ring(): return lax.ppermute(value, AXES, pairs)  17.2 us
    ppermute x5, waiting for transfers between devices, along(): return lax.ppermute(value, AXES, pairs)  16.5 us
    ppermute x5, starting transfers between devices, along(): return lax.ppermute(value, AXES, pairs)  11.3 us
    ppermute x9, starting transfers between devices, ring(): return lax.ppermute(value, AXES, pairs)  11 us
    unnamed x6, local copies, waits for them, and re-layouts  3.21 us
    ppermute x10, starting transfers between devices, other(): return lax.ppermute(value, AXES, pairs)  2.22 us
    ppermute x10, waiting for transfers between devices, other(): return lax.ppermute(value, AXES, pairs)  1.97 us
  transfers between devices with their start and end apart: 24, of which 12 were waited for; matrix products, arithmetic and copies ran while one was open for 4% of the time, Pallas kernels for 19%

profile of v6, /device:TPU:0, one launch (start us, length us, event | category | flops | bytes accessed | tf_op | source)
XLA Modules:
  0.0 83.8 jit_solution(6785141624234156978)
XLA Ops:
  0.6 3.0 %collective-permute-start.1 = (bf16[2,256,512]{2,1,0:T(8,128)(2,1)}, bf16[2,256,512]{2,1,0:T(8,128)(2,1)S(1)}, u32[]{:S(2)}, u32[]{:S(2)}) collective-permute-start(bf16[2,256,512]{2,1,0:T(8,128)(2,1)} %refs_2_.1), channel_id=1, source_target_pairs={{0,16},{1,17},{2,18},{3,19},{4,12},{5,13},{6,14},{7,15},{16,24},{1... | collective-permute-start | bytes 1572872 | tf_op jit(solution)/shard_map/ring0:1/ppermute | solution.py:33
  3.6 1.6 %collective-permute-start.2 = (bf16[2,256,512]{2,1,0:T(8,128)(2,1)}, bf16[2,256,512]{2,1,0:T(8,128)(2,1)S(1)}, u32[]{:S(2)}, u32[]{:S(2)}) collective-permute-start(bf16[2,256,512]{2,1,0:T(8,128)(2,1)} %refs_2_.1), channel_id=1, source_target_pairs={{0,1},{1,2},{2,3},{3,0},{4,5},{5,6},{6,7},{7,4},{16,17},{17,18},{1... | collective-permute-start | bytes 1572872 | tf_op jit(solution)/shard_map/along1:0/ppermute | solution.py:37
  5.2 2.2 %copy.11 = bf16[24,8,2,2048]{3,1,2,0:T(8,128)(2,1)S(1)} copy(bf16[24,8,2,2048]{3,2,1,0:T(2,128)(2,1)} %bitcast.18) | data formatting | bytes 3145728
  7.4 0.6 copy.12
  8.1 0.4 copy-done
  8.5 0.5 collective-permute-start
  9.0 3.8 %collective-permute-done.1.refs_3_ = bf16[2,256,512]{2,1,0:T(8,128)(2,1)S(1)} collective-permute-done((bf16[2,256,512]{2,1,0:T(8,128)(2,1)}, bf16[2,256,512]{2,1,0:T(8,128)(2,1)S(1)}, u32[]{:S(2)}, u32[]{:S(2)}) %collective-permute-start.1) | collective-permute-done | bytes 524320 | tf_op jit(solution)/shard_map/ring0:1/ppermute | solution.py:33
  12.8 2.4 %collective-permute-start.4 = (bf16[2,256,512]{2,1,0:T(8,128)(2,1)S(1)}, bf16[2,256,512]{2,1,0:T(8,128)(2,1)S(1)}, u32[]{:S(2)}, u32[]{:S(2)}) collective-permute-start(bf16[2,256,512]{2,1,0:T(8,128)(2,1)S(1)} %collective-permute-done.1.refs_3_), channel_id=1, source_target_pairs={{0,16},{1,17},{2,18},{3,19},{4,12},{5,13},{6,14},{7,15},{16,24},{1... | collective-permute-start | bytes 1572872 | tf_op jit(solution)/shard_map/ring0:2/ppermute | solution.py:33
  15.2 3.9 %collective-permute-done.2.refs_0_ = bf16[2,256,512]{2,1,0:T(8,128)(2,1)S(1)} collective-permute-done((bf16[2,256,512]{2,1,0:T(8,128)(2,1)}, bf16[2,256,512]{2,1,0:T(8,128)(2,1)S(1)}, u32[]{:S(2)}, u32[]{:S(2)}) %collective-permute-start.2) | collective-permute-done | bytes 524320 | tf_op jit(solution)/shard_map/along1:0/ppermute | solution.py:37
  19.1 0.5 collective-permute-start.5
  19.6 2.8 %collective-permute-done.refs_4_ = bf16[2,256,512]{2,1,0:T(8,128)(2,1)S(1)} collective-permute-done((bf16[2,256,512]{2,1,0:T(8,128)(2,1)S(1)}, bf16[2,256,512]{2,1,0:T(8,128)(2,1)S(1)}, u32[]{:S(2)}, u32[]{:S(2)}) %collective-permute-start) | collective-permute-done | bytes 524320 | tf_op jit(solution)/shard_map/ring0:-1/ppermute | solution.py:33
  22.5 0.5 collective-permute-done.4.refs_5_
  23.0 6.3 %collective-permute-start.3 = (bf16[2,128,512]{2,1,0:T(8,128)(2,1)S(1)}, bf16[2,128,512]{2,1,0:T(8,128)(2,1)S(1)}, u32[]{:S(2)}, u32[]{:S(2)}) collective-permute-start(bf16[2,128,512]{2,1,0:T(8,128)(2,1)S(1)} %get-tuple-element.39), channel_id=1, source_target_pairs={{0,3},{1,0},{2,1},{3,2},{4,7},{5,4},{6,5},{7,6},{16,19},{17,16},{1... | collective-permute-start | bytes 786440 | tf_op jit(solution)/shard_map/along_upper/ppermute | solution.py:37
  29.2 9.8 %collective-permute-done.3 = bf16[2,128,512]{2,1,0:T(8,128)(2,1)S(1)} collective-permute-done((bf16[2,128,512]{2,1,0:T(8,128)(2,1)S(1)}, bf16[2,128,512]{2,1,0:T(8,128)(2,1)S(1)}, u32[]{:S(2)}, u32[]{:S(2)}) %collective-permute-start.3) | collective-permute-done | bytes 262176 | tf_op jit(solution)/shard_map/along_upper/ppermute | solution.py:37
  39.1 0.3 pad_maximum_fusion
  39.3 0.1 collective-permute-start.12
  39.4 0.2 pad_maximum_fusion.1
  39.6 0.5 collective-permute-start.13
  40.2 0.1 pad_maximum_fusion.3
  40.3 0.7 collective-permute-start.10
  41.0 0.1 pad_maximum_fusion.5
  41.1 2.2 %collective-permute-start.11 = (bf16[2,256,512]{2,1,0:T(8,128)(2,1)S(1)}, bf16[2,256,512]{2,1,0:T(8,128)(2,1)S(1)}, u32[]{:S(2)}, u32[]{:S(2)}) collective-permute-start(bf16[2,256,512]{2,1,0:T(8,128)(2,1)S(1)} %collective-permute-done.8.refs_3_), channel_id=1, source_target_pairs={{0,8},{1,9},{2,10},{3,11},{4,20},{5,21},{6,22},{7,23},{16,0},{17,1... | collective-permute-start | bytes 1572872 | tf_op jit(solution)/shard_map/ring2:-1/ppermute | solution.py:33
  43.2 0.3 collective-permute-start.9
  43.5 0.1 collective-permute-done.12.refs_1_
  43.6 5.2 %shard_map.50 = (bf16[192,2,2048]{2,1,0:T(2,128)(2,1)}, bf16[192,2,2048]{2,1,0:T(2,128)(2,1)}, f32[768,512]{1,0:T(8,128)S(1)}) custom-call(bf16[192,4096]{1,0:T(8,128)(2,1)S(1)} %bitcast.4, bf16[192,4096]{1,0:T(8,128)(2,1)S(1)} %bitcast.11, bf16[2,256,512]{2,1,0:T(8,128)(2,1)S(1)} %collective-permute-done.2.refs_0_, ...), custom_call_target="tpu_custom_call" | custom-call | flops 4026531840 | bytes 10485760 | tf_op jit(solution)/shard_map/pallas_call | solution.py:118
  48.8 2.6 %shard_map.51 = (f32[768,512]{1,0:T(8,128)S(1)}, f32[768,512]{1,0:T(8,128)S(1)}) custom-call(bf16[192,4096]{1,0:T(8,128)(2,1)S(1)} %bitcast.5, bf16[192,4096]{1,0:T(8,128)(2,1)S(1)} %bitcast.12, bf16[2,256,512]{2,1,0:T(8,128)(2,1)S(1)} %collective-permute-done.5.refs_0_, bf16[2,256,512]{2,1,0:T(8,128)(2,1)S(1)} %collective-permute-done.6.refs_1_, ...), custom_call_target="tpu_custom_call" | custom-call | flops 2415919104 | bytes 6291456 | tf_op jit(solution)/shard_map/pallas_call | solution.py:118
  51.5 0.2 collective-permute-start.14
  51.7 9.8 %collective-permute-done.10.refs_0_ = bf16[4,256,512]{2,1,0:T(8,128)(2,1)S(1)} collective-permute-done((bf16[4,256,512]{2,1,0:T(8,128)(2,1)S(1)}, bf16[4,256,512]{2,1,0:T(8,128)(2,1)S(1)}, u32[]{:S(2)}, u32[]{:S(2)}) %collective-permute-start.10) | collective-permute-done | bytes 1048608 | tf_op jit(solution)/shard_map/ring1:2_2:1/ppermute | solution.py:33
  61.5 0.1 fusion
  61.6 0.9 %collective-permute-done.9 = bf16[2,384,512]{2,1,0:T(8,128)(2,1)S(1)} collective-permute-done((bf16[2,384,512]{2,1,0:T(8,128)(2,1)S(1)}, bf16[2,384,512]{2,1,0:T(8,128)(2,1)S(1)}, u32[]{:S(2)}, u32[]{:S(2)}) %collective-permute-start.9) | collective-permute-done | bytes 786464 | tf_op jit(solution)/shard_map/along_lower/ppermute | solution.py:37
  62.4 0.2 pad_maximum_fusion.2
  62.6 0.1 collective-permute-start.18
  62.8 0.1 pad_maximum_fusion.4
  62.9 0.6 collective-permute-start.15
  63.5 3.1 %collective-permute-start.21 = (bf16[2,256,512]{2,1,0:T(8,128)(2,1)S(1)}, bf16[2,256,512]{2,1,0:T(8,128)(2,1)S(1)}, u32[]{:S(2)}, u32[]{:S(2)}) collective-permute-start(bf16[2,256,512]{2,1,0:T(8,128)(2,1)S(1)} %collective-permute-done.4.refs_5_), channel_id=1, source_target_pairs={{0,3},{1,0},{2,1},{3,2},{4,7},{5,4},{6,5},{7,6},{16,19},{17,16},{1... | collective-permute-start | bytes 1572872 | tf_op jit(solution)/shard_map/along-1:2/ppermute | solution.py:37
  66.6 1.0 %collective-permute-done.15.refs_5_ = bf16[4,256,512]{2,1,0:T(8,128)(2,1)S(1)} collective-permute-done((bf16[4,256,512]{2,1,0:T(8,128)(2,1)S(1)}, bf16[4,256,512]{2,1,0:T(8,128)(2,1)S(1)}, u32[]{:S(2)}, u32[]{:S(2)}) %collective-permute-start.15) | collective-permute-done | bytes 1048608 | tf_op jit(solution)/shard_map/core-1:0_-1:1/ppermute | solution.py:41
  67.6 1.7 %collective-permute-start.16 = (bf16[2,256,512]{2,1,0:T(8,128)(2,1)S(1)}, bf16[2,256,512]{2,1,0:T(8,128)(2,1)S(1)}, u32[]{:S(2)}, u32[]{:S(2)}) collective-permute-start(bf16[2,256,512]{2,1,0:T(8,128)(2,1)S(1)} %pad_maximum_fusion.6.refs_3_), channel_id=1, source_target_pairs={{0,8},{1,9},{2,10},{3,11},{4,20},{5,21},{6,22},{7,23},{16,0},{17,1... | collective-permute-start | bytes 1572872 | tf_op jit(solution)/shard_map/ring-1:-1/ppermute | solution.py:33
  69.3 5.3 %shard_map.52 = (bf16[192,2,2048]{2,1,0:T(2,128)(2,1)}, bf16[192,2,2048]{2,1,0:T(2,128)(2,1)}, f32[768,512]{1,0:T(8,128)S(1)}, f32[768,512]{1,0:T(8,128)S(1)}) custom-call(bf16[192,4096]{1,0:T(8,128)(2,1)S(1)} %bitcast.6, bf16[192,4096]{1,0:T(8,128)(2,1)S(1)} %bitcast.13, ...), custom_call_target="tpu_custom_call", output_to_operand_aliasing={{0}: (10, {}), {1}: (11, {})} | custom-call | flops 4026531840 | bytes 10485760 | tf_op jit(solution)/shard_map/pallas_call | solution.py:118
  74.6 0.1 collective-permute-start.19
  74.7 0.3 collective-permute-done.17.refs_0_
  74.9 0.9 %collective-permute-done.19 = bf16[1,16,128]{2,1,0:T(8,128)(2,1)S(1)} collective-permute-done((bf16[1,16,128]{2,1,0:T(8,128)(2,1)S(1)}, bf16[1,16,128]{2,1,0:T(8,128)(2,1)S(1)}, u32[]{:S(2)}, u32[]{:S(2)}) %collective-permute-start.19) | collective-permute-done | bytes 4128 | tf_op jit(solution)/shard_map/token/ppermute | solution.py:41
  75.8 0.2 collective-permute-start.23
  76.0 0.6 shard_map.53.refs_1_
  76.6 1.8 %collective-permute-done.21.refs_1_ = bf16[2,256,512]{2,1,0:T(8,128)(2,1)S(1)} collective-permute-done((bf16[2,256,512]{2,1,0:T(8,128)(2,1)S(1)}, bf16[2,256,512]{2,1,0:T(8,128)(2,1)S(1)}, u32[]{:S(2)}, u32[]{:S(2)}) %collective-permute-start.21) | collective-permute-done | bytes 524320 | tf_op jit(solution)/shard_map/along-1:2/ppermute | solution.py:37
  78.4 0.5 collective-permute-start.22
  78.9 1.0 %shard_map.54.refs_2_ = f32[768,512]{1,0:T(8,128)S(1)} custom-call(bf16[192,4096]{1,0:T(8,128)(2,1)S(1)} %bitcast.8, bf16[192,4096]{1,0:T(8,128)(2,1)S(1)} %bitcast.15, bf16[2,256,512]{2,1,0:T(8,128)(2,1)S(1)} %collective-permute-done.16.refs_0_, bf16[2,256,512]{2,1,0:T(8,128)(2,1)S(1)} %collective-permute-done.21.refs_1_, ...), custom_call_target="tpu_custom_call" | custom-call | flops 805306368 | bytes 2097152 | tf_op jit(solution)/shard_map/pallas_call | solution.py:118
  79.9 1.6 %shard_map.55 = (bf16[192,2,2048]{2,1,0:T(2,128)(2,1)}, bf16[192,2,2048]{2,1,0:T(2,128)(2,1)}) custom-call(bf16[192,4096]{1,0:T(8,128)(2,1)S(1)} %bitcast.9, bf16[192,4096]{1,0:T(8,128)(2,1)S(1)} %bitcast.16, bf16[2,256,512]{2,1,0:T(8,128)(2,1)S(1)} %collective-permute-done.23.refs_0_, ...), custom_call_target="tpu_custom_call", output_to_operand_aliasing={{0}: (4, {}), {1}: (5, {})} | custom-call | flops 402653184 | bytes 1048576 | tf_op jit(solution)/shard_map/pallas_call | solution.py:118
  81.6 2.0 %shard_map.56 = (bf16[192,2,2048]{2,1,0:T(2,128)(2,1)}, bf16[192,2,2048]{2,1,0:T(2,128)(2,1)}) custom-call(bf16[192,4096]{1,0:T(8,128)(2,1)S(1)} %bitcast.10, bf16[192,4096]{1,0:T(8,128)(2,1)S(1)} %bitcast.17, bf16[2,256,512]{2,1,0:T(8,128)(2,1)S(1)} %collective-permute-done.20.refs_0_, ...), custom_call_target="tpu_custom_call", output_to_operand_aliasing={{0}: (5, {}), {1}: (6, {})} | custom-call | flops 805306368 | bytes 2097152 | tf_op jit(solution)/shard_map/pallas_call | solution.py:118
  (25 shorter events, 0.2 us)
Async XLA Ops:
  0.6 12.2 %collective-permute-start.1 = (bf16[2,256,512]{2,1,0:T(8,128)(2,1)}, bf16[2,256,512]{2,1,0:T(8,128)(2,1)S(1)}, u32[]{:S(2)}, u32[]{:S(2)}) collective-permute-start(bf16[2,256,512]{2,1,0:T(8,128)(2,1)} %refs_2_.1), channel_id=1, source_target_pairs={{0,16},{1,17},{2,18},{3,19},{4,12},{5,13},{6,14},{7,15},{16,24},{1... | collective-permute-start | bytes 1572872 | tf_op jit(solution)/shard_map/ring0:1/ppermute | solution.py:33
  3.6 15.5 %collective-permute-start.2 = (bf16[2,256,512]{2,1,0:T(8,128)(2,1)}, bf16[2,256,512]{2,1,0:T(8,128)(2,1)S(1)}, u32[]{:S(2)}, u32[]{:S(2)}) collective-permute-start(bf16[2,256,512]{2,1,0:T(8,128)(2,1)} %refs_2_.1), channel_id=1, source_target_pairs={{0,1},{1,2},{2,3},{3,0},{4,5},{5,6},{6,7},{7,4},{16,17},{17,18},{1... | collective-permute-start | bytes 1572872 | tf_op jit(solution)/shard_map/along1:0/ppermute | solution.py:37
  5.2 2.2 %copy-start.1 = (bf16[192,2,2048]{2,1,0:T(2,128)(2,1)S(1)}, bf16[192,2,2048]{2,1,0:T(2,128)(2,1)}, u32[]{:S(2)}) copy-start(bf16[192,2,2048]{2,1,0:T(2,128)(2,1)} %param.4) | copy-start | bytes 4718596
  7.4 1.0 %copy-start = (bf16[2,256,512]{2,1,0:T(8,128)(2,1)S(1)}, bf16[2,256,512]{2,1,0:T(8,128)(2,1)}, u32[]{:S(2)}) copy-start(bf16[2,256,512]{2,1,0:T(8,128)(2,1)} %refs_2_.1) | copy-start | bytes 1572868
  8.5 14.0 %collective-permute-start = (bf16[2,256,512]{2,1,0:T(8,128)(2,1)S(1)}, bf16[2,256,512]{2,1,0:T(8,128)(2,1)S(1)}, u32[]{:S(2)}, u32[]{:S(2)}) collective-permute-start(bf16[2,256,512]{2,1,0:T(8,128)(2,1)S(1)} %copy-done), channel_id=1, source_target_pairs={{0,8},{1,9},{2,10},{3,11},{4,20},{5,21},{6,22},{7,23},{16,0},{17,1... | collective-permute-start | bytes 1572872 | tf_op jit(solution)/shard_map/ring0:-1/ppermute | solution.py:33
  12.8 10.2 %collective-permute-start.4 = (bf16[2,256,512]{2,1,0:T(8,128)(2,1)S(1)}, bf16[2,256,512]{2,1,0:T(8,128)(2,1)S(1)}, u32[]{:S(2)}, u32[]{:S(2)}) collective-permute-start(bf16[2,256,512]{2,1,0:T(8,128)(2,1)S(1)} %collective-permute-done.1.refs_3_), channel_id=1, source_target_pairs={{0,16},{1,17},{2,18},{3,19},{4,12},{5,13},{6,14},{7,15},{16,24},{1... | collective-permute-start | bytes 1572872 | tf_op jit(solution)/shard_map/ring0:2/ppermute | solution.py:33
  15.2 14.1 %collective-permute-start.7 = (bf16[2,256,512]{2,1,0:T(8,128)(2,1)S(1)}, bf16[2,256,512]{2,1,0:T(8,128)(2,1)S(1)}, u32[]{:S(2)}, u32[]{:S(2)}) collective-permute-start(bf16[2,256,512]{2,1,0:T(8,128)(2,1)S(1)} %copy-done), channel_id=1, source_target_pairs={{0,4},{1,5},{2,6},{3,7},{4,0},{5,1},{6,2},{7,3},{16,20},{17,21},{1... | collective-permute-start | bytes 1572872 | tf_op jit(solution)/shard_map/core0:0/ppermute | solution.py:41
  19.1 20.0 %collective-permute-start.8 = (bf16[2,256,512]{2,1,0:T(8,128)(2,1)S(1)}, bf16[2,256,512]{2,1,0:T(8,128)(2,1)S(1)}, u32[]{:S(2)}, u32[]{:S(2)}) collective-permute-start(bf16[2,256,512]{2,1,0:T(8,128)(2,1)S(1)} %collective-permute-done.2.refs_0_), channel_id=1, source_target_pairs={{0,1},{1,2},{2,3},{3,0},{4,5},{5,6},{6,7},{7,4},{16,17},{17,18},{1... | collective-permute-start | bytes 1572872 | tf_op jit(solution)/shard_map/along2:0/ppermute | solution.py:37
  19.1 20.0 %collective-permute-start.5 = (bf16[2,256,512]{2,1,0:T(8,128)(2,1)S(1)}, bf16[2,256,512]{2,1,0:T(8,128)(2,1)S(1)}, u32[]{:S(2)}, u32[]{:S(2)}) collective-permute-start(bf16[2,256,512]{2,1,0:T(8,128)(2,1)S(1)} %collective-permute-done.2.refs_0_), channel_id=1, source_target_pairs={{0,16},{1,17},{2,18},{3,19},{4,12},{5,13},{6,14},{7,15},{16,24},{1... | collective-permute-start | bytes 1572872 | tf_op jit(solution)/shard_map/ring1:1/ppermute | solution.py:33
  22.4 16.7 %collective-permute-start.6 = (bf16[2,256,512]{2,1,0:T(8,128)(2,1)S(1)}, bf16[2,256,512]{2,1,0:T(8,128)(2,1)S(1)}, u32[]{:S(2)}, u32[]{:S(2)}) collective-permute-start(bf16[2,256,512]{2,1,0:T(8,128)(2,1)S(1)} %collective-permute-done.2.refs_0_), channel_id=1, source_target_pairs={{0,8},{1,9},{2,10},{3,11},{4,20},{5,21},{6,22},{7,23},{16,0},{17,1... | collective-permute-start | bytes 1572872 | tf_op jit(solution)/shard_map/ring1:-1/ppermute | solution.py:33
  23.0 16.1 %collective-permute-start.3 = (bf16[2,128,512]{2,1,0:T(8,128)(2,1)S(1)}, bf16[2,128,512]{2,1,0:T(8,128)(2,1)S(1)}, u32[]{:S(2)}, u32[]{:S(2)}) collective-permute-start(bf16[2,128,512]{2,1,0:T(8,128)(2,1)S(1)} %get-tuple-element.39), channel_id=1, source_target_pairs={{0,3},{1,0},{2,1},{3,2},{4,7},{5,4},{6,5},{7,6},{16,19},{17,16},{1... | collective-permute-start | bytes 786440 | tf_op jit(solution)/shard_map/along_upper/ppermute | solution.py:37
  39.3 4.2 %collective-permute-start.12 = (bf16[8,256,512]{2,1,0:T(8,128)(2,1)S(1)}, bf16[8,256,512]{2,1,0:T(8,128)(2,1)S(1)}, u32[]{:S(2)}, u32[]{:S(2)}) collective-permute-start(bf16[8,256,512]{2,1,0:T(8,128)(2,1)S(1)} %pad_maximum_fusion), channel_id=1, source_target_pairs={{0,4},{1,5},{2,6},{3,7},{4,0},{5,1},{6,2},{7,3},{16,20},{17,21},{1... | collective-permute-start | bytes 6291464 | tf_op jit(solution)/shard_map/core0:1_0:-1_0:2_1:0/ppermute | solution.py:41
  39.6 9.2 %collective-permute-start.13 = (bf16[6,256,512]{2,1,0:T(8,128)(2,1)S(1)}, bf16[6,256,512]{2,1,0:T(8,128)(2,1)S(1)}, u32[]{:S(2)}, u32[]{:S(2)}) collective-permute-start(bf16[6,256,512]{2,1,0:T(8,128)(2,1)S(1)} %pad_maximum_fusion.1), channel_id=1, source_target_pairs={{0,4},{1,5},{2,6},{3,7},{4,0},{5,1},{6,2},{7,3},{16,20},{17,21},{1... | collective-permute-start | bytes 4718600 | tf_op jit(solution)/shard_map/core1:1_1:-1_2:0/ppermute | solution.py:41
  40.3 21.2 %collective-permute-start.10 = (bf16[4,256,512]{2,1,0:T(8,128)(2,1)S(1)}, bf16[4,256,512]{2,1,0:T(8,128)(2,1)S(1)}, u32[]{:S(2)}, u32[]{:S(2)}) collective-permute-start(bf16[4,256,512]{2,1,0:T(8,128)(2,1)S(1)} %pad_maximum_fusion.3), channel_id=1, source_target_pairs={{0,16},{1,17},{2,18},{3,19},{4,12},{5,13},{6,14},{7,15},{16,24},{1... | collective-permute-start | bytes 3145736 | tf_op jit(solution)/shard_map/ring1:2_2:1/ppermute | solution.py:33
  41.1 20.5 %collective-permute-start.11 = (bf16[2,256,512]{2,1,0:T(8,128)(2,1)S(1)}, bf16[2,256,512]{2,1,0:T(8,128)(2,1)S(1)}, u32[]{:S(2)}, u32[]{:S(2)}) collective-permute-start(bf16[2,256,512]{2,1,0:T(8,128)(2,1)S(1)} %collective-permute-done.8.refs_3_), channel_id=1, source_target_pairs={{0,8},{1,9},{2,10},{3,11},{4,20},{5,21},{6,22},{7,23},{16,0},{17,1... | collective-permute-start | bytes 1572872 | tf_op jit(solution)/shard_map/ring2:-1/ppermute | solution.py:33
  43.2 19.2 %collective-permute-start.9 = (bf16[2,384,512]{2,1,0:T(8,128)(2,1)S(1)}, bf16[2,384,512]{2,1,0:T(8,128)(2,1)S(1)}, u32[]{:S(2)}, u32[]{:S(2)}) collective-permute-start(bf16[2,384,512]{2,1,0:T(8,128)(2,1)S(1)} %pad_maximum_fusion.5), channel_id=1, source_target_pairs={{0,3},{1,0},{2,1},{3,2},{4,7},{5,4},{6,5},{7,6},{16,19},{17,16},{1... | collective-permute-start | bytes 2359304 | tf_op jit(solution)/shard_map/along_lower/ppermute | solution.py:37
  51.5 11.0 %collective-permute-start.14 = (bf16[1,16,128]{2,1,0:T(8,128)(2,1)S(1)}, bf16[1,16,128]{2,1,0:T(8,128)(2,1)S(1)}, u32[]{:S(2)}, u32[]{:S(2)}) collective-permute-start(bf16[1,16,128]{2,1,0:T(8,128)(2,1)S(1)} %get-tuple-element.53), channel_id=1, source_target_pairs={{0,4},{1,5},{2,6},{3,7},{4,0},{5,1},{6,2},{7,3},{16,20},{17,21},{1... | collective-permute-start | bytes 12296 | tf_op jit(solution)/shard_map/token/ppermute | solution.py:41
  62.6 6.7 %collective-permute-start.18 = (bf16[6,256,512]{2,1,0:T(8,128)(2,1)S(1)}, bf16[6,256,512]{2,1,0:T(8,128)(2,1)S(1)}, u32[]{:S(2)}, u32[]{:S(2)}) collective-permute-start(bf16[6,256,512]{2,1,0:T(8,128)(2,1)S(1)} %pad_maximum_fusion.2), channel_id=1, source_target_pairs={{0,4},{1,5},{2,6},{3,7},{4,0},{5,1},{6,2},{7,3},{16,20},{17,21},{1... | collective-permute-start | bytes 4718600 | tf_op jit(solution)/shard_map/core1:2_2:1_2:-1/ppermute | solution.py:41
  62.9 4.7 %collective-permute-start.15 = (bf16[4,256,512]{2,1,0:T(8,128)(2,1)S(1)}, bf16[4,256,512]{2,1,0:T(8,128)(2,1)S(1)}, u32[]{:S(2)}, u32[]{:S(2)}) collective-permute-start(bf16[4,256,512]{2,1,0:T(8,128)(2,1)S(1)} %pad_maximum_fusion.4), channel_id=1, source_target_pairs={{0,4},{1,5},{2,6},{3,7},{4,0},{5,1},{6,2},{7,3},{16,20},{17,21},{1... | collective-permute-start | bytes 3145736 | tf_op jit(solution)/shard_map/core-1:0_-1:1/ppermute | solution.py:41
  63.5 11.4 %collective-permute-start.17 = (bf16[2,256,512]{2,1,0:T(8,128)(2,1)S(1)}, bf16[2,256,512]{2,1,0:T(8,128)(2,1)S(1)}, u32[]{:S(2)}, u32[]{:S(2)}) collective-permute-start(bf16[2,256,512]{2,1,0:T(8,128)(2,1)S(1)} %get-tuple-element.57), channel_id=1, source_target_pairs={{0,16},{1,17},{2,18},{3,19},{4,12},{5,13},{6,14},{7,15},{16,24},{1... | collective-permute-start | bytes 1572872 | tf_op jit(solution)/shard_map/ring2:2/ppermute | solution.py:33
  63.5 14.9 %collective-permute-start.21 = (bf16[2,256,512]{2,1,0:T(8,128)(2,1)S(1)}, bf16[2,256,512]{2,1,0:T(8,128)(2,1)S(1)}, u32[]{:S(2)}, u32[]{:S(2)}) collective-permute-start(bf16[2,256,512]{2,1,0:T(8,128)(2,1)S(1)} %collective-permute-done.4.refs_5_), channel_id=1, source_target_pairs={{0,3},{1,0},{2,1},{3,2},{4,7},{5,4},{6,5},{7,6},{16,19},{17,16},{1... | collective-permute-start | bytes 1572872 | tf_op jit(solution)/shard_map/along-1:2/ppermute | solution.py:37
  67.6 10.8 %collective-permute-start.16 = (bf16[2,256,512]{2,1,0:T(8,128)(2,1)S(1)}, bf16[2,256,512]{2,1,0:T(8,128)(2,1)S(1)}, u32[]{:S(2)}, u32[]{:S(2)}) collective-permute-start(bf16[2,256,512]{2,1,0:T(8,128)(2,1)S(1)} %pad_maximum_fusion.6.refs_3_), channel_id=1, source_target_pairs={{0,8},{1,9},{2,10},{3,11},{4,20},{5,21},{6,22},{7,23},{16,0},{17,1... | collective-permute-start | bytes 1572872 | tf_op jit(solution)/shard_map/ring-1:-1/ppermute | solution.py:33
  74.6 1.2 %collective-permute-start.19 = (bf16[1,16,128]{2,1,0:T(8,128)(2,1)S(1)}, bf16[1,16,128]{2,1,0:T(8,128)(2,1)S(1)}, u32[]{:S(2)}, u32[]{:S(2)}) collective-permute-start(bf16[1,16,128]{2,1,0:T(8,128)(2,1)S(1)} %get-tuple-element.64), channel_id=1, source_target_pairs={{0,4},{1,5},{2,6},{3,7},{4,0},{5,1},{6,2},{7,3},{16,20},{17,21},{1... | collective-permute-start | bytes 12296 | tf_op jit(solution)/shard_map/token/ppermute | solution.py:41
  75.8 4.1 %collective-permute-start.23 = (bf16[2,256,512]{2,1,0:T(8,128)(2,1)S(1)}, bf16[2,256,512]{2,1,0:T(8,128)(2,1)S(1)}, u32[]{:S(2)}, u32[]{:S(2)}) collective-permute-start(bf16[2,256,512]{2,1,0:T(8,128)(2,1)S(1)} %collective-permute-done.17.refs_0_), channel_id=1, source_target_pairs={{0,4},{1,5},{2,6},{3,7},{4,0},{5,1},{6,2},{7,3},{16,20},{17,21},{1... | collective-permute-start | bytes 1572872 | tf_op jit(solution)/shard_map/core2:2/ppermute | solution.py:41
  78.4 3.1 %collective-permute-start.20 = (bf16[2,256,512]{2,1,0:T(8,128)(2,1)S(1)}, bf16[2,256,512]{2,1,0:T(8,128)(2,1)S(1)}, u32[]{:S(2)}, u32[]{:S(2)}) collective-permute-start(bf16[2,256,512]{2,1,0:T(8,128)(2,1)S(1)} %collective-permute-done.16.refs_0_), channel_id=1, source_target_pairs={{0,4},{1,5},{2,6},{3,7},{4,0},{5,1},{6,2},{7,3},{16,20},{17,21},{1... | collective-permute-start | bytes 1572872 | tf_op jit(solution)/shard_map/core-1:-1/ppermute | solution.py:41
  78.4 3.1 %collective-permute-start.22 = (bf16[2,256,512]{2,1,0:T(8,128)(2,1)S(1)}, bf16[2,256,512]{2,1,0:T(8,128)(2,1)S(1)}, u32[]{:S(2)}, u32[]{:S(2)}) collective-permute-start(bf16[2,256,512]{2,1,0:T(8,128)(2,1)S(1)} %collective-permute-done.21.refs_1_), channel_id=1, source_target_pairs={{0,4},{1,5},{2,6},{3,7},{4,0},{5,1},{6,2},{7,3},{16,20},{17,21},{1... | collective-permute-start | bytes 1572872 | tf_op jit(solution)/shard_map/core-1:2/ppermute | solution.py:41

commit v7 on v6

--- a/solution.py
+++ b/solution.py
@@ -123,7 +123,7 @@
         scratch_shapes=scratch,
         input_output_aliases=aliases,
         compiler_params=pltpu.CompilerParams(vmem_limit_bytes=28 * 2**20),
-        cost_estimate=pl.CostEstimate(flops=weight * 2 * 8 * g * depth * width * count, bytes_accessed=2**20 * count, transcendentals=0),
+        cost_estimate=pl.CostEstimate(flops=weight * 2 * 8 * g * depth * width * count, bytes_accessed=max(1, min(weight, 1) * 2**20 * count), transcendentals=0),
     )(*operands)
     return (tuple(result[:2]), result[2:]) if finishing else (outs, result)
 
@@ -186,8 +186,8 @@
 
     z1 = move("along", 1, [((0, 0), (1, 0))])
     p1 = move("ring", 1, [((0, 0), (0, 1))])
-    m1 = move("ring", -1, [((0, 0), (0, -1))], *lefts)
-    e1 = swap([(0, 0)], *lefts)
+    m1 = move("ring", -1, [((0, 0), (0, -1))], p1, *lefts)
+    e1 = swap([(0, 0)], p1, *lefts)
     x2 = move("ring", 1, [((0, 1), (0, 2))], *lefts)
     gate = (p1, z1)
     z2 = move("along", 1, [((1, 0), (2, 0))], *gate)
@@ -196,12 +196,12 @@
     upper = down(ritz[:, :cut], "along_upper", m1, *gate)
     gate = (lax.slice(x2, (0, 0, 0), (1, 16, 128)), s1, m2, e1, z2, upper)
     p3 = move("ring", 1, [((1, 1), (1, 2)), ((2, 0), (2, 1))], *gate)
-    m3 = move("ring", -1, [((2, 0), (2, -1))], *gate)
     lower = down(jnp.concatenate([ritz[:, cut:], mine[0, 1][0]], 1), "along_lower", *gate)
     e3 = swap([(0, 1), (0, -1), (0, 2), (1, 0)], *gate)
     e3b = swap([(1, 1), (1, -1), (2, 0)], *gate)
-    products(both, [(0, 0), (0, 1), (0, -1), (0, 2), (1, 0)])
-    t = token(products(both, [(1, 1), (1, -1), (2, 0)]))
+    m3 = move("ring", -1, [((2, 0), (2, -1))], e3, *gate)
+    products(both, [(0, 0), (0, 1), (0, -1), (0, 2), (1, 0)], weight=0)
+    t = token(products(both, [(1, 1), (1, -1), (2, 0)], weight=0))
     mine[-1, 0] = jnp.concatenate([upper, lower[:, : ritz.shape[1] - cut]], 1), 0
     mine[-1, 1] = lower[:, ritz.shape[1] - cut :], 0
     gate = (p3, m3, e3, t)

time: 83.9 us -> 82.5 us (0.983)
  waiting for transfers between devices: 35.7 us -> 32.5 us
  starting transfers between devices: 24.5 us -> 26.6 us
    ppermute x5, waiting for transfers between devices: 16.5 us -> 14.5 us  [along(): return lax.ppermute(value, AXES, pairs)]
    ppermute x9, waiting for transfers between devices: 17.2 us -> 15.6 us  [ring(): return lax.ppermute(value, AXES, pairs)]
    ppermute x9, starting transfers between devices: 11 us -> 12.6 us  [ring(): return lax.ppermute(value, AXES, pairs)]
  transfers between devices with their start and end apart: 24 -> 24, of which waited for: 12 -> 10; matrix products, arithmetic and copies ran while one was open for 4% -> 4% of each run, Pallas kernels for 19% -> 20%
where the time goes in v7:
time: 82.5 us; the launch traced here: 82.3 us
  waiting for transfers between devices  32.5 us (39%)
  starting transfers between devices  26.6 us (32%)
  Pallas kernels  18.4 us (22%)
  local copies, waits for them, and re-layouts  2.99 us (4%)
  between operations  1.05 us (1%)
  other arithmetic  0.88 us (1%)
    pallas_call x7, Pallas kernels, run_parts(): pl.pallas_call(functools.partial(parts_kernel, plan, rows, cols, len(arra...  18.4 us
    ppermute x9, waiting for transfers between devices, ring(): return lax.ppermute(value, AXES, pairs)  15.6 us
    ppermute x5, waiting for transfers between devices, along(): return lax.ppermute(value, AXES, pairs)  14.5 us
    ppermute x9, starting transfers between devices, ring(): return lax.ppermute(value, AXES, pairs)  12.6 us
    ppermute x5, starting transfers between devices, along(): return lax.ppermute(value, AXES, pairs)  11.2 us
    unnamed x6, local copies, waits for them, and re-layouts  2.83 us
    ppermute x10, starting transfers between devices, other(): return lax.ppermute(value, AXES, pairs)  2.74 us
    ppermute x10, waiting for transfers between devices, other(): return lax.ppermute(value, AXES, pairs)  2.41 us
  transfers between devices with their start and end apart: 24, of which 10 were waited for; matrix products, arithmetic and copies ran while one was open for 4% of the time, Pallas kernels for 20%

profile of v7, /device:TPU:0, one launch (start us, length us, event | category | flops | bytes accessed | tf_op | source)
XLA Modules:
  0.0 82.3 jit_solution(7614967247680450861)
XLA Ops:
  0.6 3.0 %collective-permute-start = (bf16[2,256,512]{2,1,0:T(8,128)(2,1)}, bf16[2,256,512]{2,1,0:T(8,128)(2,1)S(1)}, u32[]{:S(2)}, u32[]{:S(2)}) collective-permute-start(bf16[2,256,512]{2,1,0:T(8,128)(2,1)} %refs_2_.1), channel_id=1, source_target_pairs={{0,16},{1,17},{2,18},{3,19},{4,12},{5,13},{6,14},{7,15},{16,24},{1... | collective-permute-start | bytes 1572872 | tf_op jit(solution)/shard_map/ring0:1/ppermute | solution.py:33
  3.6 1.6 %collective-permute-start.2 = (bf16[2,256,512]{2,1,0:T(8,128)(2,1)}, bf16[2,256,512]{2,1,0:T(8,128)(2,1)S(1)}, u32[]{:S(2)}, u32[]{:S(2)}) collective-permute-start(bf16[2,256,512]{2,1,0:T(8,128)(2,1)} %refs_2_.1), channel_id=1, source_target_pairs={{0,1},{1,2},{2,3},{3,0},{4,5},{5,6},{6,7},{7,4},{16,17},{17,18},{1... | collective-permute-start | bytes 1572872 | tf_op jit(solution)/shard_map/along1:0/ppermute | solution.py:37
  5.2 2.2 %copy.11 = bf16[24,8,2,2048]{3,1,2,0:T(8,128)(2,1)S(1)} copy(bf16[24,8,2,2048]{3,2,1,0:T(2,128)(2,1)} %bitcast.18) | data formatting | bytes 3145728
  7.4 0.6 copy.12
  8.1 2.9 %collective-permute-done.refs_3_ = bf16[2,256,512]{2,1,0:T(8,128)(2,1)S(1)} collective-permute-done((bf16[2,256,512]{2,1,0:T(8,128)(2,1)}, bf16[2,256,512]{2,1,0:T(8,128)(2,1)S(1)}, u32[]{:S(2)}, u32[]{:S(2)}) %collective-permute-start) | collective-permute-done | bytes 524320 | tf_op jit(solution)/shard_map/ring0:1/ppermute | solution.py:33
  11.0 2.0 %collective-permute-start.1 = (bf16[2,256,512]{2,1,0:T(8,128)(2,1)S(1)}, bf16[2,256,512]{2,1,0:T(8,128)(2,1)S(1)}, u32[]{:S(2)}, u32[]{:S(2)}) collective-permute-start(bf16[2,256,512]{2,1,0:T(8,128)(2,1)S(1)} %copy-done), channel_id=1, source_target_pairs={{0,8},{1,9},{2,10},{3,11},{4,20},{5,21},{6,22},{7,23},{16,0},{17,1... | collective-permute-start | bytes 1572872 | tf_op jit(solution)/shard_map/ring0:-1/ppermute | solution.py:33
  13.0 6.1 %collective-permute-done.2.refs_0_ = bf16[2,256,512]{2,1,0:T(8,128)(2,1)S(1)} collective-permute-done((bf16[2,256,512]{2,1,0:T(8,128)(2,1)}, bf16[2,256,512]{2,1,0:T(8,128)(2,1)S(1)}, u32[]{:S(2)}, u32[]{:S(2)}) %collective-permute-start.2) | collective-permute-done | bytes 524320 | tf_op jit(solution)/shard_map/along1:0/ppermute | solution.py:37
  19.1 0.5 collective-permute-start.5
  19.6 0.7 collective-permute-start.7
  20.3 5.5 %collective-permute-done.1.refs_4_ = bf16[2,256,512]{2,1,0:T(8,128)(2,1)S(1)} collective-permute-done((bf16[2,256,512]{2,1,0:T(8,128)(2,1)S(1)}, bf16[2,256,512]{2,1,0:T(8,128)(2,1)S(1)}, u32[]{:S(2)}, u32[]{:S(2)}) %collective-permute-start.1) | collective-permute-done | bytes 524320 | tf_op jit(solution)/shard_map/ring0:-1/ppermute | solution.py:33
  25.8 2.1 %collective-permute-start.6 = (bf16[2,256,512]{2,1,0:T(8,128)(2,1)S(1)}, bf16[2,256,512]{2,1,0:T(8,128)(2,1)S(1)}, u32[]{:S(2)}, u32[]{:S(2)}) collective-permute-start(bf16[2,256,512]{2,1,0:T(8,128)(2,1)S(1)} %collective-permute-done.2.refs_0_), channel_id=1, source_target_pairs={{0,8},{1,9},{2,10},{3,11},{4,20},{5,21},{6,22},{7,23},{16,0},{17,1... | collective-permute-start | bytes 1572872 | tf_op jit(solution)/shard_map/ring1:-1/ppermute | solution.py:33
  27.9 3.7 %collective-permute-start.3 = (bf16[2,128,512]{2,1,0:T(8,128)(2,1)S(1)}, bf16[2,128,512]{2,1,0:T(8,128)(2,1)S(1)}, u32[]{:S(2)}, u32[]{:S(2)}) collective-permute-start(bf16[2,128,512]{2,1,0:T(8,128)(2,1)S(1)} %get-tuple-element.40), channel_id=1, source_target_pairs={{0,3},{1,0},{2,1},{3,2},{4,7},{5,4},{6,5},{7,6},{16,19},{17,16},{1... | collective-permute-start | bytes 786440 | tf_op jit(solution)/shard_map/along_upper/ppermute | solution.py:37
  31.6 4.2 %collective-permute-done.8.refs_3_ = bf16[2,256,512]{2,1,0:T(8,128)(2,1)S(1)} collective-permute-done((bf16[2,256,512]{2,1,0:T(8,128)(2,1)S(1)}, bf16[2,256,512]{2,1,0:T(8,128)(2,1)S(1)}, u32[]{:S(2)}, u32[]{:S(2)}) %collective-permute-start.8) | collective-permute-done | bytes 524320 | tf_op jit(solution)/shard_map/along2:0/ppermute | solution.py:37
  35.8 3.2 %collective-permute-done.3 = bf16[2,128,512]{2,1,0:T(8,128)(2,1)S(1)} collective-permute-done((bf16[2,128,512]{2,1,0:T(8,128)(2,1)S(1)}, bf16[2,128,512]{2,1,0:T(8,128)(2,1)S(1)}, u32[]{:S(2)}, u32[]{:S(2)}) %collective-permute-start.3) | collective-permute-done | bytes 262176 | tf_op jit(solution)/shard_map/along_upper/ppermute | solution.py:37
  39.1 0.3 pad_maximum_fusion
  39.3 0.1 collective-permute-start.11
  39.4 0.2 pad_maximum_fusion.1
  39.6 0.6 collective-permute-start.13
  40.1 0.1 pad_maximum_fusion.3
  40.2 0.1 collective-permute-start.10
  40.3 0.1 pad_maximum_fusion.5
  40.4 2.9 %collective-permute-start.9 = (bf16[2,384,512]{2,1,0:T(8,128)(2,1)S(1)}, bf16[2,384,512]{2,1,0:T(8,128)(2,1)S(1)}, u32[]{:S(2)}, u32[]{:S(2)}) collective-permute-start(bf16[2,384,512]{2,1,0:T(8,128)(2,1)S(1)} %pad_maximum_fusion.5), channel_id=1, source_target_pairs={{0,3},{1,0},{2,1},{3,2},{4,7},{5,4},{6,5},{7,6},{16,19},{17,16},{1... | collective-permute-start | bytes 2359304 | tf_op jit(solution)/shard_map/along_lower/ppermute | solution.py:37
  43.2 0.3 collective-permute-done.11.refs_1_
  43.6 2.8 %collective-permute-start.12 = (bf16[2,256,512]{2,1,0:T(8,128)(2,1)S(1)}, bf16[2,256,512]{2,1,0:T(8,128)(2,1)S(1)}, u32[]{:S(2)}, u32[]{:S(2)}) collective-permute-start(bf16[2,256,512]{2,1,0:T(8,128)(2,1)S(1)} %collective-permute-done.8.refs_3_), channel_id=1, source_target_pairs={{0,8},{1,9},{2,10},{3,11},{4,20},{5,21},{6,22},{7,23},{16,0},{17,1... | collective-permute-start | bytes 1572872 | tf_op jit(solution)/shard_map/ring2:-1/ppermute | solution.py:33
  46.3 5.2 %shard_map.50 = (bf16[192,2,2048]{2,1,0:T(2,128)(2,1)}, bf16[192,2,2048]{2,1,0:T(2,128)(2,1)}, f32[768,512]{1,0:T(8,128)S(1)}) custom-call(bf16[192,4096]{1,0:T(8,128)(2,1)S(1)} %bitcast.4, bf16[192,4096]{1,0:T(8,128)(2,1)S(1)} %bitcast.11, bf16[2,256,512]{2,1,0:T(8,128)(2,1)S(1)} %collective-permute-done.2.refs_0_, ...), custom_call_target="tpu_custom_call" | custom-call | bytes 1 | tf_op jit(solution)/shard_map/pallas_call | solution.py:118
  51.6 2.6 %shard_map.51 = (f32[768,512]{1,0:T(8,128)S(1)}, f32[768,512]{1,0:T(8,128)S(1)}) custom-call(bf16[192,4096]{1,0:T(8,128)(2,1)S(1)} %bitcast.5, bf16[192,4096]{1,0:T(8,128)(2,1)S(1)} %bitcast.12, bf16[2,256,512]{2,1,0:T(8,128)(2,1)S(1)} %collective-permute-done.5.refs_0_, bf16[2,256,512]{2,1,0:T(8,128)(2,1)S(1)} %collective-permute-done.6.refs_1_, ...), custom_call_target="tpu_custom_call" | custom-call | bytes 1 | tf_op jit(solution)/shard_map/pallas_call | solution.py:118
  54.2 0.1 collective-permute-start.14
  54.3 7.2 %collective-permute-done.10.refs_0_ = bf16[4,256,512]{2,1,0:T(8,128)(2,1)S(1)} collective-permute-done((bf16[4,256,512]{2,1,0:T(8,128)(2,1)S(1)}, bf16[4,256,512]{2,1,0:T(8,128)(2,1)S(1)}, u32[]{:S(2)}, u32[]{:S(2)}) %collective-permute-start.10) | collective-permute-done | bytes 1048608 | tf_op jit(solution)/shard_map/ring1:2_2:1/ppermute | solution.py:33
  61.5 0.1 fusion
  61.6 0.2 pad_maximum_fusion.2
  61.7 0.1 collective-permute-start.18
  61.9 0.1 pad_maximum_fusion.4
  62.0 0.6 collective-permute-start.15
  62.6 0.1 collective-permute-start.17
  62.6 3.1 %collective-permute-start.21 = (bf16[2,256,512]{2,1,0:T(8,128)(2,1)S(1)}, bf16[2,256,512]{2,1,0:T(8,128)(2,1)S(1)}, u32[]{:S(2)}, u32[]{:S(2)}) collective-permute-start(bf16[2,256,512]{2,1,0:T(8,128)(2,1)S(1)} %collective-permute-done.4.refs_5_), channel_id=1, source_target_pairs={{0,3},{1,0},{2,1},{3,2},{4,7},{5,4},{6,5},{7,6},{16,19},{17,16},{1... | collective-permute-start | bytes 1572872 | tf_op jit(solution)/shard_map/along-1:2/ppermute | solution.py:37
  65.8 0.9 %collective-permute-done.15.refs_5_ = bf16[4,256,512]{2,1,0:T(8,128)(2,1)S(1)} collective-permute-done((bf16[4,256,512]{2,1,0:T(8,128)(2,1)S(1)}, bf16[4,256,512]{2,1,0:T(8,128)(2,1)S(1)}, u32[]{:S(2)}, u32[]{:S(2)}) %collective-permute-start.15) | collective-permute-done | bytes 1048608 | tf_op jit(solution)/shard_map/core-1:0_-1:1/ppermute | solution.py:41
  66.7 2.0 %collective-permute-start.16 = (bf16[2,256,512]{2,1,0:T(8,128)(2,1)S(1)}, bf16[2,256,512]{2,1,0:T(8,128)(2,1)S(1)}, u32[]{:S(2)}, u32[]{:S(2)}) collective-permute-start(bf16[2,256,512]{2,1,0:T(8,128)(2,1)S(1)} %pad_maximum_fusion.6.refs_3_), channel_id=1, source_target_pairs={{0,8},{1,9},{2,10},{3,11},{4,20},{5,21},{6,22},{7,23},{16,0},{17,1... | collective-permute-start | bytes 1572872 | tf_op jit(solution)/shard_map/ring-1:-1/ppermute | solution.py:33
  68.7 5.3 %shard_map.52 = (bf16[192,2,2048]{2,1,0:T(2,128)(2,1)}, bf16[192,2,2048]{2,1,0:T(2,128)(2,1)}, f32[768,512]{1,0:T(8,128)S(1)}, f32[768,512]{1,0:T(8,128)S(1)}) custom-call(bf16[192,4096]{1,0:T(8,128)(2,1)S(1)} %bitcast.6, bf16[192,4096]{1,0:T(8,128)(2,1)S(1)} %bitcast.13, ...), custom_call_target="tpu_custom_call", output_to_operand_aliasing={{0}: (10, {}), {1}: (11, {})} | custom-call | flops 4026531840 | bytes 10485760 | tf_op jit(solution)/shard_map/pallas_call | solution.py:118
  74.0 0.1 collective-permute-start.19
  74.1 1.1 %collective-permute-done.19 = bf16[1,16,128]{2,1,0:T(8,128)(2,1)S(1)} collective-permute-done((bf16[1,16,128]{2,1,0:T(8,128)(2,1)S(1)}, bf16[1,16,128]{2,1,0:T(8,128)(2,1)S(1)}, u32[]{:S(2)}, u32[]{:S(2)}) %collective-permute-start.19) | collective-permute-done | bytes 4128 | tf_op jit(solution)/shard_map/token/ppermute | solution.py:41
  75.3 0.2 collective-permute-start.23
  75.4 0.6 shard_map.53.refs_1_
  76.0 0.9 %collective-permute-done.21.refs_1_ = bf16[2,256,512]{2,1,0:T(8,128)(2,1)S(1)} collective-permute-done((bf16[2,256,512]{2,1,0:T(8,128)(2,1)S(1)}, bf16[2,256,512]{2,1,0:T(8,128)(2,1)S(1)}, u32[]{:S(2)}, u32[]{:S(2)}) %collective-permute-start.21) | collective-permute-done | bytes 524320 | tf_op jit(solution)/shard_map/along-1:2/ppermute | solution.py:37
  77.0 0.3 collective-permute-start.20
  77.3 0.2 collective-permute-start.22
  77.5 1.0 %shard_map.54.refs_2_ = f32[768,512]{1,0:T(8,128)S(1)} custom-call(bf16[192,4096]{1,0:T(8,128)(2,1)S(1)} %bitcast.8, bf16[192,4096]{1,0:T(8,128)(2,1)S(1)} %bitcast.15, bf16[2,256,512]{2,1,0:T(8,128)(2,1)S(1)} %collective-permute-done.16.refs_0_, bf16[2,256,512]{2,1,0:T(8,128)(2,1)S(1)} %collective-permute-done.21.refs_1_, ...), custom_call_target="tpu_custom_call" | custom-call | flops 805306368 | bytes 2097152 | tf_op jit(solution)/shard_map/pallas_call | solution.py:118
  78.5 1.6 %shard_map.55 = (bf16[192,2,2048]{2,1,0:T(2,128)(2,1)}, bf16[192,2,2048]{2,1,0:T(2,128)(2,1)}) custom-call(bf16[192,4096]{1,0:T(8,128)(2,1)S(1)} %bitcast.9, bf16[192,4096]{1,0:T(8,128)(2,1)S(1)} %bitcast.16, bf16[2,256,512]{2,1,0:T(8,128)(2,1)S(1)} %collective-permute-done.23.refs_0_, ...), custom_call_target="tpu_custom_call", output_to_operand_aliasing={{0}: (4, {}), {1}: (5, {})} | custom-call | flops 402653184 | bytes 1048576 | tf_op jit(solution)/shard_map/pallas_call | solution.py:118
  80.1 2.0 %shard_map.56 = (bf16[192,2,2048]{2,1,0:T(2,128)(2,1)}, bf16[192,2,2048]{2,1,0:T(2,128)(2,1)}) custom-call(bf16[192,4096]{1,0:T(8,128)(2,1)S(1)} %bitcast.10, bf16[192,4096]{1,0:T(8,128)(2,1)S(1)} %bitcast.17, bf16[2,256,512]{2,1,0:T(8,128)(2,1)S(1)} %collective-permute-done.20.refs_0_, ...), custom_call_target="tpu_custom_call", output_to_operand_aliasing={{0}: (5, {}), {1}: (6, {})} | custom-call | flops 805306368 | bytes 2097152 | tf_op jit(solution)/shard_map/pallas_call | solution.py:118
  (25 shorter events, 0.2 us)
Async XLA Ops:
  0.6 10.4 %collective-permute-start = (bf16[2,256,512]{2,1,0:T(8,128)(2,1)}, bf16[2,256,512]{2,1,0:T(8,128)(2,1)S(1)}, u32[]{:S(2)}, u32[]{:S(2)}) collective-permute-start(bf16[2,256,512]{2,1,0:T(8,128)(2,1)} %refs_2_.1), channel_id=1, source_target_pairs={{0,16},{1,17},{2,18},{3,19},{4,12},{5,13},{6,14},{7,15},{16,24},{1... | collective-permute-start | bytes 1572872 | tf_op jit(solution)/shard_map/ring0:1/ppermute | solution.py:33
  3.6 15.5 %collective-permute-start.2 = (bf16[2,256,512]{2,1,0:T(8,128)(2,1)}, bf16[2,256,512]{2,1,0:T(8,128)(2,1)S(1)}, u32[]{:S(2)}, u32[]{:S(2)}) collective-permute-start(bf16[2,256,512]{2,1,0:T(8,128)(2,1)} %refs_2_.1), channel_id=1, source_target_pairs={{0,1},{1,2},{2,3},{3,0},{4,5},{5,6},{6,7},{7,4},{16,17},{17,18},{1... | collective-permute-start | bytes 1572872 | tf_op jit(solution)/shard_map/along1:0/ppermute | solution.py:37
  5.2 2.2 %copy-start.1 = (bf16[192,2,2048]{2,1,0:T(2,128)(2,1)S(1)}, bf16[192,2,2048]{2,1,0:T(2,128)(2,1)}, u32[]{:S(2)}) copy-start(bf16[192,2,2048]{2,1,0:T(2,128)(2,1)} %param.4) | copy-start | bytes 4718596
  7.4 3.6 %copy-start = (bf16[2,256,512]{2,1,0:T(8,128)(2,1)S(1)}, bf16[2,256,512]{2,1,0:T(8,128)(2,1)}, u32[]{:S(2)}) copy-start(bf16[2,256,512]{2,1,0:T(8,128)(2,1)} %refs_2_.1) | copy-start | bytes 1572868
  11.0 14.8 %collective-permute-start.1 = (bf16[2,256,512]{2,1,0:T(8,128)(2,1)S(1)}, bf16[2,256,512]{2,1,0:T(8,128)(2,1)S(1)}, u32[]{:S(2)}, u32[]{:S(2)}) collective-permute-start(bf16[2,256,512]{2,1,0:T(8,128)(2,1)S(1)} %copy-done), channel_id=1, source_target_pairs={{0,8},{1,9},{2,10},{3,11},{4,20},{5,21},{6,22},{7,23},{16,0},{17,1... | collective-permute-start | bytes 1572872 | tf_op jit(solution)/shard_map/ring0:-1/ppermute | solution.py:33
  13.0 14.9 %collective-permute-start.4 = (bf16[2,256,512]{2,1,0:T(8,128)(2,1)S(1)}, bf16[2,256,512]{2,1,0:T(8,128)(2,1)S(1)}, u32[]{:S(2)}, u32[]{:S(2)}) collective-permute-start(bf16[2,256,512]{2,1,0:T(8,128)(2,1)S(1)} %collective-permute-done.refs_3_), channel_id=1, source_target_pairs={{0,16},{1,17},{2,18},{3,19},{4,12},{5,13},{6,14},{7,15},{16,24},{1... | collective-permute-start | bytes 1572872 | tf_op jit(solution)/shard_map/ring0:2/ppermute | solution.py:33
  19.1 16.7 %collective-permute-start.8 = (bf16[2,256,512]{2,1,0:T(8,128)(2,1)S(1)}, bf16[2,256,512]{2,1,0:T(8,128)(2,1)S(1)}, u32[]{:S(2)}, u32[]{:S(2)}) collective-permute-start(bf16[2,256,512]{2,1,0:T(8,128)(2,1)S(1)} %collective-permute-done.2.refs_0_), channel_id=1, source_target_pairs={{0,1},{1,2},{2,3},{3,0},{4,5},{5,6},{6,7},{7,4},{16,17},{17,18},{1... | collective-permute-start | bytes 1572872 | tf_op jit(solution)/shard_map/along2:0/ppermute | solution.py:37
  19.1 16.7 %collective-permute-start.5 = (bf16[2,256,512]{2,1,0:T(8,128)(2,1)S(1)}, bf16[2,256,512]{2,1,0:T(8,128)(2,1)S(1)}, u32[]{:S(2)}, u32[]{:S(2)}) collective-permute-start(bf16[2,256,512]{2,1,0:T(8,128)(2,1)S(1)} %collective-permute-done.2.refs_0_), channel_id=1, source_target_pairs={{0,16},{1,17},{2,18},{3,19},{4,12},{5,13},{6,14},{7,15},{16,24},{1... | collective-permute-start | bytes 1572872 | tf_op jit(solution)/shard_map/ring1:1/ppermute | solution.py:33
  19.6 16.2 %collective-permute-start.7 = (bf16[2,256,512]{2,1,0:T(8,128)(2,1)S(1)}, bf16[2,256,512]{2,1,0:T(8,128)(2,1)S(1)}, u32[]{:S(2)}, u32[]{:S(2)}) collective-permute-start(bf16[2,256,512]{2,1,0:T(8,128)(2,1)S(1)} %copy-done), channel_id=1, source_target_pairs={{0,4},{1,5},{2,6},{3,7},{4,0},{5,1},{6,2},{7,3},{16,20},{17,21},{1... | collective-permute-start | bytes 1572872 | tf_op jit(solution)/shard_map/core0:0/ppermute | solution.py:41
  25.8 13.2 %collective-permute-start.6 = (bf16[2,256,512]{2,1,0:T(8,128)(2,1)S(1)}, bf16[2,256,512]{2,1,0:T(8,128)(2,1)S(1)}, u32[]{:S(2)}, u32[]{:S(2)}) collective-permute-start(bf16[2,256,512]{2,1,0:T(8,128)(2,1)S(1)} %collective-permute-done.2.refs_0_), channel_id=1, source_target_pairs={{0,8},{1,9},{2,10},{3,11},{4,20},{5,21},{6,22},{7,23},{16,0},{17,1... | collective-permute-start | bytes 1572872 | tf_op jit(solution)/shard_map/ring1:-1/ppermute | solution.py:33
  27.9 11.1 %collective-permute-start.3 = (bf16[2,128,512]{2,1,0:T(8,128)(2,1)S(1)}, bf16[2,128,512]{2,1,0:T(8,128)(2,1)S(1)}, u32[]{:S(2)}, u32[]{:S(2)}) collective-permute-start(bf16[2,128,512]{2,1,0:T(8,128)(2,1)S(1)} %get-tuple-element.40), channel_id=1, source_target_pairs={{0,3},{1,0},{2,1},{3,2},{4,7},{5,4},{6,5},{7,6},{16,19},{17,16},{1... | collective-permute-start | bytes 786440 | tf_op jit(solution)/shard_map/along_upper/ppermute | solution.py:37
  39.3 4.2 %collective-permute-start.11 = (bf16[8,256,512]{2,1,0:T(8,128)(2,1)S(1)}, bf16[8,256,512]{2,1,0:T(8,128)(2,1)S(1)}, u32[]{:S(2)}, u32[]{:S(2)}) collective-permute-start(bf16[8,256,512]{2,1,0:T(8,128)(2,1)S(1)} %pad_maximum_fusion), channel_id=1, source_target_pairs={{0,4},{1,5},{2,6},{3,7},{4,0},{5,1},{6,2},{7,3},{16,20},{17,21},{1... | collective-permute-start | bytes 6291464 | tf_op jit(solution)/shard_map/core0:1_0:-1_0:2_1:0/ppermute | solution.py:41
  39.6 12.0 %collective-permute-start.13 = (bf16[6,256,512]{2,1,0:T(8,128)(2,1)S(1)}, bf16[6,256,512]{2,1,0:T(8,128)(2,1)S(1)}, u32[]{:S(2)}, u32[]{:S(2)}) collective-permute-start(bf16[6,256,512]{2,1,0:T(8,128)(2,1)S(1)} %pad_maximum_fusion.1), channel_id=1, source_target_pairs={{0,4},{1,5},{2,6},{3,7},{4,0},{5,1},{6,2},{7,3},{16,20},{17,21},{1... | collective-permute-start | bytes 4718600 | tf_op jit(solution)/shard_map/core1:1_1:-1_2:0/ppermute | solution.py:41
  40.2 21.2 %collective-permute-start.10 = (bf16[4,256,512]{2,1,0:T(8,128)(2,1)S(1)}, bf16[4,256,512]{2,1,0:T(8,128)(2,1)S(1)}, u32[]{:S(2)}, u32[]{:S(2)}) collective-permute-start(bf16[4,256,512]{2,1,0:T(8,128)(2,1)S(1)} %pad_maximum_fusion.3), channel_id=1, source_target_pairs={{0,16},{1,17},{2,18},{3,19},{4,12},{5,13},{6,14},{7,15},{16,24},{1... | collective-permute-start | bytes 3145736 | tf_op jit(solution)/shard_map/ring1:2_2:1/ppermute | solution.py:33
  40.4 21.2 %collective-permute-start.9 = (bf16[2,384,512]{2,1,0:T(8,128)(2,1)S(1)}, bf16[2,384,512]{2,1,0:T(8,128)(2,1)S(1)}, u32[]{:S(2)}, u32[]{:S(2)}) collective-permute-start(bf16[2,384,512]{2,1,0:T(8,128)(2,1)S(1)} %pad_maximum_fusion.5), channel_id=1, source_target_pairs={{0,3},{1,0},{2,1},{3,2},{4,7},{5,4},{6,5},{7,6},{16,19},{17,16},{1... | collective-permute-start | bytes 2359304 | tf_op jit(solution)/shard_map/along_lower/ppermute | solution.py:37
  43.6 18.0 %collective-permute-start.12 = (bf16[2,256,512]{2,1,0:T(8,128)(2,1)S(1)}, bf16[2,256,512]{2,1,0:T(8,128)(2,1)S(1)}, u32[]{:S(2)}, u32[]{:S(2)}) collective-permute-start(bf16[2,256,512]{2,1,0:T(8,128)(2,1)S(1)} %collective-permute-done.8.refs_3_), channel_id=1, source_target_pairs={{0,8},{1,9},{2,10},{3,11},{4,20},{5,21},{6,22},{7,23},{16,0},{17,1... | collective-permute-start | bytes 1572872 | tf_op jit(solution)/shard_map/ring2:-1/ppermute | solution.py:33
  54.2 7.3 %collective-permute-start.14 = (bf16[1,16,128]{2,1,0:T(8,128)(2,1)S(1)}, bf16[1,16,128]{2,1,0:T(8,128)(2,1)S(1)}, u32[]{:S(2)}, u32[]{:S(2)}) collective-permute-start(bf16[1,16,128]{2,1,0:T(8,128)(2,1)S(1)} %get-tuple-element.55), channel_id=1, source_target_pairs={{0,4},{1,5},{2,6},{3,7},{4,0},{5,1},{6,2},{7,3},{16,20},{17,21},{1... | collective-permute-start | bytes 12296 | tf_op jit(solution)/shard_map/token/ppermute | solution.py:41
  61.7 7.0 %collective-permute-start.18 = (bf16[6,256,512]{2,1,0:T(8,128)(2,1)S(1)}, bf16[6,256,512]{2,1,0:T(8,128)(2,1)S(1)}, u32[]{:S(2)}, u32[]{:S(2)}) collective-permute-start(bf16[6,256,512]{2,1,0:T(8,128)(2,1)S(1)} %pad_maximum_fusion.2), channel_id=1, source_target_pairs={{0,4},{1,5},{2,6},{3,7},{4,0},{5,1},{6,2},{7,3},{16,20},{17,21},{1... | collective-permute-start | bytes 4718600 | tf_op jit(solution)/shard_map/core1:2_2:1_2:-1/ppermute | solution.py:41
  62.0 4.7 %collective-permute-start.15 = (bf16[4,256,512]{2,1,0:T(8,128)(2,1)S(1)}, bf16[4,256,512]{2,1,0:T(8,128)(2,1)S(1)}, u32[]{:S(2)}, u32[]{:S(2)}) collective-permute-start(bf16[4,256,512]{2,1,0:T(8,128)(2,1)S(1)} %pad_maximum_fusion.4), channel_id=1, source_target_pairs={{0,4},{1,5},{2,6},{3,7},{4,0},{5,1},{6,2},{7,3},{16,20},{17,21},{1... | collective-permute-start | bytes 3145736 | tf_op jit(solution)/shard_map/core-1:0_-1:1/ppermute | solution.py:41
  62.6 11.5 %collective-permute-start.17 = (bf16[2,256,512]{2,1,0:T(8,128)(2,1)S(1)}, bf16[2,256,512]{2,1,0:T(8,128)(2,1)S(1)}, u32[]{:S(2)}, u32[]{:S(2)}) collective-permute-start(bf16[2,256,512]{2,1,0:T(8,128)(2,1)S(1)} %get-tuple-element.59), channel_id=1, source_target_pairs={{0,16},{1,17},{2,18},{3,19},{4,12},{5,13},{6,14},{7,15},{16,24},{1... | collective-permute-start | bytes 1572872 | tf_op jit(solution)/shard_map/ring2:2/ppermute | solution.py:33
  62.6 14.3 %collective-permute-start.21 = (bf16[2,256,512]{2,1,0:T(8,128)(2,1)S(1)}, bf16[2,256,512]{2,1,0:T(8,128)(2,1)S(1)}, u32[]{:S(2)}, u32[]{:S(2)}) collective-permute-start(bf16[2,256,512]{2,1,0:T(8,128)(2,1)S(1)} %collective-permute-done.4.refs_5_), channel_id=1, source_target_pairs={{0,3},{1,0},{2,1},{3,2},{4,7},{5,4},{6,5},{7,6},{16,19},{17,16},{1... | collective-permute-start | bytes 1572872 | tf_op jit(solution)/shard_map/along-1:2/ppermute | solution.py:37
  66.7 10.2 %collective-permute-start.16 = (bf16[2,256,512]{2,1,0:T(8,128)(2,1)S(1)}, bf16[2,256,512]{2,1,0:T(8,128)(2,1)S(1)}, u32[]{:S(2)}, u32[]{:S(2)}) collective-permute-start(bf16[2,256,512]{2,1,0:T(8,128)(2,1)S(1)} %pad_maximum_fusion.6.refs_3_), channel_id=1, source_target_pairs={{0,8},{1,9},{2,10},{3,11},{4,20},{5,21},{6,22},{7,23},{16,0},{17,1... | collective-permute-start | bytes 1572872 | tf_op jit(solution)/shard_map/ring-1:-1/ppermute | solution.py:33
  74.0 1.2 %collective-permute-start.19 = (bf16[1,16,128]{2,1,0:T(8,128)(2,1)S(1)}, bf16[1,16,128]{2,1,0:T(8,128)(2,1)S(1)}, u32[]{:S(2)}, u32[]{:S(2)}) collective-permute-start(bf16[1,16,128]{2,1,0:T(8,128)(2,1)S(1)} %get-tuple-element.66), channel_id=1, source_target_pairs={{0,4},{1,5},{2,6},{3,7},{4,0},{5,1},{6,2},{7,3},{16,20},{17,21},{1... | collective-permute-start | bytes 12296 | tf_op jit(solution)/shard_map/token/ppermute | solution.py:41
  75.3 3.2 %collective-permute-start.23 = (bf16[2,256,512]{2,1,0:T(8,128)(2,1)S(1)}, bf16[2,256,512]{2,1,0:T(8,128)(2,1)S(1)}, u32[]{:S(2)}, u32[]{:S(2)}) collective-permute-start(bf16[2,256,512]{2,1,0:T(8,128)(2,1)S(1)} %collective-permute-done.17.refs_0_), channel_id=1, source_target_pairs={{0,4},{1,5},{2,6},{3,7},{4,0},{5,1},{6,2},{7,3},{16,20},{17,21},{1... | collective-permute-start | bytes 1572872 | tf_op jit(solution)/shard_map/core2:2/ppermute | solution.py:41
  77.0 3.1 %collective-permute-start.20 = (bf16[2,256,512]{2,1,0:T(8,128)(2,1)S(1)}, bf16[2,256,512]{2,1,0:T(8,128)(2,1)S(1)}, u32[]{:S(2)}, u32[]{:S(2)}) collective-permute-start(bf16[2,256,512]{2,1,0:T(8,128)(2,1)S(1)} %collective-permute-done.16.refs_0_), channel_id=1, source_target_pairs={{0,4},{1,5},{2,6},{3,7},{4,0},{5,1},{6,2},{7,3},{16,20},{17,21},{1... | collective-permute-start | bytes 1572872 | tf_op jit(solution)/shard_map/core-1:-1/ppermute | solution.py:41
  77.3 2.8 %collective-permute-start.22 = (bf16[2,256,512]{2,1,0:T(8,128)(2,1)S(1)}, bf16[2,256,512]{2,1,0:T(8,128)(2,1)S(1)}, u32[]{:S(2)}, u32[]{:S(2)}) collective-permute-start(bf16[2,256,512]{2,1,0:T(8,128)(2,1)S(1)} %collective-permute-done.21.refs_1_), channel_id=1, source_target_pairs={{0,4},{1,5},{2,6},{3,7},{4,0},{5,1},{6,2},{7,3},{16,20},{17,21},{1... | collective-permute-start | bytes 1572872 | tf_op jit(solution)/shard_map/core-1:2/ppermute | solution.py:41

commit v8 on v7

--- a/solution.py
+++ b/solution.py
@@ -186,9 +186,9 @@
 
     z1 = move("along", 1, [((0, 0), (1, 0))])
     p1 = move("ring", 1, [((0, 0), (0, 1))])
-    m1 = move("ring", -1, [((0, 0), (0, -1))], p1, *lefts)
+    m1 = move("ring", -1, [((0, 0), (0, -1))], *lefts)
     e1 = swap([(0, 0)], p1, *lefts)
-    x2 = move("ring", 1, [((0, 1), (0, 2))], *lefts)
+    x2 = move("ring", 1, [((0, 1), (0, 2))])
     gate = (p1, z1)
     z2 = move("along", 1, [((1, 0), (2, 0))], *gate)
     s1 = move("ring", 1, [((1, 0), (1, 1))], *gate)
@@ -211,7 +211,7 @@
     e4 = swap([(1, 2), (2, 1), (2, -1)], *gate)
     e4b = swap([(-1, 0), (-1, 1)], *gate)
     m4 = move("ring", -1, [((-1, 0), (-1, -1))], e4b, *gate)
-    t = token(products(both, [(1, 2), (2, 1), (2, -1), (-1, 0), (-1, 1)]))
+    t = products(both, [(1, 2), (2, 1), (2, -1), (-1, 0), (-1, 1)])
     swap([(2, 2)], t, e4)
     first = products([mine], [(2, 2)])
     swap([(-1, -1)], first, t)

time: 82.5 us -> 82.5 us (level)
  starting transfers between devices: 26.6 us -> 25 us
  waiting for transfers between devices: 32.5 us -> 33.7 us
    ppermute x5, waiting for transfers between devices: 14.5 us -> 16 us  [along(): return lax.ppermute(value, AXES, pairs)]
    ppermute x9, waiting for transfers between devices: 15.6 us -> 14.3 us  [ring(): return lax.ppermute(value, AXES, pairs)]
    ppermute x9, starting transfers between devices: 12.6 us -> 11.3 us  [ring(): return lax.ppermute(value, AXES, pairs)]
    ppermute x10 -> x9, waiting for transfers between devices: 2.41 us -> 3.39 us  [other(): return lax.ppermute(value, AXES, pairs)]
    ppermute x10 -> x9, starting transfers between devices: 2.74 us -> 1.92 us  [other(): return lax.ppermute(value, AXES, pairs)]
  transfers between devices with their start and end apart: 24 -> 23, of which waited for: 10 -> 9; matrix products, arithmetic and copies ran while one was open for 4% -> 4% of each run, Pallas kernels for 20% -> 20%
where the time goes in v8:
time: 82.5 us; the launch traced here: 82.3 us
  waiting for transfers between devices  33.7 us (41%)
  starting transfers between devices  25 us (30%)
  Pallas kernels  18.4 us (22%)
  local copies, waits for them, and re-layouts  3.37 us (4%)
  between operations  1.05 us (1%)
  other arithmetic  0.88 us (1%)
    pallas_call x7, Pallas kernels, run_parts(): pl.pallas_call(functools.partial(parts_kernel, plan, rows, cols, len(arra...  18.4 us
    ppermute x5, waiting for transfers between devices, along(): return lax.ppermute(value, AXES, pairs)  16 us
    ppermute x9, waiting for transfers between devices, ring(): return lax.ppermute(value, AXES, pairs)  14.3 us
    ppermute x5, starting transfers between devices, along(): return lax.ppermute(value, AXES, pairs)  11.7 us
    ppermute x9, starting transfers between devices, ring(): return lax.ppermute(value, AXES, pairs)  11.3 us
    ppermute x9, waiting for transfers between devices, other(): return lax.ppermute(value, AXES, pairs)  3.39 us
    unnamed x6, local copies, waits for them, and re-layouts  3.21 us
    ppermute x9, starting transfers between devices, other(): return lax.ppermute(value, AXES, pairs)  1.92 us
  transfers between devices with their start and end apart: 23, of which 9 were waited for; matrix products, arithmetic and copies ran while one was open for 4% of the time, Pallas kernels for 20%

profile of v8, /device:TPU:0, one launch (start us, length us, event | category | flops | bytes accessed | tf_op | source)
XLA Modules:
  0.0 82.3 jit_solution(8823534466185456333)
XLA Ops:
  0.6 3.0 %collective-permute-start.1 = (bf16[2,256,512]{2,1,0:T(8,128)(2,1)}, bf16[2,256,512]{2,1,0:T(8,128)(2,1)S(1)}, u32[]{:S(2)}, u32[]{:S(2)}) collective-permute-start(bf16[2,256,512]{2,1,0:T(8,128)(2,1)} %refs_2_.1), channel_id=1, source_target_pairs={{0,16},{1,17},{2,18},{3,19},{4,12},{5,13},{6,14},{7,15},{16,24},{1... | collective-permute-start | bytes 1572872 | tf_op jit(solution)/shard_map/ring0:1/ppermute | solution.py:33
  3.6 1.6 %collective-permute-start.2 = (bf16[2,256,512]{2,1,0:T(8,128)(2,1)}, bf16[2,256,512]{2,1,0:T(8,128)(2,1)S(1)}, u32[]{:S(2)}, u32[]{:S(2)}) collective-permute-start(bf16[2,256,512]{2,1,0:T(8,128)(2,1)} %refs_2_.1), channel_id=1, source_target_pairs={{0,1},{1,2},{2,3},{3,0},{4,5},{5,6},{6,7},{7,4},{16,17},{17,18},{1... | collective-permute-start | bytes 1572872 | tf_op jit(solution)/shard_map/along1:0/ppermute | solution.py:37
  5.2 2.2 %copy.11 = bf16[24,8,2,2048]{3,1,2,0:T(8,128)(2,1)S(1)} copy(bf16[24,8,2,2048]{3,2,1,0:T(2,128)(2,1)} %bitcast.18) | data formatting | bytes 3145728
  7.4 0.0 copy-start
  7.4 0.6 copy.12
  8.1 0.4 copy-done
  8.5 0.5 collective-permute-start
  9.0 3.8 %collective-permute-done.1.refs_3_ = bf16[2,256,512]{2,1,0:T(8,128)(2,1)S(1)} collective-permute-done((bf16[2,256,512]{2,1,0:T(8,128)(2,1)}, bf16[2,256,512]{2,1,0:T(8,128)(2,1)S(1)}, u32[]{:S(2)}, u32[]{:S(2)}) %collective-permute-start.1) | collective-permute-done | bytes 524320 | tf_op jit(solution)/shard_map/ring0:1/ppermute | solution.py:33
  12.8 2.4 %collective-permute-start.4 = (bf16[2,256,512]{2,1,0:T(8,128)(2,1)S(1)}, bf16[2,256,512]{2,1,0:T(8,128)(2,1)S(1)}, u32[]{:S(2)}, u32[]{:S(2)}) collective-permute-start(bf16[2,256,512]{2,1,0:T(8,128)(2,1)S(1)} %collective-permute-done.1.refs_3_), channel_id=1, source_target_pairs={{0,16},{1,17},{2,18},{3,19},{4,12},{5,13},{6,14},{7,15},{16,24},{1... | collective-permute-start | bytes 1572872 | tf_op jit(solution)/shard_map/ring0:2/ppermute | solution.py:33
  15.2 3.9 %collective-permute-done.2.refs_0_ = bf16[2,256,512]{2,1,0:T(8,128)(2,1)S(1)} collective-permute-done((bf16[2,256,512]{2,1,0:T(8,128)(2,1)}, bf16[2,256,512]{2,1,0:T(8,128)(2,1)S(1)}, u32[]{:S(2)}, u32[]{:S(2)}) %collective-permute-start.2) | collective-permute-done | bytes 524320 | tf_op jit(solution)/shard_map/along1:0/ppermute | solution.py:37
  19.1 0.0 collective-permute-start.8
  19.1 0.5 collective-permute-start.5
  19.6 2.8 %collective-permute-done.refs_4_ = bf16[2,256,512]{2,1,0:T(8,128)(2,1)S(1)} collective-permute-done((bf16[2,256,512]{2,1,0:T(8,128)(2,1)S(1)}, bf16[2,256,512]{2,1,0:T(8,128)(2,1)S(1)}, u32[]{:S(2)}, u32[]{:S(2)}) %collective-permute-start) | collective-permute-done | bytes 524320 | tf_op jit(solution)/shard_map/ring0:-1/ppermute | solution.py:33
  22.5 0.5 collective-permute-done.4.refs_5_
  23.0 6.3 %collective-permute-start.3 = (bf16[2,128,512]{2,1,0:T(8,128)(2,1)S(1)}, bf16[2,128,512]{2,1,0:T(8,128)(2,1)S(1)}, u32[]{:S(2)}, u32[]{:S(2)}) collective-permute-start(bf16[2,128,512]{2,1,0:T(8,128)(2,1)S(1)} %get-tuple-element.39), channel_id=1, source_target_pairs={{0,3},{1,0},{2,1},{3,2},{4,7},{5,4},{6,5},{7,6},{16,19},{17,16},{1... | collective-permute-start | bytes 786440 | tf_op jit(solution)/shard_map/along_upper/ppermute | solution.py:37
  29.2 9.8 %collective-permute-done.3 = bf16[2,128,512]{2,1,0:T(8,128)(2,1)S(1)} collective-permute-done((bf16[2,128,512]{2,1,0:T(8,128)(2,1)S(1)}, bf16[2,128,512]{2,1,0:T(8,128)(2,1)S(1)}, u32[]{:S(2)}, u32[]{:S(2)}) %collective-permute-start.3) | collective-permute-done | bytes 262176 | tf_op jit(solution)/shard_map/along_upper/ppermute | solution.py:37
  39.1 0.3 pad_maximum_fusion
  39.4 0.1 collective-permute-start.11
  39.5 0.2 pad_maximum_fusion.1
  39.6 0.5 collective-permute-start.13
  40.2 0.1 pad_maximum_fusion.3
  40.3 0.1 collective-permute-start.10
  40.3 0.1 pad_maximum_fusion.5
  40.4 1.6 %collective-permute-start.9 = (bf16[2,384,512]{2,1,0:T(8,128)(2,1)S(1)}, bf16[2,384,512]{2,1,0:T(8,128)(2,1)S(1)}, u32[]{:S(2)}, u32[]{:S(2)}) collective-permute-start(bf16[2,384,512]{2,1,0:T(8,128)(2,1)S(1)} %pad_maximum_fusion.5), channel_id=1, source_target_pairs={{0,3},{1,0},{2,1},{3,2},{4,7},{5,4},{6,5},{7,6},{16,19},{17,16},{1... | collective-permute-start | bytes 2359304 | tf_op jit(solution)/shard_map/along_lower/ppermute | solution.py:37
  42.0 1.6 %collective-permute-done.11.refs_1_ = bf16[8,256,512]{2,1,0:T(8,128)(2,1)S(1)} collective-permute-done((bf16[8,256,512]{2,1,0:T(8,128)(2,1)S(1)}, bf16[8,256,512]{2,1,0:T(8,128)(2,1)S(1)}, u32[]{:S(2)}, u32[]{:S(2)}) %collective-permute-start.11) | collective-permute-done | bytes 2097184 | tf_op jit(solution)/shard_map/core0:1_0:-1_0:2_1:0/ppermute | solution.py:41
  43.6 2.8 %collective-permute-start.12 = (bf16[2,256,512]{2,1,0:T(8,128)(2,1)S(1)}, bf16[2,256,512]{2,1,0:T(8,128)(2,1)S(1)}, u32[]{:S(2)}, u32[]{:S(2)}) collective-permute-start(bf16[2,256,512]{2,1,0:T(8,128)(2,1)S(1)} %collective-permute-done.8.refs_3_), channel_id=1, source_target_pairs={{0,8},{1,9},{2,10},{3,11},{4,20},{5,21},{6,22},{7,23},{16,0},{17,1... | collective-permute-start | bytes 1572872 | tf_op jit(solution)/shard_map/ring2:-1/ppermute | solution.py:33
  46.4 5.2 %shard_map.50 = (bf16[192,2,2048]{2,1,0:T(2,128)(2,1)}, bf16[192,2,2048]{2,1,0:T(2,128)(2,1)}, f32[768,512]{1,0:T(8,128)S(1)}) custom-call(bf16[192,4096]{1,0:T(8,128)(2,1)S(1)} %bitcast.4, bf16[192,4096]{1,0:T(8,128)(2,1)S(1)} %bitcast.11, bf16[2,256,512]{2,1,0:T(8,128)(2,1)S(1)} %collective-permute-done.2.refs_0_, ...), custom_call_target="tpu_custom_call" | custom-call | bytes 1 | tf_op jit(solution)/shard_map/pallas_call | solution.py:118
  51.6 2.6 %shard_map.51 = (f32[768,512]{1,0:T(8,128)S(1)}, f32[768,512]{1,0:T(8,128)S(1)}) custom-call(bf16[192,4096]{1,0:T(8,128)(2,1)S(1)} %bitcast.5, bf16[192,4096]{1,0:T(8,128)(2,1)S(1)} %bitcast.12, bf16[2,256,512]{2,1,0:T(8,128)(2,1)S(1)} %collective-permute-done.5.refs_0_, bf16[2,256,512]{2,1,0:T(8,128)(2,1)S(1)} %collective-permute-done.6.refs_1_, ...), custom_call_target="tpu_custom_call" | custom-call | bytes 1 | tf_op jit(solution)/shard_map/pallas_call | solution.py:118
  54.2 0.1 collective-permute-start.14
  54.3 7.2 %collective-permute-done.10.refs_0_ = bf16[4,256,512]{2,1,0:T(8,128)(2,1)S(1)} collective-permute-done((bf16[4,256,512]{2,1,0:T(8,128)(2,1)S(1)}, bf16[4,256,512]{2,1,0:T(8,128)(2,1)S(1)}, u32[]{:S(2)}, u32[]{:S(2)}) %collective-permute-start.10) | collective-permute-done | bytes 1048608 | tf_op jit(solution)/shard_map/ring1:2_2:1/ppermute | solution.py:33
  61.5 0.1 fusion
  61.6 0.2 pad_maximum_fusion.2
  61.8 0.1 collective-permute-start.18
  62.0 0.1 pad_maximum_fusion.4
  62.1 0.6 collective-permute-start.15
  62.6 0.1 collective-permute-start.17
  62.7 2.3 %collective-permute-start.20 = (bf16[2,256,512]{2,1,0:T(8,128)(2,1)S(1)}, bf16[2,256,512]{2,1,0:T(8,128)(2,1)S(1)}, u32[]{:S(2)}, u32[]{:S(2)}) collective-permute-start(bf16[2,256,512]{2,1,0:T(8,128)(2,1)S(1)} %collective-permute-done.4.refs_5_), channel_id=1, source_target_pairs={{0,3},{1,0},{2,1},{3,2},{4,7},{5,4},{6,5},{7,6},{16,19},{17,16},{1... | collective-permute-start | bytes 1572872 | tf_op jit(solution)/shard_map/along-1:2/ppermute | solution.py:37
  65.0 1.8 %collective-permute-done.15.refs_5_ = bf16[4,256,512]{2,1,0:T(8,128)(2,1)S(1)} collective-permute-done((bf16[4,256,512]{2,1,0:T(8,128)(2,1)S(1)}, bf16[4,256,512]{2,1,0:T(8,128)(2,1)S(1)}, u32[]{:S(2)}, u32[]{:S(2)}) %collective-permute-start.15) | collective-permute-done | bytes 1048608 | tf_op jit(solution)/shard_map/core-1:0_-1:1/ppermute | solution.py:41
  66.7 2.0 %collective-permute-start.16 = (bf16[2,256,512]{2,1,0:T(8,128)(2,1)S(1)}, bf16[2,256,512]{2,1,0:T(8,128)(2,1)S(1)}, u32[]{:S(2)}, u32[]{:S(2)}) collective-permute-start(bf16[2,256,512]{2,1,0:T(8,128)(2,1)S(1)} %pad_maximum_fusion.6.refs_3_), channel_id=1, source_target_pairs={{0,8},{1,9},{2,10},{3,11},{4,20},{5,21},{6,22},{7,23},{16,0},{17,1... | collective-permute-start | bytes 1572872 | tf_op jit(solution)/shard_map/ring-1:-1/ppermute | solution.py:33
  68.8 5.3 %shard_map.52 = (bf16[192,2,2048]{2,1,0:T(2,128)(2,1)}, bf16[192,2,2048]{2,1,0:T(2,128)(2,1)}, f32[768,512]{1,0:T(8,128)S(1)}, f32[768,512]{1,0:T(8,128)S(1)}) custom-call(bf16[192,4096]{1,0:T(8,128)(2,1)S(1)} %bitcast.6, bf16[192,4096]{1,0:T(8,128)(2,1)S(1)} %bitcast.13, ...), custom_call_target="tpu_custom_call", output_to_operand_aliasing={{0}: (10, {}), {1}: (11, {})} | custom-call | flops 4026531840 | bytes 10485760 | tf_op jit(solution)/shard_map/pallas_call | solution.py:118
  74.1 0.1 collective-permute-start.22
  74.2 0.6 shard_map.53.refs_1_
  74.7 2.2 %collective-permute-done.20.refs_1_ = bf16[2,256,512]{2,1,0:T(8,128)(2,1)S(1)} collective-permute-done((bf16[2,256,512]{2,1,0:T(8,128)(2,1)S(1)}, bf16[2,256,512]{2,1,0:T(8,128)(2,1)S(1)}, u32[]{:S(2)}, u32[]{:S(2)}) %collective-permute-start.20) | collective-permute-done | bytes 524320 | tf_op jit(solution)/shard_map/along-1:2/ppermute | solution.py:37
  77.0 0.5 collective-permute-start.19
  77.4 0.1 collective-permute-start.21
  77.5 1.0 %shard_map.54.refs_2_ = f32[768,512]{1,0:T(8,128)S(1)} custom-call(bf16[192,4096]{1,0:T(8,128)(2,1)S(1)} %bitcast.8, bf16[192,4096]{1,0:T(8,128)(2,1)S(1)} %bitcast.15, bf16[2,256,512]{2,1,0:T(8,128)(2,1)S(1)} %collective-permute-done.16.refs_0_, bf16[2,256,512]{2,1,0:T(8,128)(2,1)S(1)} %collective-permute-done.20.refs_1_, ...), custom_call_target="tpu_custom_call" | custom-call | flops 805306368 | bytes 2097152 | tf_op jit(solution)/shard_map/pallas_call | solution.py:118
  78.5 1.6 %shard_map.55 = (bf16[192,2,2048]{2,1,0:T(2,128)(2,1)}, bf16[192,2,2048]{2,1,0:T(2,128)(2,1)}) custom-call(bf16[192,4096]{1,0:T(8,128)(2,1)S(1)} %bitcast.9, bf16[192,4096]{1,0:T(8,128)(2,1)S(1)} %bitcast.16, bf16[2,256,512]{2,1,0:T(8,128)(2,1)S(1)} %collective-permute-done.22.refs_0_, ...), custom_call_target="tpu_custom_call", output_to_operand_aliasing={{0}: (4, {}), {1}: (5, {})} | custom-call | flops 402653184 | bytes 1048576 | tf_op jit(solution)/shard_map/pallas_call | solution.py:118
  80.1 2.0 %shard_map.56 = (bf16[192,2,2048]{2,1,0:T(2,128)(2,1)}, bf16[192,2,2048]{2,1,0:T(2,128)(2,1)}) custom-call(bf16[192,4096]{1,0:T(8,128)(2,1)S(1)} %bitcast.10, bf16[192,4096]{1,0:T(8,128)(2,1)S(1)} %bitcast.17, bf16[2,256,512]{2,1,0:T(8,128)(2,1)S(1)} %collective-permute-done.19.refs_0_, ...), custom_call_target="tpu_custom_call", output_to_operand_aliasing={{0}: (5, {}), {1}: (6, {})} | custom-call | flops 805306368 | bytes 2097152 | tf_op jit(solution)/shard_map/pallas_call | solution.py:118
  (23 shorter events, 0.2 us)
Async XLA Ops:
  0.6 12.2 %collective-permute-start.1 = (bf16[2,256,512]{2,1,0:T(8,128)(2,1)}, bf16[2,256,512]{2,1,0:T(8,128)(2,1)S(1)}, u32[]{:S(2)}, u32[]{:S(2)}) collective-permute-start(bf16[2,256,512]{2,1,0:T(8,128)(2,1)} %refs_2_.1), channel_id=1, source_target_pairs={{0,16},{1,17},{2,18},{3,19},{4,12},{5,13},{6,14},{7,15},{16,24},{1... | collective-permute-start | bytes 1572872 | tf_op jit(solution)/shard_map/ring0:1/ppermute | solution.py:33
  3.6 15.5 %collective-permute-start.2 = (bf16[2,256,512]{2,1,0:T(8,128)(2,1)}, bf16[2,256,512]{2,1,0:T(8,128)(2,1)S(1)}, u32[]{:S(2)}, u32[]{:S(2)}) collective-permute-start(bf16[2,256,512]{2,1,0:T(8,128)(2,1)} %refs_2_.1), channel_id=1, source_target_pairs={{0,1},{1,2},{2,3},{3,0},{4,5},{5,6},{6,7},{7,4},{16,17},{17,18},{1... | collective-permute-start | bytes 1572872 | tf_op jit(solution)/shard_map/along1:0/ppermute | solution.py:37
  5.2 2.2 %copy-start.1 = (bf16[192,2,2048]{2,1,0:T(2,128)(2,1)S(1)}, bf16[192,2,2048]{2,1,0:T(2,128)(2,1)}, u32[]{:S(2)}) copy-start(bf16[192,2,2048]{2,1,0:T(2,128)(2,1)} %param.4) | copy-start | bytes 4718596
  7.4 1.0 %copy-start = (bf16[2,256,512]{2,1,0:T(8,128)(2,1)S(1)}, bf16[2,256,512]{2,1,0:T(8,128)(2,1)}, u32[]{:S(2)}) copy-start(bf16[2,256,512]{2,1,0:T(8,128)(2,1)} %refs_2_.1) | copy-start | bytes 1572868
  8.5 14.0 %collective-permute-start = (bf16[2,256,512]{2,1,0:T(8,128)(2,1)S(1)}, bf16[2,256,512]{2,1,0:T(8,128)(2,1)S(1)}, u32[]{:S(2)}, u32[]{:S(2)}) collective-permute-start(bf16[2,256,512]{2,1,0:T(8,128)(2,1)S(1)} %copy-done), channel_id=1, source_target_pairs={{0,8},{1,9},{2,10},{3,11},{4,20},{5,21},{6,22},{7,23},{16,0},{17,1... | collective-permute-start | bytes 1572872 | tf_op jit(solution)/shard_map/ring0:-1/ppermute | solution.py:33
  12.8 10.2 %collective-permute-start.4 = (bf16[2,256,512]{2,1,0:T(8,128)(2,1)S(1)}, bf16[2,256,512]{2,1,0:T(8,128)(2,1)S(1)}, u32[]{:S(2)}, u32[]{:S(2)}) collective-permute-start(bf16[2,256,512]{2,1,0:T(8,128)(2,1)S(1)} %collective-permute-done.1.refs_3_), channel_id=1, source_target_pairs={{0,16},{1,17},{2,18},{3,19},{4,12},{5,13},{6,14},{7,15},{16,24},{1... | collective-permute-start | bytes 1572872 | tf_op jit(solution)/shard_map/ring0:2/ppermute | solution.py:33
  19.1 20.0 %collective-permute-start.8 = (bf16[2,256,512]{2,1,0:T(8,128)(2,1)S(1)}, bf16[2,256,512]{2,1,0:T(8,128)(2,1)S(1)}, u32[]{:S(2)}, u32[]{:S(2)}) collective-permute-start(bf16[2,256,512]{2,1,0:T(8,128)(2,1)S(1)} %collective-permute-done.2.refs_0_), channel_id=1, source_target_pairs={{0,1},{1,2},{2,3},{3,0},{4,5},{5,6},{6,7},{7,4},{16,17},{17,18},{1... | collective-permute-start | bytes 1572872 | tf_op jit(solution)/shard_map/along2:0/ppermute | solution.py:37
  19.1 20.0 %collective-permute-start.5 = (bf16[2,256,512]{2,1,0:T(8,128)(2,1)S(1)}, bf16[2,256,512]{2,1,0:T(8,128)(2,1)S(1)}, u32[]{:S(2)}, u32[]{:S(2)}) collective-permute-start(bf16[2,256,512]{2,1,0:T(8,128)(2,1)S(1)} %collective-permute-done.2.refs_0_), channel_id=1, source_target_pairs={{0,16},{1,17},{2,18},{3,19},{4,12},{5,13},{6,14},{7,15},{16,24},{1... | collective-permute-start | bytes 1572872 | tf_op jit(solution)/shard_map/ring1:1/ppermute | solution.py:33
  22.4 16.7 %collective-permute-start.6 = (bf16[2,256,512]{2,1,0:T(8,128)(2,1)S(1)}, bf16[2,256,512]{2,1,0:T(8,128)(2,1)S(1)}, u32[]{:S(2)}, u32[]{:S(2)}) collective-permute-start(bf16[2,256,512]{2,1,0:T(8,128)(2,1)S(1)} %collective-permute-done.2.refs_0_), channel_id=1, source_target_pairs={{0,8},{1,9},{2,10},{3,11},{4,20},{5,21},{6,22},{7,23},{16,0},{17,1... | collective-permute-start | bytes 1572872 | tf_op jit(solution)/shard_map/ring1:-1/ppermute | solution.py:33
  22.4 16.7 %collective-permute-start.7 = (bf16[2,256,512]{2,1,0:T(8,128)(2,1)S(1)}, bf16[2,256,512]{2,1,0:T(8,128)(2,1)S(1)}, u32[]{:S(2)}, u32[]{:S(2)}) collective-permute-start(bf16[2,256,512]{2,1,0:T(8,128)(2,1)S(1)} %copy-done), channel_id=1, source_target_pairs={{0,4},{1,5},{2,6},{3,7},{4,0},{5,1},{6,2},{7,3},{16,20},{17,21},{1... | collective-permute-start | bytes 1572872 | tf_op jit(solution)/shard_map/core0:0/ppermute | solution.py:41
  23.0 16.1 %collective-permute-start.3 = (bf16[2,128,512]{2,1,0:T(8,128)(2,1)S(1)}, bf16[2,128,512]{2,1,0:T(8,128)(2,1)S(1)}, u32[]{:S(2)}, u32[]{:S(2)}) collective-permute-start(bf16[2,128,512]{2,1,0:T(8,128)(2,1)S(1)} %get-tuple-element.39), channel_id=1, source_target_pairs={{0,3},{1,0},{2,1},{3,2},{4,7},{5,4},{6,5},{7,6},{16,19},{17,16},{1... | collective-permute-start | bytes 786440 | tf_op jit(solution)/shard_map/along_upper/ppermute | solution.py:37
  39.4 4.2 %collective-permute-start.11 = (bf16[8,256,512]{2,1,0:T(8,128)(2,1)S(1)}, bf16[8,256,512]{2,1,0:T(8,128)(2,1)S(1)}, u32[]{:S(2)}, u32[]{:S(2)}) collective-permute-start(bf16[8,256,512]{2,1,0:T(8,128)(2,1)S(1)} %pad_maximum_fusion), channel_id=1, source_target_pairs={{0,4},{1,5},{2,6},{3,7},{4,0},{5,1},{6,2},{7,3},{16,20},{17,21},{1... | collective-permute-start | bytes 6291464 | tf_op jit(solution)/shard_map/core0:1_0:-1_0:2_1:0/ppermute | solution.py:41
  39.6 12.0 %collective-permute-start.13 = (bf16[6,256,512]{2,1,0:T(8,128)(2,1)S(1)}, bf16[6,256,512]{2,1,0:T(8,128)(2,1)S(1)}, u32[]{:S(2)}, u32[]{:S(2)}) collective-permute-start(bf16[6,256,512]{2,1,0:T(8,128)(2,1)S(1)} %pad_maximum_fusion.1), channel_id=1, source_target_pairs={{0,4},{1,5},{2,6},{3,7},{4,0},{5,1},{6,2},{7,3},{16,20},{17,21},{1... | collective-permute-start | bytes 4718600 | tf_op jit(solution)/shard_map/core1:1_1:-1_2:0/ppermute | solution.py:41
  40.3 21.2 %collective-permute-start.10 = (bf16[4,256,512]{2,1,0:T(8,128)(2,1)S(1)}, bf16[4,256,512]{2,1,0:T(8,128)(2,1)S(1)}, u32[]{:S(2)}, u32[]{:S(2)}) collective-permute-start(bf16[4,256,512]{2,1,0:T(8,128)(2,1)S(1)} %pad_maximum_fusion.3), channel_id=1, source_target_pairs={{0,16},{1,17},{2,18},{3,19},{4,12},{5,13},{6,14},{7,15},{16,24},{1... | collective-permute-start | bytes 3145736 | tf_op jit(solution)/shard_map/ring1:2_2:1/ppermute | solution.py:33
  40.4 21.2 %collective-permute-start.9 = (bf16[2,384,512]{2,1,0:T(8,128)(2,1)S(1)}, bf16[2,384,512]{2,1,0:T(8,128)(2,1)S(1)}, u32[]{:S(2)}, u32[]{:S(2)}) collective-permute-start(bf16[2,384,512]{2,1,0:T(8,128)(2,1)S(1)} %pad_maximum_fusion.5), channel_id=1, source_target_pairs={{0,3},{1,0},{2,1},{3,2},{4,7},{5,4},{6,5},{7,6},{16,19},{17,16},{1... | collective-permute-start | bytes 2359304 | tf_op jit(solution)/shard_map/along_lower/ppermute | solution.py:37
  43.6 18.0 %collective-permute-start.12 = (bf16[2,256,512]{2,1,0:T(8,128)(2,1)S(1)}, bf16[2,256,512]{2,1,0:T(8,128)(2,1)S(1)}, u32[]{:S(2)}, u32[]{:S(2)}) collective-permute-start(bf16[2,256,512]{2,1,0:T(8,128)(2,1)S(1)} %collective-permute-done.8.refs_3_), channel_id=1, source_target_pairs={{0,8},{1,9},{2,10},{3,11},{4,20},{5,21},{6,22},{7,23},{16,0},{17,1... | collective-permute-start | bytes 1572872 | tf_op jit(solution)/shard_map/ring2:-1/ppermute | solution.py:33
  54.2 7.3 %collective-permute-start.14 = (bf16[1,16,128]{2,1,0:T(8,128)(2,1)S(1)}, bf16[1,16,128]{2,1,0:T(8,128)(2,1)S(1)}, u32[]{:S(2)}, u32[]{:S(2)}) collective-permute-start(bf16[1,16,128]{2,1,0:T(8,128)(2,1)S(1)} %slice.29), channel_id=1, source_target_pairs={{0,4},{1,5},{2,6},{3,7},{4,0},{5,1},{6,2},{7,3},{16,20},{17,21},{1... | collective-permute-start | bytes 12296 | tf_op jit(solution)/shard_map/token/ppermute | solution.py:41
  61.8 7.0 %collective-permute-start.18 = (bf16[6,256,512]{2,1,0:T(8,128)(2,1)S(1)}, bf16[6,256,512]{2,1,0:T(8,128)(2,1)S(1)}, u32[]{:S(2)}, u32[]{:S(2)}) collective-permute-start(bf16[6,256,512]{2,1,0:T(8,128)(2,1)S(1)} %pad_maximum_fusion.2), channel_id=1, source_target_pairs={{0,4},{1,5},{2,6},{3,7},{4,0},{5,1},{6,2},{7,3},{16,20},{17,21},{1... | collective-permute-start | bytes 4718600 | tf_op jit(solution)/shard_map/core1:2_2:1_2:-1/ppermute | solution.py:41
  62.1 4.7 %collective-permute-start.15 = (bf16[4,256,512]{2,1,0:T(8,128)(2,1)S(1)}, bf16[4,256,512]{2,1,0:T(8,128)(2,1)S(1)}, u32[]{:S(2)}, u32[]{:S(2)}) collective-permute-start(bf16[4,256,512]{2,1,0:T(8,128)(2,1)S(1)} %pad_maximum_fusion.4), channel_id=1, source_target_pairs={{0,4},{1,5},{2,6},{3,7},{4,0},{5,1},{6,2},{7,3},{16,20},{17,21},{1... | collective-permute-start | bytes 3145736 | tf_op jit(solution)/shard_map/core-1:0_-1:1/ppermute | solution.py:41
  62.6 11.4 %collective-permute-start.17 = (bf16[2,256,512]{2,1,0:T(8,128)(2,1)S(1)}, bf16[2,256,512]{2,1,0:T(8,128)(2,1)S(1)}, u32[]{:S(2)}, u32[]{:S(2)}) collective-permute-start(bf16[2,256,512]{2,1,0:T(8,128)(2,1)S(1)} %get-tuple-element.58), channel_id=1, source_target_pairs={{0,16},{1,17},{2,18},{3,19},{4,12},{5,13},{6,14},{7,15},{16,24},{1... | collective-permute-start | bytes 1572872 | tf_op jit(solution)/shard_map/ring2:2/ppermute | solution.py:33
  62.7 14.3 %collective-permute-start.20 = (bf16[2,256,512]{2,1,0:T(8,128)(2,1)S(1)}, bf16[2,256,512]{2,1,0:T(8,128)(2,1)S(1)}, u32[]{:S(2)}, u32[]{:S(2)}) collective-permute-start(bf16[2,256,512]{2,1,0:T(8,128)(2,1)S(1)} %collective-permute-done.4.refs_5_), channel_id=1, source_target_pairs={{0,3},{1,0},{2,1},{3,2},{4,7},{5,4},{6,5},{7,6},{16,19},{17,16},{1... | collective-permute-start | bytes 1572872 | tf_op jit(solution)/shard_map/along-1:2/ppermute | solution.py:37
  66.7 10.2 %collective-permute-start.16 = (bf16[2,256,512]{2,1,0:T(8,128)(2,1)S(1)}, bf16[2,256,512]{2,1,0:T(8,128)(2,1)S(1)}, u32[]{:S(2)}, u32[]{:S(2)}) collective-permute-start(bf16[2,256,512]{2,1,0:T(8,128)(2,1)S(1)} %pad_maximum_fusion.6.refs_3_), channel_id=1, source_target_pairs={{0,8},{1,9},{2,10},{3,11},{4,20},{5,21},{6,22},{7,23},{16,0},{17,1... | collective-permute-start | bytes 1572872 | tf_op jit(solution)/shard_map/ring-1:-1/ppermute | solution.py:33
  74.1 4.4 %collective-permute-start.22 = (bf16[2,256,512]{2,1,0:T(8,128)(2,1)S(1)}, bf16[2,256,512]{2,1,0:T(8,128)(2,1)S(1)}, u32[]{:S(2)}, u32[]{:S(2)}) collective-permute-start(bf16[2,256,512]{2,1,0:T(8,128)(2,1)S(1)} %collective-permute-done.17.refs_0_), channel_id=1, source_target_pairs={{0,4},{1,5},{2,6},{3,7},{4,0},{5,1},{6,2},{7,3},{16,20},{17,21},{1... | collective-permute-start | bytes 1572872 | tf_op jit(solution)/shard_map/core2:2/ppermute | solution.py:41
  77.0 3.1 %collective-permute-start.19 = (bf16[2,256,512]{2,1,0:T(8,128)(2,1)S(1)}, bf16[2,256,512]{2,1,0:T(8,128)(2,1)S(1)}, u32[]{:S(2)}, u32[]{:S(2)}) collective-permute-start(bf16[2,256,512]{2,1,0:T(8,128)(2,1)S(1)} %collective-permute-done.16.refs_0_), channel_id=1, source_target_pairs={{0,4},{1,5},{2,6},{3,7},{4,0},{5,1},{6,2},{7,3},{16,20},{17,21},{1... | collective-permute-start | bytes 1572872 | tf_op jit(solution)/shard_map/core-1:-1/ppermute | solution.py:41
  77.4 2.7 %collective-permute-start.21 = (bf16[2,256,512]{2,1,0:T(8,128)(2,1)S(1)}, bf16[2,256,512]{2,1,0:T(8,128)(2,1)S(1)}, u32[]{:S(2)}, u32[]{:S(2)}) collective-permute-start(bf16[2,256,512]{2,1,0:T(8,128)(2,1)S(1)} %collective-permute-done.20.refs_1_), channel_id=1, source_target_pairs={{0,4},{1,5},{2,6},{3,7},{4,0},{5,1},{6,2},{7,3},{16,20},{17,21},{1... | collective-permute-start | bytes 1572872 | tf_op jit(solution)/shard_map/core-1:2/ppermute | solution.py:41

commit v9 on v7

--- a/solution.py
+++ b/solution.py
@@ -200,8 +200,7 @@
     e3 = swap([(0, 1), (0, -1), (0, 2), (1, 0)], *gate)
     e3b = swap([(1, 1), (1, -1), (2, 0)], *gate)
     m3 = move("ring", -1, [((2, 0), (2, -1))], e3, *gate)
-    products(both, [(0, 0), (0, 1), (0, -1), (0, 2), (1, 0)], weight=0)
-    t = token(products(both, [(1, 1), (1, -1), (2, 0)], weight=0))
+    t = token(products(both, [(0, 0), (0, 1), (0, -1), (0, 2), (1, 0), (1, 1), (1, -1), (2, 0)], weight=0))
     mine[-1, 0] = jnp.concatenate([upper, lower[:, : ritz.shape[1] - cut]], 1), 0
     mine[-1, 1] = lower[:, ritz.shape[1] - cut :], 0
     gate = (p3, m3, e3, t)

time: 82.5 us -> 82.5 us (level)
    pallas_call x7 -> x6, Pallas kernels: 18.4 us -> 18.2 us  [run_parts(): pl.pallas_call(functools.partial(parts_kernel, plan, rows, cols, len(arra...]
where the time goes in v9:
time: 82.5 us; the launch traced here: 82.3 us
  waiting for transfers between devices  32.7 us (40%)
  starting transfers between devices  26.6 us (32%)
  Pallas kernels  18.2 us (22%)
  local copies, waits for them, and re-layouts  2.99 us (4%)
  between operations  1.04 us (1%)
  other arithmetic  0.88 us (1%)
    pallas_call x6, Pallas kernels, run_parts(): pl.pallas_call(functools.partial(parts_kernel, plan, rows, cols, len(arra...  18.2 us
    ppermute x9, waiting for transfers between devices, ring(): return lax.ppermute(value, AXES, pairs)  15.8 us
    ppermute x5, waiting for transfers between devices, along(): return lax.ppermute(value, AXES, pairs)  14.5 us
    ppermute x9, starting transfers between devices, ring(): return lax.ppermute(value, AXES, pairs)  12.6 us
    ppermute x5, starting transfers between devices, along(): return lax.ppermute(value, AXES, pairs)  11.2 us
    unnamed x6, local copies, waits for them, and re-layouts  2.83 us
    ppermute x10, starting transfers between devices, other(): return lax.ppermute(value, AXES, pairs)  2.74 us
    ppermute x10, waiting for transfers between devices, other(): return lax.ppermute(value, AXES, pairs)  2.41 us
  transfers between devices with their start and end apart: 24, of which 10 were waited for; matrix products, arithmetic and copies ran while one was open for 4% of the time, Pallas kernels for 20%

profile of v9, /device:TPU:0, one launch (start us, length us, event | category | flops | bytes accessed | tf_op | source)
XLA Modules:
  0.0 82.3 jit_solution(8742029831071003013)
XLA Ops:
  0.6 3.0 %collective-permute-start = (bf16[2,256,512]{2,1,0:T(8,128)(2,1)}, bf16[2,256,512]{2,1,0:T(8,128)(2,1)S(1)}, u32[]{:S(2)}, u32[]{:S(2)}) collective-permute-start(bf16[2,256,512]{2,1,0:T(8,128)(2,1)} %refs_6_.1), channel_id=1, source_target_pairs={{0,16},{1,17},{2,18},{3,19},{4,12},{5,13},{6,14},{7,15},{16,24},{1... | collective-permute-start | bytes 1572872 | tf_op jit(solution)/shard_map/ring0:1/ppermute | solution.py:33
  3.6 1.6 %collective-permute-start.2 = (bf16[2,256,512]{2,1,0:T(8,128)(2,1)}, bf16[2,256,512]{2,1,0:T(8,128)(2,1)S(1)}, u32[]{:S(2)}, u32[]{:S(2)}) collective-permute-start(bf16[2,256,512]{2,1,0:T(8,128)(2,1)} %refs_6_.1), channel_id=1, source_target_pairs={{0,1},{1,2},{2,3},{3,0},{4,5},{5,6},{6,7},{7,4},{16,17},{17,18},{1... | collective-permute-start | bytes 1572872 | tf_op jit(solution)/shard_map/along1:0/ppermute | solution.py:37
  5.2 2.2 %copy.11 = bf16[24,8,2,2048]{3,1,2,0:T(8,128)(2,1)S(1)} copy(bf16[24,8,2,2048]{3,2,1,0:T(2,128)(2,1)} %bitcast.16) | data formatting | bytes 3145728
  7.4 0.6 copy.12
  8.1 2.9 %collective-permute-done.refs_7_ = bf16[2,256,512]{2,1,0:T(8,128)(2,1)S(1)} collective-permute-done((bf16[2,256,512]{2,1,0:T(8,128)(2,1)}, bf16[2,256,512]{2,1,0:T(8,128)(2,1)S(1)}, u32[]{:S(2)}, u32[]{:S(2)}) %collective-permute-start) | collective-permute-done | bytes 524320 | tf_op jit(solution)/shard_map/ring0:1/ppermute | solution.py:33
  11.0 2.0 %collective-permute-start.1 = (bf16[2,256,512]{2,1,0:T(8,128)(2,1)S(1)}, bf16[2,256,512]{2,1,0:T(8,128)(2,1)S(1)}, u32[]{:S(2)}, u32[]{:S(2)}) collective-permute-start(bf16[2,256,512]{2,1,0:T(8,128)(2,1)S(1)} %copy-done), channel_id=1, source_target_pairs={{0,8},{1,9},{2,10},{3,11},{4,20},{5,21},{6,22},{7,23},{16,0},{17,1... | collective-permute-start | bytes 1572872 | tf_op jit(solution)/shard_map/ring0:-1/ppermute | solution.py:33
  13.0 0.0 collective-permute-start.4
  13.0 6.1 %collective-permute-done.2.refs_0_ = bf16[2,256,512]{2,1,0:T(8,128)(2,1)S(1)} collective-permute-done((bf16[2,256,512]{2,1,0:T(8,128)(2,1)}, bf16[2,256,512]{2,1,0:T(8,128)(2,1)S(1)}, u32[]{:S(2)}, u32[]{:S(2)}) %collective-permute-start.2) | collective-permute-done | bytes 524320 | tf_op jit(solution)/shard_map/along1:0/ppermute | solution.py:37
  19.1 0.5 collective-permute-start.5
  19.6 0.7 collective-permute-start.7
  20.3 5.5 %collective-permute-done.1.refs_8_ = bf16[2,256,512]{2,1,0:T(8,128)(2,1)S(1)} collective-permute-done((bf16[2,256,512]{2,1,0:T(8,128)(2,1)S(1)}, bf16[2,256,512]{2,1,0:T(8,128)(2,1)S(1)}, u32[]{:S(2)}, u32[]{:S(2)}) %collective-permute-start.1) | collective-permute-done | bytes 524320 | tf_op jit(solution)/shard_map/ring0:-1/ppermute | solution.py:33
  25.8 2.1 %collective-permute-start.6 = (bf16[2,256,512]{2,1,0:T(8,128)(2,1)S(1)}, bf16[2,256,512]{2,1,0:T(8,128)(2,1)S(1)}, u32[]{:S(2)}, u32[]{:S(2)}) collective-permute-start(bf16[2,256,512]{2,1,0:T(8,128)(2,1)S(1)} %collective-permute-done.2.refs_0_), channel_id=1, source_target_pairs={{0,8},{1,9},{2,10},{3,11},{4,20},{5,21},{6,22},{7,23},{16,0},{17,1... | collective-permute-start | bytes 1572872 | tf_op jit(solution)/shard_map/ring1:-1/ppermute | solution.py:33
  27.9 3.7 %collective-permute-start.3 = (bf16[2,128,512]{2,1,0:T(8,128)(2,1)S(1)}, bf16[2,128,512]{2,1,0:T(8,128)(2,1)S(1)}, u32[]{:S(2)}, u32[]{:S(2)}) collective-permute-start(bf16[2,128,512]{2,1,0:T(8,128)(2,1)S(1)} %get-tuple-element.39), channel_id=1, source_target_pairs={{0,3},{1,0},{2,1},{3,2},{4,7},{5,4},{6,5},{7,6},{16,19},{17,16},{1... | collective-permute-start | bytes 786440 | tf_op jit(solution)/shard_map/along_upper/ppermute | solution.py:37
  31.6 4.2 %collective-permute-done.8.refs_5_ = bf16[2,256,512]{2,1,0:T(8,128)(2,1)S(1)} collective-permute-done((bf16[2,256,512]{2,1,0:T(8,128)(2,1)S(1)}, bf16[2,256,512]{2,1,0:T(8,128)(2,1)S(1)}, u32[]{:S(2)}, u32[]{:S(2)}) %collective-permute-start.8) | collective-permute-done | bytes 524320 | tf_op jit(solution)/shard_map/along2:0/ppermute | solution.py:37
  35.8 3.2 %collective-permute-done.3 = bf16[2,128,512]{2,1,0:T(8,128)(2,1)S(1)} collective-permute-done((bf16[2,128,512]{2,1,0:T(8,128)(2,1)S(1)}, bf16[2,128,512]{2,1,0:T(8,128)(2,1)S(1)}, u32[]{:S(2)}, u32[]{:S(2)}) %collective-permute-start.3) | collective-permute-done | bytes 262176 | tf_op jit(solution)/shard_map/along_upper/ppermute | solution.py:37
  39.1 0.3 pad_maximum_fusion
  39.3 0.1 collective-permute-start.11
  39.4 0.2 pad_maximum_fusion.1
  39.6 0.6 collective-permute-start.13
  40.1 0.1 pad_maximum_fusion.3
  40.2 0.1 collective-permute-start.10
  40.3 0.1 pad_maximum_fusion.5
  40.4 2.9 %collective-permute-start.9 = (bf16[2,384,512]{2,1,0:T(8,128)(2,1)S(1)}, bf16[2,384,512]{2,1,0:T(8,128)(2,1)S(1)}, u32[]{:S(2)}, u32[]{:S(2)}) collective-permute-start(bf16[2,384,512]{2,1,0:T(8,128)(2,1)S(1)} %pad_maximum_fusion.5), channel_id=1, source_target_pairs={{0,3},{1,0},{2,1},{3,2},{4,7},{5,4},{6,5},{7,6},{16,19},{17,16},{1... | collective-permute-start | bytes 2359304 | tf_op jit(solution)/shard_map/along_lower/ppermute | solution.py:37
  43.2 0.3 collective-permute-done.11.refs_3_
  43.6 2.8 %collective-permute-start.12 = (bf16[2,256,512]{2,1,0:T(8,128)(2,1)S(1)}, bf16[2,256,512]{2,1,0:T(8,128)(2,1)S(1)}, u32[]{:S(2)}, u32[]{:S(2)}) collective-permute-start(bf16[2,256,512]{2,1,0:T(8,128)(2,1)S(1)} %collective-permute-done.8.refs_5_), channel_id=1, source_target_pairs={{0,8},{1,9},{2,10},{3,11},{4,20},{5,21},{6,22},{7,23},{16,0},{17,1... | collective-permute-start | bytes 1572872 | tf_op jit(solution)/shard_map/ring2:-1/ppermute | solution.py:33
  46.3 7.7 %shard_map.50 = (bf16[192,2,2048]{2,1,0:T(2,128)(2,1)}, bf16[192,2,2048]{2,1,0:T(2,128)(2,1)}, f32[768,512]{1,0:T(8,128)S(1)}, f32[768,512]{1,0:T(8,128)S(1)}) custom-call(bf16[192,4096]{1,0:T(8,128)(2,1)S(1)} %bitcast.4, bf16[192,4096]{1,0:T(8,128)(2,1)S(1)} %bitcast.10, bf16[2,256,512]{2,1,0:T(8,128)(2,1)S(1)} %collective-permute-done.2.refs_0_, ...), custom_call_target="tpu_custom_call" | custom-call | bytes 1 | tf_op jit(solution)/shard_map/pallas_call | solution.py:118
  54.0 0.1 collective-permute-start.14
  54.1 7.4 %collective-permute-done.10.refs_0_ = bf16[4,256,512]{2,1,0:T(8,128)(2,1)S(1)} collective-permute-done((bf16[4,256,512]{2,1,0:T(8,128)(2,1)S(1)}, bf16[4,256,512]{2,1,0:T(8,128)(2,1)S(1)}, u32[]{:S(2)}, u32[]{:S(2)}) %collective-permute-start.10) | collective-permute-done | bytes 1048608 | tf_op jit(solution)/shard_map/ring1:2_2:1/ppermute | solution.py:33
  61.5 0.1 fusion
  61.6 0.2 pad_maximum_fusion.2
  61.7 0.1 collective-permute-start.18
  61.9 0.1 pad_maximum_fusion.4
  62.0 0.6 collective-permute-start.15
  62.6 0.1 collective-permute-start.17
  62.6 3.1 %collective-permute-start.21 = (bf16[2,256,512]{2,1,0:T(8,128)(2,1)S(1)}, bf16[2,256,512]{2,1,0:T(8,128)(2,1)S(1)}, u32[]{:S(2)}, u32[]{:S(2)}) collective-permute-start(bf16[2,256,512]{2,1,0:T(8,128)(2,1)S(1)} %collective-permute-done.4.refs_9_), channel_id=1, source_target_pairs={{0,3},{1,0},{2,1},{3,2},{4,7},{5,4},{6,5},{7,6},{16,19},{17,16},{1... | collective-permute-start | bytes 1572872 | tf_op jit(solution)/shard_map/along-1:2/ppermute | solution.py:37
  65.8 0.9 %collective-permute-done.15.refs_5_ = bf16[4,256,512]{2,1,0:T(8,128)(2,1)S(1)} collective-permute-done((bf16[4,256,512]{2,1,0:T(8,128)(2,1)S(1)}, bf16[4,256,512]{2,1,0:T(8,128)(2,1)S(1)}, u32[]{:S(2)}, u32[]{:S(2)}) %collective-permute-start.15) | collective-permute-done | bytes 1048608 | tf_op jit(solution)/shard_map/core-1:0_-1:1/ppermute | solution.py:41
  66.7 2.0 %collective-permute-start.16 = (bf16[2,256,512]{2,1,0:T(8,128)(2,1)S(1)}, bf16[2,256,512]{2,1,0:T(8,128)(2,1)S(1)}, u32[]{:S(2)}, u32[]{:S(2)}) collective-permute-start(bf16[2,256,512]{2,1,0:T(8,128)(2,1)S(1)} %pad_maximum_fusion.6.refs_3_), channel_id=1, source_target_pairs={{0,8},{1,9},{2,10},{3,11},{4,20},{5,21},{6,22},{7,23},{16,0},{17,1... | collective-permute-start | bytes 1572872 | tf_op jit(solution)/shard_map/ring-1:-1/ppermute | solution.py:33
  68.7 5.3 %shard_map.51 = (bf16[192,2,2048]{2,1,0:T(2,128)(2,1)}, bf16[192,2,2048]{2,1,0:T(2,128)(2,1)}, f32[768,512]{1,0:T(8,128)S(1)}, f32[768,512]{1,0:T(8,128)S(1)}) custom-call(bf16[192,4096]{1,0:T(8,128)(2,1)S(1)} %bitcast.5, bf16[192,4096]{1,0:T(8,128)(2,1)S(1)} %bitcast.11, ...), custom_call_target="tpu_custom_call", output_to_operand_aliasing={{0}: (10, {}), {1}: (11, {})} | custom-call | flops 4026531840 | bytes 10485760 | tf_op jit(solution)/shard_map/pallas_call | solution.py:118
  74.0 0.1 collective-permute-start.19
  74.1 1.1 %collective-permute-done.19 = bf16[1,16,128]{2,1,0:T(8,128)(2,1)S(1)} collective-permute-done((bf16[1,16,128]{2,1,0:T(8,128)(2,1)S(1)}, bf16[1,16,128]{2,1,0:T(8,128)(2,1)S(1)}, u32[]{:S(2)}, u32[]{:S(2)}) %collective-permute-start.19) | collective-permute-done | bytes 4128 | tf_op jit(solution)/shard_map/token/ppermute | solution.py:41
  75.3 0.2 collective-permute-start.23
  75.4 0.6 shard_map.52.refs_1_
  76.0 0.9 %collective-permute-done.21.refs_1_ = bf16[2,256,512]{2,1,0:T(8,128)(2,1)S(1)} collective-permute-done((bf16[2,256,512]{2,1,0:T(8,128)(2,1)S(1)}, bf16[2,256,512]{2,1,0:T(8,128)(2,1)S(1)}, u32[]{:S(2)}, u32[]{:S(2)}) %collective-permute-start.21) | collective-permute-done | bytes 524320 | tf_op jit(solution)/shard_map/along-1:2/ppermute | solution.py:37
  77.0 0.3 collective-permute-start.20
  77.3 0.2 collective-permute-start.22
  77.5 1.0 %shard_map.53.refs_2_ = f32[768,512]{1,0:T(8,128)S(1)} custom-call(bf16[192,4096]{1,0:T(8,128)(2,1)S(1)} %bitcast.7, bf16[192,4096]{1,0:T(8,128)(2,1)S(1)} %bitcast.13, bf16[2,256,512]{2,1,0:T(8,128)(2,1)S(1)} %collective-permute-done.16.refs_0_, bf16[2,256,512]{2,1,0:T(8,128)(2,1)S(1)} %collective-permute-done.21.refs_1_, ...), custom_call_target="tpu_custom_call" | custom-call | flops 805306368 | bytes 2097152 | tf_op jit(solution)/shard_map/pallas_call | solution.py:118
  78.5 1.6 %shard_map.54 = (bf16[192,2,2048]{2,1,0:T(2,128)(2,1)}, bf16[192,2,2048]{2,1,0:T(2,128)(2,1)}) custom-call(bf16[192,4096]{1,0:T(8,128)(2,1)S(1)} %bitcast.8, bf16[192,4096]{1,0:T(8,128)(2,1)S(1)} %bitcast.14, bf16[2,256,512]{2,1,0:T(8,128)(2,1)S(1)} %collective-permute-done.23.refs_0_, ...), custom_call_target="tpu_custom_call", output_to_operand_aliasing={{0}: (4, {}), {1}: (5, {})} | custom-call | flops 402653184 | bytes 1048576 | tf_op jit(solution)/shard_map/pallas_call | solution.py:118
  80.1 2.0 %shard_map.55 = (bf16[192,2,2048]{2,1,0:T(2,128)(2,1)}, bf16[192,2,2048]{2,1,0:T(2,128)(2,1)}) custom-call(bf16[192,4096]{1,0:T(8,128)(2,1)S(1)} %bitcast.9, bf16[192,4096]{1,0:T(8,128)(2,1)S(1)} %bitcast.15, bf16[2,256,512]{2,1,0:T(8,128)(2,1)S(1)} %collective-permute-done.20.refs_0_, ...), custom_call_target="tpu_custom_call", output_to_operand_aliasing={{0}: (5, {}), {1}: (6, {})} | custom-call | flops 805306368 | bytes 2097152 | tf_op jit(solution)/shard_map/pallas_call | solution.py:118
  (24 shorter events, 0.2 us)
Async XLA Ops:
  0.6 10.4 %collective-permute-start = (bf16[2,256,512]{2,1,0:T(8,128)(2,1)}, bf16[2,256,512]{2,1,0:T(8,128)(2,1)S(1)}, u32[]{:S(2)}, u32[]{:S(2)}) collective-permute-start(bf16[2,256,512]{2,1,0:T(8,128)(2,1)} %refs_6_.1), channel_id=1, source_target_pairs={{0,16},{1,17},{2,18},{3,19},{4,12},{5,13},{6,14},{7,15},{16,24},{1... | collective-permute-start | bytes 1572872 | tf_op jit(solution)/shard_map/ring0:1/ppermute | solution.py:33
  3.6 15.5 %collective-permute-start.2 = (bf16[2,256,512]{2,1,0:T(8,128)(2,1)}, bf16[2,256,512]{2,1,0:T(8,128)(2,1)S(1)}, u32[]{:S(2)}, u32[]{:S(2)}) collective-permute-start(bf16[2,256,512]{2,1,0:T(8,128)(2,1)} %refs_6_.1), channel_id=1, source_target_pairs={{0,1},{1,2},{2,3},{3,0},{4,5},{5,6},{6,7},{7,4},{16,17},{17,18},{1... | collective-permute-start | bytes 1572872 | tf_op jit(solution)/shard_map/along1:0/ppermute | solution.py:37
  5.2 2.2 %copy-start.1 = (bf16[192,2,2048]{2,1,0:T(2,128)(2,1)S(1)}, bf16[192,2,2048]{2,1,0:T(2,128)(2,1)}, u32[]{:S(2)}) copy-start(bf16[192,2,2048]{2,1,0:T(2,128)(2,1)} %param.4) | copy-start | bytes 4718596
  7.4 3.6 %copy-start = (bf16[2,256,512]{2,1,0:T(8,128)(2,1)S(1)}, bf16[2,256,512]{2,1,0:T(8,128)(2,1)}, u32[]{:S(2)}) copy-start(bf16[2,256,512]{2,1,0:T(8,128)(2,1)} %refs_6_.1) | copy-start | bytes 1572868
  11.0 14.8 %collective-permute-start.1 = (bf16[2,256,512]{2,1,0:T(8,128)(2,1)S(1)}, bf16[2,256,512]{2,1,0:T(8,128)(2,1)S(1)}, u32[]{:S(2)}, u32[]{:S(2)}) collective-permute-start(bf16[2,256,512]{2,1,0:T(8,128)(2,1)S(1)} %copy-done), channel_id=1, source_target_pairs={{0,8},{1,9},{2,10},{3,11},{4,20},{5,21},{6,22},{7,23},{16,0},{17,1... | collective-permute-start | bytes 1572872 | tf_op jit(solution)/shard_map/ring0:-1/ppermute | solution.py:33
  13.0 14.9 %collective-permute-start.4 = (bf16[2,256,512]{2,1,0:T(8,128)(2,1)S(1)}, bf16[2,256,512]{2,1,0:T(8,128)(2,1)S(1)}, u32[]{:S(2)}, u32[]{:S(2)}) collective-permute-start(bf16[2,256,512]{2,1,0:T(8,128)(2,1)S(1)} %collective-permute-done.refs_7_), channel_id=1, source_target_pairs={{0,16},{1,17},{2,18},{3,19},{4,12},{5,13},{6,14},{7,15},{16,24},{1... | collective-permute-start | bytes 1572872 | tf_op jit(solution)/shard_map/ring0:2/ppermute | solution.py:33
  19.1 16.7 %collective-permute-start.8 = (bf16[2,256,512]{2,1,0:T(8,128)(2,1)S(1)}, bf16[2,256,512]{2,1,0:T(8,128)(2,1)S(1)}, u32[]{:S(2)}, u32[]{:S(2)}) collective-permute-start(bf16[2,256,512]{2,1,0:T(8,128)(2,1)S(1)} %collective-permute-done.2.refs_0_), channel_id=1, source_target_pairs={{0,1},{1,2},{2,3},{3,0},{4,5},{5,6},{6,7},{7,4},{16,17},{17,18},{1... | collective-permute-start | bytes 1572872 | tf_op jit(solution)/shard_map/along2:0/ppermute | solution.py:37
  19.1 16.7 %collective-permute-start.5 = (bf16[2,256,512]{2,1,0:T(8,128)(2,1)S(1)}, bf16[2,256,512]{2,1,0:T(8,128)(2,1)S(1)}, u32[]{:S(2)}, u32[]{:S(2)}) collective-permute-start(bf16[2,256,512]{2,1,0:T(8,128)(2,1)S(1)} %collective-permute-done.2.refs_0_), channel_id=1, source_target_pairs={{0,16},{1,17},{2,18},{3,19},{4,12},{5,13},{6,14},{7,15},{16,24},{1... | collective-permute-start | bytes 1572872 | tf_op jit(solution)/shard_map/ring1:1/ppermute | solution.py:33
  19.6 16.2 %collective-permute-start.7 = (bf16[2,256,512]{2,1,0:T(8,128)(2,1)S(1)}, bf16[2,256,512]{2,1,0:T(8,128)(2,1)S(1)}, u32[]{:S(2)}, u32[]{:S(2)}) collective-permute-start(bf16[2,256,512]{2,1,0:T(8,128)(2,1)S(1)} %copy-done), channel_id=1, source_target_pairs={{0,4},{1,5},{2,6},{3,7},{4,0},{5,1},{6,2},{7,3},{16,20},{17,21},{1... | collective-permute-start | bytes 1572872 | tf_op jit(solution)/shard_map/core0:0/ppermute | solution.py:41
  25.8 13.2 %collective-permute-start.6 = (bf16[2,256,512]{2,1,0:T(8,128)(2,1)S(1)}, bf16[2,256,512]{2,1,0:T(8,128)(2,1)S(1)}, u32[]{:S(2)}, u32[]{:S(2)}) collective-permute-start(bf16[2,256,512]{2,1,0:T(8,128)(2,1)S(1)} %collective-permute-done.2.refs_0_), channel_id=1, source_target_pairs={{0,8},{1,9},{2,10},{3,11},{4,20},{5,21},{6,22},{7,23},{16,0},{17,1... | collective-permute-start | bytes 1572872 | tf_op jit(solution)/shard_map/ring1:-1/ppermute | solution.py:33
  27.9 11.1 %collective-permute-start.3 = (bf16[2,128,512]{2,1,0:T(8,128)(2,1)S(1)}, bf16[2,128,512]{2,1,0:T(8,128)(2,1)S(1)}, u32[]{:S(2)}, u32[]{:S(2)}) collective-permute-start(bf16[2,128,512]{2,1,0:T(8,128)(2,1)S(1)} %get-tuple-element.39), channel_id=1, source_target_pairs={{0,3},{1,0},{2,1},{3,2},{4,7},{5,4},{6,5},{7,6},{16,19},{17,16},{1... | collective-permute-start | bytes 786440 | tf_op jit(solution)/shard_map/along_upper/ppermute | solution.py:37
  39.3 4.2 %collective-permute-start.11 = (bf16[8,256,512]{2,1,0:T(8,128)(2,1)S(1)}, bf16[8,256,512]{2,1,0:T(8,128)(2,1)S(1)}, u32[]{:S(2)}, u32[]{:S(2)}) collective-permute-start(bf16[8,256,512]{2,1,0:T(8,128)(2,1)S(1)} %pad_maximum_fusion), channel_id=1, source_target_pairs={{0,4},{1,5},{2,6},{3,7},{4,0},{5,1},{6,2},{7,3},{16,20},{17,21},{1... | collective-permute-start | bytes 6291464 | tf_op jit(solution)/shard_map/core0:1_0:-1_0:2_1:0/ppermute | solution.py:41
  39.6 6.7 %collective-permute-start.13 = (bf16[6,256,512]{2,1,0:T(8,128)(2,1)S(1)}, bf16[6,256,512]{2,1,0:T(8,128)(2,1)S(1)}, u32[]{:S(2)}, u32[]{:S(2)}) collective-permute-start(bf16[6,256,512]{2,1,0:T(8,128)(2,1)S(1)} %pad_maximum_fusion.1), channel_id=1, source_target_pairs={{0,4},{1,5},{2,6},{3,7},{4,0},{5,1},{6,2},{7,3},{16,20},{17,21},{1... | collective-permute-start | bytes 4718600 | tf_op jit(solution)/shard_map/core1:1_1:-1_2:0/ppermute | solution.py:41
  40.2 21.2 %collective-permute-start.10 = (bf16[4,256,512]{2,1,0:T(8,128)(2,1)S(1)}, bf16[4,256,512]{2,1,0:T(8,128)(2,1)S(1)}, u32[]{:S(2)}, u32[]{:S(2)}) collective-permute-start(bf16[4,256,512]{2,1,0:T(8,128)(2,1)S(1)} %pad_maximum_fusion.3), channel_id=1, source_target_pairs={{0,16},{1,17},{2,18},{3,19},{4,12},{5,13},{6,14},{7,15},{16,24},{1... | collective-permute-start | bytes 3145736 | tf_op jit(solution)/shard_map/ring1:2_2:1/ppermute | solution.py:33
  40.4 21.2 %collective-permute-start.9 = (bf16[2,384,512]{2,1,0:T(8,128)(2,1)S(1)}, bf16[2,384,512]{2,1,0:T(8,128)(2,1)S(1)}, u32[]{:S(2)}, u32[]{:S(2)}) collective-permute-start(bf16[2,384,512]{2,1,0:T(8,128)(2,1)S(1)} %pad_maximum_fusion.5), channel_id=1, source_target_pairs={{0,3},{1,0},{2,1},{3,2},{4,7},{5,4},{6,5},{7,6},{16,19},{17,16},{1... | collective-permute-start | bytes 2359304 | tf_op jit(solution)/shard_map/along_lower/ppermute | solution.py:37
  43.6 18.0 %collective-permute-start.12 = (bf16[2,256,512]{2,1,0:T(8,128)(2,1)S(1)}, bf16[2,256,512]{2,1,0:T(8,128)(2,1)S(1)}, u32[]{:S(2)}, u32[]{:S(2)}) collective-permute-start(bf16[2,256,512]{2,1,0:T(8,128)(2,1)S(1)} %collective-permute-done.8.refs_5_), channel_id=1, source_target_pairs={{0,8},{1,9},{2,10},{3,11},{4,20},{5,21},{6,22},{7,23},{16,0},{17,1... | collective-permute-start | bytes 1572872 | tf_op jit(solution)/shard_map/ring2:-1/ppermute | solution.py:33
  54.0 7.5 %collective-permute-start.14 = (bf16[1,16,128]{2,1,0:T(8,128)(2,1)S(1)}, bf16[1,16,128]{2,1,0:T(8,128)(2,1)S(1)}, u32[]{:S(2)}, u32[]{:S(2)}) collective-permute-start(bf16[1,16,128]{2,1,0:T(8,128)(2,1)S(1)} %get-tuple-element.53), channel_id=1, source_target_pairs={{0,4},{1,5},{2,6},{3,7},{4,0},{5,1},{6,2},{7,3},{16,20},{17,21},{1... | collective-permute-start | bytes 12296 | tf_op jit(solution)/shard_map/token/ppermute | solution.py:41
  61.7 7.0 %collective-permute-start.18 = (bf16[6,256,512]{2,1,0:T(8,128)(2,1)S(1)}, bf16[6,256,512]{2,1,0:T(8,128)(2,1)S(1)}, u32[]{:S(2)}, u32[]{:S(2)}) collective-permute-start(bf16[6,256,512]{2,1,0:T(8,128)(2,1)S(1)} %pad_maximum_fusion.2), channel_id=1, source_target_pairs={{0,4},{1,5},{2,6},{3,7},{4,0},{5,1},{6,2},{7,3},{16,20},{17,21},{1... | collective-permute-start | bytes 4718600 | tf_op jit(solution)/shard_map/core1:2_2:1_2:-1/ppermute | solution.py:41
  62.0 4.7 %collective-permute-start.15 = (bf16[4,256,512]{2,1,0:T(8,128)(2,1)S(1)}, bf16[4,256,512]{2,1,0:T(8,128)(2,1)S(1)}, u32[]{:S(2)}, u32[]{:S(2)}) collective-permute-start(bf16[4,256,512]{2,1,0:T(8,128)(2,1)S(1)} %pad_maximum_fusion.4), channel_id=1, source_target_pairs={{0,4},{1,5},{2,6},{3,7},{4,0},{5,1},{6,2},{7,3},{16,20},{17,21},{1... | collective-permute-start | bytes 3145736 | tf_op jit(solution)/shard_map/core-1:0_-1:1/ppermute | solution.py:41
  62.6 11.5 %collective-permute-start.17 = (bf16[2,256,512]{2,1,0:T(8,128)(2,1)S(1)}, bf16[2,256,512]{2,1,0:T(8,128)(2,1)S(1)}, u32[]{:S(2)}, u32[]{:S(2)}) collective-permute-start(bf16[2,256,512]{2,1,0:T(8,128)(2,1)S(1)} %get-tuple-element.57), channel_id=1, source_target_pairs={{0,16},{1,17},{2,18},{3,19},{4,12},{5,13},{6,14},{7,15},{16,24},{1... | collective-permute-start | bytes 1572872 | tf_op jit(solution)/shard_map/ring2:2/ppermute | solution.py:33
  62.6 14.3 %collective-permute-start.21 = (bf16[2,256,512]{2,1,0:T(8,128)(2,1)S(1)}, bf16[2,256,512]{2,1,0:T(8,128)(2,1)S(1)}, u32[]{:S(2)}, u32[]{:S(2)}) collective-permute-start(bf16[2,256,512]{2,1,0:T(8,128)(2,1)S(1)} %collective-permute-done.4.refs_9_), channel_id=1, source_target_pairs={{0,3},{1,0},{2,1},{3,2},{4,7},{5,4},{6,5},{7,6},{16,19},{17,16},{1... | collective-permute-start | bytes 1572872 | tf_op jit(solution)/shard_map/along-1:2/ppermute | solution.py:37
  66.7 10.2 %collective-permute-start.16 = (bf16[2,256,512]{2,1,0:T(8,128)(2,1)S(1)}, bf16[2,256,512]{2,1,0:T(8,128)(2,1)S(1)}, u32[]{:S(2)}, u32[]{:S(2)}) collective-permute-start(bf16[2,256,512]{2,1,0:T(8,128)(2,1)S(1)} %pad_maximum_fusion.6.refs_3_), channel_id=1, source_target_pairs={{0,8},{1,9},{2,10},{3,11},{4,20},{5,21},{6,22},{7,23},{16,0},{17,1... | collective-permute-start | bytes 1572872 | tf_op jit(solution)/shard_map/ring-1:-1/ppermute | solution.py:33
  74.0 1.2 %collective-permute-start.19 = (bf16[1,16,128]{2,1,0:T(8,128)(2,1)S(1)}, bf16[1,16,128]{2,1,0:T(8,128)(2,1)S(1)}, u32[]{:S(2)}, u32[]{:S(2)}) collective-permute-start(bf16[1,16,128]{2,1,0:T(8,128)(2,1)S(1)} %get-tuple-element.64), channel_id=1, source_target_pairs={{0,4},{1,5},{2,6},{3,7},{4,0},{5,1},{6,2},{7,3},{16,20},{17,21},{1... | collective-permute-start | bytes 12296 | tf_op jit(solution)/shard_map/token/ppermute | solution.py:41
  75.3 3.2 %collective-permute-start.23 = (bf16[2,256,512]{2,1,0:T(8,128)(2,1)S(1)}, bf16[2,256,512]{2,1,0:T(8,128)(2,1)S(1)}, u32[]{:S(2)}, u32[]{:S(2)}) collective-permute-start(bf16[2,256,512]{2,1,0:T(8,128)(2,1)S(1)} %collective-permute-done.17.refs_0_), channel_id=1, source_target_pairs={{0,4},{1,5},{2,6},{3,7},{4,0},{5,1},{6,2},{7,3},{16,20},{17,21},{1... | collective-permute-start | bytes 1572872 | tf_op jit(solution)/shard_map/core2:2/ppermute | solution.py:41
  77.0 3.1 %collective-permute-start.20 = (bf16[2,256,512]{2,1,0:T(8,128)(2,1)S(1)}, bf16[2,256,512]{2,1,0:T(8,128)(2,1)S(1)}, u32[]{:S(2)}, u32[]{:S(2)}) collective-permute-start(bf16[2,256,512]{2,1,0:T(8,128)(2,1)S(1)} %collective-permute-done.16.refs_0_), channel_id=1, source_target_pairs={{0,4},{1,5},{2,6},{3,7},{4,0},{5,1},{6,2},{7,3},{16,20},{17,21},{1... | collective-permute-start | bytes 1572872 | tf_op jit(solution)/shard_map/core-1:-1/ppermute | solution.py:41
  77.3 2.8 %collective-permute-start.22 = (bf16[2,256,512]{2,1,0:T(8,128)(2,1)S(1)}, bf16[2,256,512]{2,1,0:T(8,128)(2,1)S(1)}, u32[]{:S(2)}, u32[]{:S(2)}) collective-permute-start(bf16[2,256,512]{2,1,0:T(8,128)(2,1)S(1)} %collective-permute-done.21.refs_1_), channel_id=1, source_target_pairs={{0,4},{1,5},{2,6},{3,7},{4,0},{5,1},{6,2},{7,3},{16,20},{17,21},{1... | collective-permute-start | bytes 1572872 | tf_op jit(solution)/shard_map/core-1:2/ppermute | solution.py:41
